TPU v7x, 512 devices: a whole 4x8x8 slice. The times are simulated.
512 devices in a mesh: blk: 128 (over x_lo, z, y), feat: 4 (over x_hi, core).
Axes of the slice: x: 4 (x_hi: 2, x_lo: 2; x = x_hi * 2 + x_lo), y: 8, z: 8, core: 2. Of those that a mesh axis runs over, the one named last changes fastest.
Arguments:
- points: bfloat16 [768, 262144], P('feat', 'blk'), as said below
- centroids: bfloat16 [768, 65536], P('feat', 'blk'), as said below
- col_pot: float32 [65536], P('blk'), may hold values from -9 to 9
- row_pot: float32 [262144], P('blk'), may hold values from -9 to 9
Outputs:
- row_lse: float32 [262144], P('blk')
- col_lse: float32 [65536], P(('blk', 'feat'))
- centroid_mean: float32 [65536, 768], P(('blk', 'feat'))
Inputs may be any that keep to these rules, and one draw needn't show every extreme that they name: `centroids`: entries of order one. `points`: entries of order one.
All inputs are finite; a program needn't handle non-finite values.
Results may differ from a plain program's by a relative error of at most 0.0008.
Values may be sent and summed in bfloat16 or wider, within the bound.
No kernel may reach another device: no remote copies, remote signals or barrier semaphores. Data moves between devices by JAX's collectives and lax.ppermute only.
A program may use at most 64 MiB of HBM per device.

v0:
```python
import jax
import jax.numpy as jnp
from jax import lax
from jax.sharding import PartitionSpec as P

HOPS = 4


def from_behind(block, axis, distance):
    devices = range(lax.axis_size(axis))
    route = [((i - distance) % len(devices), i) for i in devices]
    return lax.ppermute(block, axis, route)


def combined_all(array, axis, combine):
    everything = jax.tree.map(lambda part: lax.all_gather(part, axis), array)
    first = jax.tree.map(lambda part: part[0], everything)

    def turn(k, so_far):
        return combine(so_far, jax.tree.map(lambda part: part[k], everything))

    return lax.fori_loop(1, lax.axis_size(axis), turn, first)


def merge_rows(first, second):
    top = jnp.maximum(first[0], second[0])
    return (top, first[1] * jnp.exp(first[0] - top) + second[1] * jnp.exp(second[0] - top))


def merge_cols(first, second):
    top = jnp.maximum(first[0], second[0])
    left = jnp.exp(first[0] - top)
    right = jnp.exp(second[0] - top)
    return (
        top,
        first[1] * left + second[1] * right,
        first[2] * left[:, None] + second[2] * right[:, None],
    )


def pair_terms(full_points, panel_cols, potential, row_pot):
    squares = jnp.sum(jnp.square(panel_cols.astype(jnp.float32)), axis=0)
    dots = lax.dot_general(
        full_points, panel_cols, (((0,), (0,)), ((), ())), preferred_element_type=jnp.float32
    )
    score = (dots - 0.5 * squares[None, :]) * (1.0 / (0.02 * full_points.shape[0]))
    row_terms = score + potential[None, :]
    row_max = jnp.max(row_terms, axis=1)
    row_sum = jnp.sum(jnp.exp(row_terms - row_max[:, None]), axis=1)
    col_terms = score - row_pot[:, None]
    col_max = jnp.max(col_terms, axis=0)
    expo = jnp.exp(col_terms - col_max[None, :])
    col_sum = jnp.sum(expo, axis=0)
    weight = expo.astype(jnp.bfloat16)
    col_acc = lax.dot_general(
        weight, full_points, (((0,), (1,)), ((), ())), preferred_element_type=jnp.float32
    )
    return ((row_max, row_sum), (col_max, col_sum, col_acc))


def local(points, centroids, col_pot, row_pot):
    full_points = lax.all_gather(points, "feat", axis=0, tiled=True)
    groups = lax.axis_size("feat")
    member = lax.axis_index("feat")
    quarter = centroids.shape[1] // groups
    panel_now = centroids
    potential = col_pot

    def local_terms(panel_held, potential_held):
        panel_cols = lax.all_to_all(panel_held, "feat", split_axis=1, concat_axis=0, tiled=True)
        potential_cols = lax.dynamic_slice_in_dim(potential_held, member * quarter, quarter, 0)
        return pair_terms(full_points, panel_cols, potential_cols, row_pot)

    row_state, col_state = local_terms(panel_now, potential)
    for step_index in range(HOPS):
        panel_now = from_behind(panel_now, "blk", 1)
        potential, col_max, col_sum, col_acc = from_behind(
            (potential, col_state[0], col_state[1], col_state[2]), "blk", 1
        )
        row_part, col_part = local_terms(panel_now, potential)
        row_state = merge_rows(row_state, row_part)
        col_state = merge_cols((col_max, col_sum, col_acc), col_part)
    col_state = from_behind((col_state[0], col_state[1], col_state[2]), "blk", -HOPS)
    row_max, row_sum = combined_all((row_state[0], row_state[1]), "feat", merge_rows)
    row_lse = row_max + jnp.log(row_sum)
    col_lse = col_state[0] + jnp.log(col_state[1])
    centroid_mean = col_state[2] / col_state[1][:, None]
    return (row_lse, col_lse, centroid_mean)


def solution(mesh):
    return jax.shard_map(
        local,
        mesh=mesh,
        in_specs=(P("feat", "blk"), P("feat", "blk"), P("blk"), P("blk")),
        out_specs=(P("blk"), P(("blk", "feat")), P(("blk", "feat"), None)),
        check_vma=False,
    )
```

profile of v0, /device:TPU:16, one launch (start us, length us, event | category | flops | bytes accessed | tf_op | source)
XLA Modules:
  0.0 269.8 jit_solution(556637944374200813)
XLA Ops:
  7.9 1.6 copy_bitcast_fusion.4
  9.6 4.3 %all-to-all-start = ((bf16[192,4,128]{2,0,1:T(8,128)(2,1)}), bf16[192,4,128]{2,0,1:T(8,128)(2,1)S(1)}, u32[]{:S(2)}, u32[]{:S(2)}) async-start(bf16[192,4,128]{2,0,1:T(8,128)(2,1)} %copy_bitcast_fusion.4), calls=%async_computation | async-start | bytes 393216 | tf_op jit(solution)/shard_map/all_to_all | solution.py:70
  13.8 3.5 %collective-permute-start = (bf16[192,512]{1,0:T(8,128)(2,1)}, bf16[192,512]{1,0:T(8,128)(2,1)S(1)}, u32[]{:S(2)}, u32[]{:S(2)}) collective-permute-start(bf16[192,512]{1,0:T(8,128)(2,1)} %param.7), channel_id=1, source_target_pairs={{508,0},{0,4},{4,8},{8,12},{12,16},{16,20},{20,24},{24,28},{28,32}... | collective-permute-start | bytes 589832 | tf_op jit(solution)/shard_map/ppermute | solution.py:12
  17.3 4.7 %collective-permute-start.1 = (f32[512]{0:T(512)}, f32[512]{0:T(512)S(1)}, u32[]{:S(2)}, u32[]{:S(2)}) collective-permute-start(f32[512]{0:T(512)} %param.8), channel_id=1, source_target_pairs={{508,0},{0,4},{4,8},{8,12},{12,16},{16,20},{20,24},{24,28},{28,32}... | collective-permute-start | bytes 6152 | tf_op jit(solution)/shard_map/ppermute | solution.py:12
  22.0 1.5 collective-permute-done.1
  23.5 4.2 %collective-permute-start.3 = (f32[512]{0:T(512)S(1)}, f32[512]{0:T(512)S(1)}, u32[]{:S(2)}, u32[]{:S(2)}) collective-permute-start(f32[512]{0:T(512)S(1)} %collective-permute-done.1), channel_id=1, source_target_pairs={{508,0},{0,4},{4,8},{8,12},{12,16},{16,20},{20,24},{24,28},{28,32}... | collective-permute-start | bytes 6152 | tf_op jit(solution)/shard_map/ppermute | solution.py:12
  27.7 2.6 collective-permute-done.3
  30.3 3.6 %collective-permute-start.5 = (f32[512]{0:T(512)S(1)}, f32[512]{0:T(512)S(1)}, u32[]{:S(2)}, u32[]{:S(2)}) collective-permute-start(f32[512]{0:T(512)S(1)} %collective-permute-done.3), channel_id=1, source_target_pairs={{508,0},{0,4},{4,8},{8,12},{12,16},{16,20},{20,24},{24,28},{28,32}... | collective-permute-start | bytes 6152 | tf_op jit(solution)/shard_map/ppermute | solution.py:12
  34.0 7.5 %collective-permute-done.5 = f32[512]{0:T(512)S(1)} collective-permute-done((f32[512]{0:T(512)S(1)}, f32[512]{0:T(512)S(1)}, u32[]{:S(2)}, u32[]{:S(2)}) %collective-permute-start.5) | collective-permute-done | bytes 2080 | tf_op jit(solution)/shard_map/ppermute | solution.py:12
  41.4 1.9 collective-permute-start.7
  43.3 1.3 dynamic_slice.35
  46.5 4.7 %collective-permute-done.7 = f32[512]{0:T(512)S(1)} collective-permute-done((f32[512]{0:T(512)S(1)}, f32[512]{0:T(512)S(1)}, u32[]{:S(2)}, u32[]{:S(2)}) %collective-permute-start.7) | collective-permute-done | bytes 2080 | tf_op jit(solution)/shard_map/ppermute | solution.py:12
  52.7 5.1 %all-to-all-start.1 = ((bf16[192,4,128]{2,0,1:T(8,128)(2,1)}), bf16[192,4,128]{2,0,1:T(8,128)(2,1)S(1)}, u32[]{:S(2)}, u32[]{:S(2)}) async-start(bf16[192,4,128]{2,0,1:T(8,128)(2,1)} %copy_bitcast_fusion.3), calls=%async_computation.1 | async-start | bytes 393216 | tf_op jit(solution)/shard_map/all_to_all | solution.py:70
  57.8 1.9 collective-permute-start.2
  60.2 4.4 %all-to-all-done.1 = bf16[192,4,128]{2,0,1:T(8,128)(2,1)S(1)} async-done(((bf16[192,4,128]{2,0,1:T(8,128)(2,1)}), bf16[192,4,128]{2,0,1:T(8,128)(2,1)S(1)}, u32[]{:S(2)}, u32[]{:S(2)}) %all-to-all-start.1) | async-done | bytes 196640 | tf_op jit(solution)/shard_map/all_to_all | solution.py:70
  64.7 6.7 %collective-permute-done.2 = bf16[192,512]{1,0:T(8,128)(2,1)S(1)} collective-permute-done((bf16[192,512]{1,0:T(8,128)(2,1)S(1)}, bf16[192,512]{1,0:T(8,128)(2,1)S(1)}, u32[]{:S(2)}, u32[]{:S(2)}) %collective-permute-start.2) | collective-permute-done | bytes 196640 | tf_op jit(solution)/shard_map/ppermute | solution.py:12
  71.5 0.7 copy_bitcast_fusion.2
  72.2 4.4 %all-to-all-start.2 = ((bf16[192,4,128]{2,0,1:T(8,128)(2,1)}), bf16[192,4,128]{2,0,1:T(8,128)(2,1)S(1)}, u32[]{:S(2)}, u32[]{:S(2)}) async-start(bf16[192,4,128]{2,0,1:T(8,128)(2,1)} %copy_bitcast_fusion.2), calls=%async_computation.2 | async-start | bytes 393216 | tf_op jit(solution)/shard_map/all_to_all | solution.py:70
  76.6 1.9 collective-permute-start.4
  79.0 4.4 %all-to-all-done.2 = bf16[192,4,128]{2,0,1:T(8,128)(2,1)S(1)} async-done(((bf16[192,4,128]{2,0,1:T(8,128)(2,1)}), bf16[192,4,128]{2,0,1:T(8,128)(2,1)S(1)}, u32[]{:S(2)}, u32[]{:S(2)}) %all-to-all-start.2) | async-done | bytes 196640 | tf_op jit(solution)/shard_map/all_to_all | solution.py:70
  83.6 6.7 %collective-permute-done.4 = bf16[192,512]{1,0:T(8,128)(2,1)S(1)} collective-permute-done((bf16[192,512]{1,0:T(8,128)(2,1)S(1)}, bf16[192,512]{1,0:T(8,128)(2,1)S(1)}, u32[]{:S(2)}, u32[]{:S(2)}) %collective-permute-start.4) | collective-permute-done | bytes 196640 | tf_op jit(solution)/shard_map/ppermute | solution.py:12
  90.3 0.7 copy_bitcast_fusion.1
  91.0 4.4 %all-to-all-start.3 = ((bf16[192,4,128]{2,0,1:T(8,128)(2,1)}), bf16[192,4,128]{2,0,1:T(8,128)(2,1)S(1)}, u32[]{:S(2)}, u32[]{:S(2)}) async-start(bf16[192,4,128]{2,0,1:T(8,128)(2,1)} %copy_bitcast_fusion.1), calls=%async_computation.3 | async-start | bytes 393216 | tf_op jit(solution)/shard_map/all_to_all | solution.py:70
  95.5 1.9 collective-permute-start.6
  97.4 4.9 %all-to-all-done.3 = bf16[192,4,128]{2,0,1:T(8,128)(2,1)S(1)} async-done(((bf16[192,4,128]{2,0,1:T(8,128)(2,1)}), bf16[192,4,128]{2,0,1:T(8,128)(2,1)S(1)}, u32[]{:S(2)}, u32[]{:S(2)}) %all-to-all-start.3) | async-done | bytes 196640 | tf_op jit(solution)/shard_map/all_to_all | solution.py:70
  102.4 6.5 %collective-permute-done.6 = bf16[192,512]{1,0:T(8,128)(2,1)S(1)} collective-permute-done((bf16[192,512]{1,0:T(8,128)(2,1)S(1)}, bf16[192,512]{1,0:T(8,128)(2,1)S(1)}, u32[]{:S(2)}, u32[]{:S(2)}) %collective-permute-start.6) | collective-permute-done | bytes 196640 | tf_op jit(solution)/shard_map/ppermute | solution.py:12
  109.6 4.4 %all-to-all-start.4 = ((bf16[192,4,128]{2,0,1:T(8,128)(2,1)}), bf16[192,4,128]{2,0,1:T(8,128)(2,1)S(1)}, u32[]{:S(2)}, u32[]{:S(2)}) async-start(bf16[192,4,128]{2,0,1:T(8,128)(2,1)} %copy_bitcast_fusion), calls=%async_computation.4 | async-start | bytes 393216 | tf_op jit(solution)/shard_map/all_to_all | solution.py:70
  114.1 6.8 %all-to-all-done.4 = bf16[192,4,128]{2,0,1:T(8,128)(2,1)S(1)} async-done(((bf16[192,4,128]{2,0,1:T(8,128)(2,1)}), bf16[192,4,128]{2,0,1:T(8,128)(2,1)S(1)}, u32[]{:S(2)}, u32[]{:S(2)}) %all-to-all-start.4) | async-done | bytes 196640 | tf_op jit(solution)/shard_map/all_to_all | solution.py:70
  121.6 3.6 %subtract_reduce_fusion.4 = (f32[128]{0:T(128)S(1)}, f32[2048]{0:T(1024)S(1)}, f32[2048,128]{1,0:T(8,128)S(1)}) fusion(f32[2048]{0:T(1024)S(1)} %copy-done.10, f32[128]{0:T(128)} %dynamic_slice.35, f32[128]{0:T(128)} %broadcast_multiply_fusion.4, bf16[768,2048]{1,0:T(8,128)(2,1)} %all-gather.4.cloned.1.call-done, bf16[768,128]{1,0:T(8,128)(2,1)} %bitcast.93), kind=kOutput, calls=%fused_computation.27 | convolution fusion | flops 404223872 | bytes 4408832 | tf_op jit(solution)/shard_map/dot_general | solution.py:43
  125.2 1.9 collective-permute-start.8
  127.1 1.0 fusion.2
  128.2 1.0 fusion.1
  129.3 1.0 fusion
  130.4 3.3 %fusion.6 = (f32[128]{0:T(128)S(1)}, f32[2048]{0:T(1024)}, f32[2048]{0:T(1024)S(1)}, f32[128]{0:T(128)S(1)}, f32[2048]{0:T(1024)S(1)}, /*index=5*/f32[128]{0:T(1...) fusion(f32[2048,128]{1,0:T(8,128)S(1)} %get-tuple-element.204, ...), kind=kOutput, calls=%fused_computation.34 | convolution fusion | flops 408933760 | bytes 8648704 | tf_op jit(solution)/shard_map/dot_general | solution.py:43
  133.7 1.9 collective-permute-start.13
  135.7 1.7 fusion.23
  137.4 2.1 collective-permute-start.18
  139.5 3.6 %fusion.8 = (f32[128]{0:T(128)S(1)}, f32[2048]{0:T(1024)}, f32[2048]{0:T(1024)}, f32[128]{0:T(128)}, f32[2048]{0:T(1024)}, /*index=5*/f32[128]{0:T(128)}, f32[2048]{0:T(1024)}, f32[128]{0:T(128)}) fusion(f32[2048,128]{1,0:T(8,128)S(1)} %get-tuple-element.205, f32[128]{0:T(128)S(1)} %get-tuple-element.159, f32[2048]{0:T(1024)S(1)} %copy-done.10, ...), kind=kLoop, calls=%fused_computation.36 | loop fusion | flops 6282752 | bytes 4274176 | tf_op jit(solution)/shard_map/reduce_sum | solution.py:53
  143.8 10.3 %collective-permute-done.18 = f32[128,768]{1,0:T(8,128)S(1)} collective-permute-done((f32[128,768]{1,0:T(8,128)S(1)}, f32[128,768]{1,0:T(8,128)S(1)}, u32[]{:S(2)}, u32[]{:S(2)}) %collective-permute-start.18) | collective-permute-done | bytes 393248 | tf_op jit(solution)/shard_map/ppermute | solution.py:12
  154.1 1.7 multiply_add_fusion.4
  155.8 1.9 collective-permute-start.19
  157.8 1.9 collective-permute-start.14
  159.7 1.9 collective-permute-start.9
  161.8 10.4 %collective-permute-done.14 = f32[128]{0:T(128)} collective-permute-done((f32[128]{0:T(128)}, f32[128]{0:T(128)}, u32[]{:S(2)}, u32[]{:S(2)}) %collective-permute-start.14) | collective-permute-done | bytes 544 | tf_op jit(solution)/shard_map/ppermute | solution.py:12
  172.9 3.0 %multiply_add_fusion.3 = f32[128,768]{1,0:T(8,128)S(1)} fusion(f32[128,768]{1,0:T(8,128)} %collective-permute-done.19, f32[128]{0:T(128)S(1)} %get-tuple-element.194, f32[128]{0:T(128)S(1)} %get-tuple-element.193, bf16[768,2048]{1,0:T(8,128)(2,1)S(1)} %copy-done, f32[2048,128]{1,0:T(8,128)} %copy-done.4, f32[128]{0:T(128)} %copy-done.27, ...), kind=kOutput, calls=%fused_computation.60 | convolution fusion | flops 403734528 | bytes 4990464 | tf_op jit(solution)/shard_map/dot_general | solution.py:55
  175.9 1.9 collective-permute-start.20
  178.0 6.7 %all-gather = f32[4,1,2048]{2,1,0:T(1,128)S(1)} all-gather(f32[1,1,2048]{2,1,0:T(1,128)S(1)} %get-tuple-element.203), channel_id=1, replica_groups=mesh['blk'=128,'feat'=4] {'feat'}, dimensions={0}, use_global_device_ids=true | all-gather | bytes 40960 | tf_op jit(solution)/shard_map/all_gather | solution.py:16
  184.7 1.9 collective-permute-start.15
  186.6 1.9 collective-permute-start.10
  188.6 6.7 %all-gather.1 = f32[4,1,2048]{2,1,0:T(1,128)S(1)} all-gather(f32[1,1,2048]{2,1,0:T(1,128)S(1)} %get-tuple-element.202), channel_id=1, replica_groups=mesh['blk'=128,'feat'=4] {'feat'}, dimensions={0}, use_global_device_ids=true | all-gather | bytes 40960 | tf_op jit(solution)/shard_map/all_gather | solution.py:16
  197.1 1.9 collective-permute-start.16
  199.0 1.9 collective-permute-start.11
  200.9 2.4 multiply_add_fusion.2
  203.3 1.9 collective-permute-start.21
  205.3 2.5 while.17
  205.3 0.8 constant_dynamic-slice_fusion.3
  206.1 0.8 constant_dynamic-slice_fusion.3
  207.0 0.8 constant_dynamic-slice_fusion.3
  209.1 20.2 %collective-permute-start.12 = (f32[128]{0:T(128)S(1)}, f32[128]{0:T(128)S(1)}, u32[]{:S(2)}, u32[]{:S(2)}) collective-permute-start(f32[128]{0:T(128)S(1)} %get-tuple-element.187), channel_id=1, source_target_pairs={{16,0},{20,4},{24,8},{28,12},{32,16},{36,20},{40,24},{44,28},{48,3... | collective-permute-start | bytes 1544 | tf_op jit(solution)/shard_map/ppermute | solution.py:12
  229.3 8.7 %collective-permute-start.17 = (f32[128]{0:T(128)S(1)}, f32[128]{0:T(128)S(1)}, u32[]{:S(2)}, u32[]{:S(2)}) collective-permute-start(f32[128]{0:T(128)S(1)} %get-tuple-element.184), channel_id=1, source_target_pairs={{16,0},{20,4},{24,8},{28,12},{32,16},{36,20},{40,24},{44,28},{48,3... | collective-permute-start | bytes 1544 | tf_op jit(solution)/shard_map/ppermute | solution.py:12
  238.1 3.0 %multiply_add_fusion.1 = f32[128,768]{1,0:T(8,128)S(1)} fusion(f32[128,768]{1,0:T(8,128)} %collective-permute-done.21, f32[128]{0:T(128)S(1)} %get-tuple-element.186, f32[128]{0:T(128)S(1)} %get-tuple-element.185, bf16[768,2048]{1,0:T(8,128)(2,1)S(1)} %copy-done, f32[2048,128]{1,0:T(8,128)} %copy-done.1, f32[128]{0:T(128)} %copy-done.24, f32[2048]{0:T(1024)} %param.9), kind=kOutput, calls=%fused_computation.58 | convolution fusion | flops 403734528 | bytes 4990464 | tf_op jit(solution)/shard_map/dot_general | solution.py:55
  241.1 1.9 collective-permute-start.22
  244.2 17.9 %collective-permute-done.22 = f32[128,768]{1,0:T(8,128)S(1)} collective-permute-done((f32[128,768]{1,0:T(8,128)S(1)}, f32[128,768]{1,0:T(8,128)S(1)}, u32[]{:S(2)}, u32[]{:S(2)}) %collective-permute-start.22) | collective-permute-done | bytes 393248 | tf_op jit(solution)/shard_map/ppermute | solution.py:12
  262.1 0.8 broadcast_divide_fusion
  (119 shorter events, 12.7 us)
Async XLA Ops:
  7.2 114.4 %copy-start.10 = (f32[2048]{0:T(1024)S(1)}, f32[2048]{0:T(1024)}, u32[]{:S(2)}) copy-start(f32[2048]{0:T(1024)} %param.9) | copy-start | bytes 24580
  7.2 114.4 %all-gather.4.cloned.1.call-start = ((), (), s32[]{:S(2)}) async-start(), calls=%async_computation.5 | async-start | bytes 3932160 | tf_op jit(solution)/shard_map/all_gather | solution.py:62
  9.6 42.3 %all-to-all-start = ((bf16[192,4,128]{2,0,1:T(8,128)(2,1)}), bf16[192,4,128]{2,0,1:T(8,128)(2,1)S(1)}, u32[]{:S(2)}, u32[]{:S(2)}) async-start(bf16[192,4,128]{2,0,1:T(8,128)(2,1)} %copy_bitcast_fusion.4), calls=%async_computation | async-start | bytes 393216 | tf_op jit(solution)/shard_map/all_to_all | solution.py:70
  13.8 38.2 %collective-permute-start = (bf16[192,512]{1,0:T(8,128)(2,1)}, bf16[192,512]{1,0:T(8,128)(2,1)S(1)}, u32[]{:S(2)}, u32[]{:S(2)}) collective-permute-start(bf16[192,512]{1,0:T(8,128)(2,1)} %param.7), channel_id=1, source_target_pairs={{508,0},{0,4},{4,8},{8,12},{12,16},{16,20},{20,24},{24,28},{28,32}... | collective-permute-start | bytes 589832 | tf_op jit(solution)/shard_map/ppermute | solution.py:12
  17.3 6.2 %collective-permute-start.1 = (f32[512]{0:T(512)}, f32[512]{0:T(512)S(1)}, u32[]{:S(2)}, u32[]{:S(2)}) collective-permute-start(f32[512]{0:T(512)} %param.8), channel_id=1, source_target_pairs={{508,0},{0,4},{4,8},{8,12},{12,16},{16,20},{20,24},{24,28},{28,32}... | collective-permute-start | bytes 6152 | tf_op jit(solution)/shard_map/ppermute | solution.py:12
  23.5 6.8 %collective-permute-start.3 = (f32[512]{0:T(512)S(1)}, f32[512]{0:T(512)S(1)}, u32[]{:S(2)}, u32[]{:S(2)}) collective-permute-start(f32[512]{0:T(512)S(1)} %collective-permute-done.1), channel_id=1, source_target_pairs={{508,0},{0,4},{4,8},{8,12},{12,16},{16,20},{20,24},{24,28},{28,32}... | collective-permute-start | bytes 6152 | tf_op jit(solution)/shard_map/ppermute | solution.py:12
  30.3 11.1 %collective-permute-start.5 = (f32[512]{0:T(512)S(1)}, f32[512]{0:T(512)S(1)}, u32[]{:S(2)}, u32[]{:S(2)}) collective-permute-start(f32[512]{0:T(512)S(1)} %collective-permute-done.3), channel_id=1, source_target_pairs={{508,0},{0,4},{4,8},{8,12},{12,16},{16,20},{20,24},{24,28},{28,32}... | collective-permute-start | bytes 6152 | tf_op jit(solution)/shard_map/ppermute | solution.py:12
  41.4 9.8 %collective-permute-start.7 = (f32[512]{0:T(512)S(1)}, f32[512]{0:T(512)S(1)}, u32[]{:S(2)}, u32[]{:S(2)}) collective-permute-start(f32[512]{0:T(512)S(1)} %collective-permute-done.5), channel_id=1, source_target_pairs={{508,0},{0,4},{4,8},{8,12},{12,16},{16,20},{20,24},{24,28},{28,32}... | collective-permute-start | bytes 6152 | tf_op jit(solution)/shard_map/ppermute | solution.py:12
  51.9 69.7 %copy-start.7 = (bf16[192,4,128]{2,0,1:T(8,128)(2,1)}, bf16[192,4,128]{2,0,1:T(8,128)(2,1)S(1)}, u32[]{:S(2)}) copy-start(bf16[192,4,128]{2,0,1:T(8,128)(2,1)S(1)} %all-to-all-done) | copy-start | bytes 589828
  52.7 11.9 %all-to-all-start.1 = ((bf16[192,4,128]{2,0,1:T(8,128)(2,1)}), bf16[192,4,128]{2,0,1:T(8,128)(2,1)S(1)}, u32[]{:S(2)}, u32[]{:S(2)}) async-start(bf16[192,4,128]{2,0,1:T(8,128)(2,1)} %copy_bitcast_fusion.3), calls=%async_computation.1 | async-start | bytes 393216 | tf_op jit(solution)/shard_map/all_to_all | solution.py:70
  57.8 13.7 %collective-permute-start.2 = (bf16[192,512]{1,0:T(8,128)(2,1)S(1)}, bf16[192,512]{1,0:T(8,128)(2,1)S(1)}, u32[]{:S(2)}, u32[]{:S(2)}) collective-permute-start(bf16[192,512]{1,0:T(8,128)(2,1)S(1)} %collective-permute-done), channel_id=1, source_target_pairs={{508,0},{0,4},{4,8},{8,12},{12,16},{16,20},{20,24},{24,28},{28,32}... | collective-permute-start | bytes 589832 | tf_op jit(solution)/shard_map/ppermute | solution.py:12
  64.6 45.0 %copy-start.8 = (bf16[192,4,128]{2,0,1:T(8,128)(2,1)}, bf16[192,4,128]{2,0,1:T(8,128)(2,1)S(1)}, u32[]{:S(2)}) copy-start(bf16[192,4,128]{2,0,1:T(8,128)(2,1)S(1)} %all-to-all-done.1) | copy-start | bytes 589828
  72.2 11.3 %all-to-all-start.2 = ((bf16[192,4,128]{2,0,1:T(8,128)(2,1)}), bf16[192,4,128]{2,0,1:T(8,128)(2,1)S(1)}, u32[]{:S(2)}, u32[]{:S(2)}) async-start(bf16[192,4,128]{2,0,1:T(8,128)(2,1)} %copy_bitcast_fusion.2), calls=%async_computation.2 | async-start | bytes 393216 | tf_op jit(solution)/shard_map/all_to_all | solution.py:70
  76.6 13.7 %collective-permute-start.4 = (bf16[192,512]{1,0:T(8,128)(2,1)S(1)}, bf16[192,512]{1,0:T(8,128)(2,1)S(1)}, u32[]{:S(2)}, u32[]{:S(2)}) collective-permute-start(bf16[192,512]{1,0:T(8,128)(2,1)S(1)} %collective-permute-done.2), channel_id=1, source_target_pairs={{508,0},{0,4},{4,8},{8,12},{12,16},{16,20},{20,24},{24,28},{28,32}... | collective-permute-start | bytes 589832 | tf_op jit(solution)/shard_map/ppermute | solution.py:12
  91.0 11.3 %all-to-all-start.3 = ((bf16[192,4,128]{2,0,1:T(8,128)(2,1)}), bf16[192,4,128]{2,0,1:T(8,128)(2,1)S(1)}, u32[]{:S(2)}, u32[]{:S(2)}) async-start(bf16[192,4,128]{2,0,1:T(8,128)(2,1)} %copy_bitcast_fusion.1), calls=%async_computation.3 | async-start | bytes 393216 | tf_op jit(solution)/shard_map/all_to_all | solution.py:70
  95.5 13.4 %collective-permute-start.6 = (bf16[192,512]{1,0:T(8,128)(2,1)S(1)}, bf16[192,512]{1,0:T(8,128)(2,1)S(1)}, u32[]{:S(2)}, u32[]{:S(2)}) collective-permute-start(bf16[192,512]{1,0:T(8,128)(2,1)S(1)} %collective-permute-done.4), channel_id=1, source_target_pairs={{508,0},{0,4},{4,8},{8,12},{12,16},{16,20},{20,24},{24,28},{28,32}... | collective-permute-start | bytes 589832 | tf_op jit(solution)/shard_map/ppermute | solution.py:12
  109.6 11.3 %all-to-all-start.4 = ((bf16[192,4,128]{2,0,1:T(8,128)(2,1)}), bf16[192,4,128]{2,0,1:T(8,128)(2,1)S(1)}, u32[]{:S(2)}, u32[]{:S(2)}) async-start(bf16[192,4,128]{2,0,1:T(8,128)(2,1)} %copy_bitcast_fusion), calls=%async_computation.4 | async-start | bytes 393216 | tf_op jit(solution)/shard_map/all_to_all | solution.py:70
  121.6 5.5 %copy-start = (bf16[768,2048]{1,0:T(8,128)(2,1)S(1)}, bf16[768,2048]{1,0:T(8,128)(2,1)}, u32[]{:S(2)}) copy-start(bf16[768,2048]{1,0:T(8,128)(2,1)} %all-gather.4.cloned.1.call-done) | copy-start | bytes 9437188
  125.2 5.2 %copy-start.21 = (f32[2048]{0:T(1024)}, f32[2048]{0:T(1024)S(1)}, u32[]{:S(2)}) copy-start(f32[2048]{0:T(1024)S(1)} %get-tuple-element.157) | copy-start | bytes 24580
  125.2 18.0 %collective-permute-start.8 = (f32[128]{0:T(128)S(1)}, f32[128]{0:T(128)S(1)}, u32[]{:S(2)}, u32[]{:S(2)}) collective-permute-start(f32[128]{0:T(128)S(1)} %get-tuple-element.156), channel_id=1, source_target_pairs={{508,0},{0,4},{4,8},{8,12},{12,16},{16,20},{20,24},{24,28},{28,32}... | collective-permute-start | bytes 1544 | tf_op jit(solution)/shard_map/ppermute | solution.py:12
  128.2 11.3 %copy-start.4 = (f32[2048,128]{1,0:T(8,128)}, f32[2048,128]{1,0:T(8,128)S(1)}, u32[]{:S(2)}) copy-start(f32[2048,128]{1,0:T(8,128)S(1)} %fusion.2) | copy-start | bytes 3145732
  128.2 1.1 copy-start.6
  128.2 1.1 copy-start.28
  129.2 10.3 %copy-start.2 = (f32[2048,128]{1,0:T(8,128)}, f32[2048,128]{1,0:T(8,128)S(1)}, u32[]{:S(2)}) copy-start(f32[2048,128]{1,0:T(8,128)S(1)} %fusion.1) | copy-start | bytes 3145732
  129.2 1.2 copy-start.9
  129.2 1.2 copy-start.30
  129.2 1.1 copy-start.31
  129.3 1.1 copy-start.32
  129.3 1.1 copy-start.33
  129.3 1.1 copy-start.34
  129.3 1.1 copy-start.35
  130.3 9.2 %copy-start.1 = (f32[2048,128]{1,0:T(8,128)}, f32[2048,128]{1,0:T(8,128)S(1)}, u32[]{:S(2)}) copy-start(f32[2048,128]{1,0:T(8,128)S(1)} %fusion) | copy-start | bytes 3145732
  133.7 9.4 %copy-start.11 = (f32[2048]{0:T(1024)}, f32[2048]{0:T(1024)S(1)}, u32[]{:S(2)}) copy-start(f32[2048]{0:T(1024)S(1)} %get-tuple-element.160) | copy-start | bytes 24580
  133.7 9.4 %copy-start.13 = (f32[2048]{0:T(1024)}, f32[2048]{0:T(1024)S(1)}, u32[]{:S(2)}) copy-start(f32[2048]{0:T(1024)S(1)} %get-tuple-element.162) | copy-start | bytes 24580
  133.7 9.4 %copy-start.15 = (f32[2048]{0:T(1024)}, f32[2048]{0:T(1024)S(1)}, u32[]{:S(2)}) copy-start(f32[2048]{0:T(1024)S(1)} %get-tuple-element.164) | copy-start | bytes 24580
  133.7 9.4 %copy-start.24 = (f32[128]{0:T(128)}, f32[128]{0:T(128)S(1)}, u32[]{:S(2)}) copy-start(f32[128]{0:T(128)S(1)} %get-tuple-element.165) | copy-start | bytes 1540
  133.7 9.4 %copy-start.25 = (f32[128]{0:T(128)}, f32[128]{0:T(128)S(1)}, u32[]{:S(2)}) copy-start(f32[128]{0:T(128)S(1)} %get-tuple-element.163) | copy-start | bytes 1540
  133.7 9.4 %copy-start.27 = (f32[128]{0:T(128)}, f32[128]{0:T(128)S(1)}, u32[]{:S(2)}) copy-start(f32[128]{0:T(128)S(1)} %get-tuple-element.161) | copy-start | bytes 1540
  133.7 9.4 %collective-permute-start.13 = (f32[128]{0:T(128)S(1)}, f32[128]{0:T(128)S(1)}, u32[]{:S(2)}, u32[]{:S(2)}) collective-permute-start(f32[128]{0:T(128)S(1)} %get-tuple-element.138), channel_id=1, source_target_pairs={{508,0},{0,4},{4,8},{8,12},{12,16},{16,20},{20,24},{24,28},{28,32}... | collective-permute-start | bytes 1544 | tf_op jit(solution)/shard_map/ppermute | solution.py:12
  137.4 16.8 %collective-permute-start.18 = (f32[128,768]{1,0:T(8,128)S(1)}, f32[128,768]{1,0:T(8,128)S(1)}, u32[]{:S(2)}, u32[]{:S(2)}) collective-permute-start(f32[128,768]{1,0:T(8,128)S(1)} %fusion.23), channel_id=1, source_target_pairs={{508,0},{0,4},{4,8},{8,12},{12,16},{16,20},{20,24},{24,28},{28,32}... | collective-permute-start | bytes 1179656 | tf_op jit(solution)/shard_map/ppermute | solution.py:12
  155.8 17.0 %collective-permute-start.19 = (f32[128,768]{1,0:T(8,128)S(1)}, f32[128,768]{1,0:T(8,128)}, u32[]{:S(2)}, u32[]{:S(2)}) collective-permute-start(f32[128,768]{1,0:T(8,128)S(1)} %multiply_add_fusion.4), channel_id=1, source_target_pairs={{508,0},{0,4},{4,8},{8,12},{12,16},{16,20},{20,24},{24,28},{28,32}... | collective-permute-start | bytes 1179656 | tf_op jit(solution)/shard_map/ppermute | solution.py:12
  157.8 14.4 %collective-permute-start.14 = (f32[128]{0:T(128)}, f32[128]{0:T(128)}, u32[]{:S(2)}, u32[]{:S(2)}) collective-permute-start(f32[128]{0:T(128)} %get-tuple-element.196), channel_id=1, source_target_pairs={{508,0},{0,4},{4,8},{8,12},{12,16},{16,20},{20,24},{24,28},{28,32}... | collective-permute-start | bytes 1544 | tf_op jit(solution)/shard_map/ppermute | solution.py:12
  159.7 12.5 %collective-permute-start.9 = (f32[128]{0:T(128)}, f32[128]{0:T(128)}, u32[]{:S(2)}, u32[]{:S(2)}) collective-permute-start(f32[128]{0:T(128)} %get-tuple-element.199), channel_id=1, source_target_pairs={{508,0},{0,4},{4,8},{8,12},{12,16},{16,20},{20,24},{24,28},{28,32}... | collective-permute-start | bytes 1544 | tf_op jit(solution)/shard_map/ppermute | solution.py:12
  161.6 16.2 %copy-start.12 = (f32[2048]{0:T(1024)S(1)}, f32[2048]{0:T(1024)}, u32[]{:S(2)}) copy-start(f32[2048]{0:T(1024)} %copy-done.11) | copy-start | bytes 24580
  161.6 16.2 %copy-start.14 = (f32[2048]{0:T(1024)S(1)}, f32[2048]{0:T(1024)}, u32[]{:S(2)}) copy-start(f32[2048]{0:T(1024)} %copy-done.13) | copy-start | bytes 24580
  161.7 16.2 %copy-start.16 = (f32[2048]{0:T(1024)S(1)}, f32[2048]{0:T(1024)}, u32[]{:S(2)}) copy-start(f32[2048]{0:T(1024)} %copy-done.15) | copy-start | bytes 24580
  161.7 16.2 %copy-start.17 = (f32[2048]{0:T(1024)S(1)}, f32[2048]{0:T(1024)}, u32[]{:S(2)}) copy-start(f32[2048]{0:T(1024)} %get-tuple-element.141) | copy-start | bytes 24580
  161.7 16.2 %copy-start.18 = (f32[2048]{0:T(1024)S(1)}, f32[2048]{0:T(1024)}, u32[]{:S(2)}) copy-start(f32[2048]{0:T(1024)} %get-tuple-element.166) | copy-start | bytes 24580
  161.7 16.2 %copy-start.19 = (f32[2048]{0:T(1024)S(1)}, f32[2048]{0:T(1024)}, u32[]{:S(2)}) copy-start(f32[2048]{0:T(1024)} %get-tuple-element.168) | copy-start | bytes 24580
  161.7 16.2 %copy-start.20 = (f32[2048]{0:T(1024)S(1)}, f32[2048]{0:T(1024)}, u32[]{:S(2)}) copy-start(f32[2048]{0:T(1024)} %get-tuple-element.170) | copy-start | bytes 24580
  161.7 16.2 %copy-start.22 = (f32[2048]{0:T(1024)S(1)}, f32[2048]{0:T(1024)}, u32[]{:S(2)}) copy-start(f32[2048]{0:T(1024)} %copy-done.21) | copy-start | bytes 24580
  161.7 16.2 %copy-start.23 = (f32[2048]{0:T(1024)S(1)}, f32[2048]{0:T(1024)}, u32[]{:S(2)}) copy-start(f32[2048]{0:T(1024)} %get-tuple-element.139) | copy-start | bytes 24580
  161.7 34.8 %copy-start.26 = (f32[128]{0:T(128)S(1)}, f32[128]{0:T(128)}, u32[]{:S(2)}) copy-start(f32[128]{0:T(128)} %copy-done.25) | copy-start | bytes 1540
  161.7 34.8 %copy-start.29 = (f32[128]{0:T(128)S(1)}, f32[128]{0:T(128)}, u32[]{:S(2)}) copy-start(f32[128]{0:T(128)} %get-tuple-element.169) | copy-start | bytes 1540
  161.7 39.2 %copy-start.3 = (f32[2048,128]{1,0:T(8,128)S(1)}, f32[2048,128]{1,0:T(8,128)}, u32[]{:S(2)}) copy-start(f32[2048,128]{1,0:T(8,128)} %copy-done.2) | copy-start | bytes 3145732
  175.9 25.0 %collective-permute-start.20 = (f32[128,768]{1,0:T(8,128)S(1)}, f32[128,768]{1,0:T(8,128)S(1)}, u32[]{:S(2)}, u32[]{:S(2)}) collective-permute-start(f32[128,768]{1,0:T(8,128)S(1)} %multiply_add_fusion.3), channel_id=1, source_target_pairs={{508,0},{0,4},{4,8},{8,12},{12,16},{16,20},{20,24},{24,28},{28,32}... | collective-permute-start | bytes 1179656 | tf_op jit(solution)/shard_map/ppermute | solution.py:12
  184.7 11.8 %collective-permute-start.15 = (f32[128]{0:T(128)S(1)}, f32[128]{0:T(128)S(1)}, u32[]{:S(2)}, u32[]{:S(2)}) collective-permute-start(f32[128]{0:T(128)S(1)} %get-tuple-element.192), channel_id=1, source_target_pairs={{508,0},{0,4},{4,8},{8,12},{12,16},{16,20},{20,24},{24,28},{28,32}... | collective-permute-start | bytes 1544 | tf_op jit(solution)/shard_map/ppermute | solution.py:12
  186.6 9.9 %collective-permute-start.10 = (f32[128]{0:T(128)S(1)}, f32[128]{0:T(128)S(1)}, u32[]{:S(2)}, u32[]{:S(2)}) collective-permute-start(f32[128]{0:T(128)S(1)} %get-tuple-element.195), channel_id=1, source_target_pairs={{508,0},{0,4},{4,8},{8,12},{12,16},{16,20},{20,24},{24,28},{28,32}... | collective-permute-start | bytes 1544 | tf_op jit(solution)/shard_map/ppermute | solution.py:12
  197.1 10.7 %collective-permute-start.16 = (f32[128]{0:T(128)}, f32[128]{0:T(128)}, u32[]{:S(2)}, u32[]{:S(2)}) collective-permute-start(f32[128]{0:T(128)} %get-tuple-element.188), channel_id=1, source_target_pairs={{508,0},{0,4},{4,8},{8,12},{12,16},{16,20},{20,24},{24,28},{28,32}... | collective-permute-start | bytes 1544 | tf_op jit(solution)/shard_map/ppermute | solution.py:12
  199.0 9.4 %collective-permute-start.11 = (f32[128]{0:T(128)}, f32[128]{0:T(128)}, u32[]{:S(2)}, u32[]{:S(2)}) collective-permute-start(f32[128]{0:T(128)} %get-tuple-element.191), channel_id=1, source_target_pairs={{508,0},{0,4},{4,8},{8,12},{12,16},{16,20},{20,24},{24,28},{28,32}... | collective-permute-start | bytes 1544 | tf_op jit(solution)/shard_map/ppermute | solution.py:12
  203.3 34.7 %collective-permute-start.21 = (f32[128,768]{1,0:T(8,128)S(1)}, f32[128,768]{1,0:T(8,128)}, u32[]{:S(2)}, u32[]{:S(2)}) collective-permute-start(f32[128,768]{1,0:T(8,128)S(1)} %multiply_add_fusion.2), channel_id=1, source_target_pairs={{508,0},{0,4},{4,8},{8,12},{12,16},{16,20},{20,24},{24,28},{28,32}... | collective-permute-start | bytes 1179656 | tf_op jit(solution)/shard_map/ppermute | solution.py:12
  209.1 34.5 %collective-permute-start.12 = (f32[128]{0:T(128)S(1)}, f32[128]{0:T(128)S(1)}, u32[]{:S(2)}, u32[]{:S(2)}) collective-permute-start(f32[128]{0:T(128)S(1)} %get-tuple-element.187), channel_id=1, source_target_pairs={{16,0},{20,4},{24,8},{28,12},{32,16},{36,20},{40,24},{44,28},{48,3... | collective-permute-start | bytes 1544 | tf_op jit(solution)/shard_map/ppermute | solution.py:12
  229.3 14.3 %collective-permute-start.17 = (f32[128]{0:T(128)S(1)}, f32[128]{0:T(128)S(1)}, u32[]{:S(2)}, u32[]{:S(2)}) collective-permute-start(f32[128]{0:T(128)S(1)} %get-tuple-element.184), channel_id=1, source_target_pairs={{16,0},{20,4},{24,8},{28,12},{32,16},{36,20},{40,24},{44,28},{48,3... | collective-permute-start | bytes 1544 | tf_op jit(solution)/shard_map/ppermute | solution.py:12
  241.1 21.0 %collective-permute-start.22 = (f32[128,768]{1,0:T(8,128)S(1)}, f32[128,768]{1,0:T(8,128)S(1)}, u32[]{:S(2)}, u32[]{:S(2)}) collective-permute-start(f32[128,768]{1,0:T(8,128)S(1)} %multiply_add_fusion.1), channel_id=1, source_target_pairs={{16,0},{20,4},{24,8},{28,12},{32,16},{36,20},{40,24},{44,28},{48,3... | collective-permute-start | bytes 1179656 | tf_op jit(solution)/shard_map/ppermute | solution.py:12
  (1 other events, 0.7 us)
Sparse Core Ops, SparseCore 0:
  10.1 42.3 all-gather.3
where the time goes:
time: 271 us; the launch traced here: 270 us
  starting transfers between devices  100 us (37%)
  waiting for transfers between devices  96.9 us (36%)
  matrix products  21.8 us (8%)
  between operations  14.8 us (5%)
  blocking collectives  13.4 us (5%)
  local copies, waits for them, and re-layouts  12.2 us (5%)
  other arithmetic  10.3 us (4%)
    ppermute x23, starting transfers between devices, from_behind(): return lax.ppermute(block, axis, route)  77.7 us
    ppermute x23, waiting for transfers between devices, from_behind(): return lax.ppermute(block, axis, route)  75.6 us
    all_to_all x5, starting transfers between devices, local_terms(): lax.all_to_all(panel_held, 'feat', split_axis=1, concat_axis=0, tiled=True)  22.7 us
    all_to_all x5, waiting for transfers between devices, local_terms(): lax.all_to_all(panel_held, 'feat', split_axis=1, concat_axis=0, tiled=True)  20.6 us
    all_gather x2, blocking collectives, combined_all(): everything = jax.tree.map(lambda part: lax.all_gather(part, axis), array)  13.4 us
    dot_general x5, matrix products, pair_terms(): lax.dot_general(weight, full_points, (((0,), (1,)), ((), ())), preferred_...  11.8 us
    dot_general x5, matrix products, pair_terms(): lax.dot_general(full_points, panel_cols, (((0,), (0,)), ((), ())), prefer...  9.95 us
  transfers between devices with their start and end apart: 29, of which 15 were waited for; matrix products, arithmetic and copies ran while one was open for 13% of the time, Pallas kernels for 0%

commit v1 on v0

v1 whole, which is shorter than its diff:
```python
import functools

import jax
import jax.numpy as jnp
from jax import lax
from jax.experimental import pallas as pl
from jax.experimental.pallas import tpu as pltpu
from jax.sharding import PartitionSpec as P

HOPS = 4
EXTRA = 16
CHUNK = 512
STAT = 128


def shifted(block, distance):
    size = lax.axis_size("blk")
    return lax.ppermute(block, "blk", [(i, (i + distance) % size) for i in range(size)])


def swapped(block, mask):
    size = lax.axis_size("feat")
    return lax.ppermute(block, "feat", [(i, i ^ mask) for i in range(size)])


def three_terms(value):
    high = value.astype(jnp.bfloat16).astype(jnp.float32)
    rest = value - high
    middle = rest.astype(jnp.bfloat16).astype(jnp.float32)
    return high, middle, rest - middle


def stat_lanes(lse):
    high, middle, low = three_terms(lse)
    lane = lax.broadcasted_iota(jnp.int32, (lse.shape[0], STAT), 1)
    return jnp.where(lane == 0, high, jnp.where(lane == 1, middle, jnp.where(lane == 2, low, 0.0)))


def split_kernel(cent, pot, *outs):
    member = lax.axis_index("feat")
    quarter = outs[0].shape[1]
    for mask in range(4):
        start = pl.multiple_of((member ^ mask) * quarter, quarter)
        outs[mask][...] = cent[:, pl.ds(start, quarter)]
    own = pot[:, pl.ds(pl.multiple_of(member * quarter, quarter), quarter)]
    high, middle, low = three_terms(own)
    row = lax.broadcasted_iota(jnp.int32, (EXTRA, quarter), 0)
    rows = jnp.where(row == 0, high, jnp.where(row == 1, middle, jnp.where(row == 2, low, 0.0)))
    outs[4][...] = rows.astype(jnp.bfloat16)


def split_panel(centroids, col_pot):
    depth, width = centroids.shape
    quarter = width // 4
    piece = jax.ShapeDtypeStruct((depth, quarter), centroids.dtype)
    return pl.pallas_call(
        split_kernel,
        out_shape=(piece,) * 4 + (jax.ShapeDtypeStruct((EXTRA, quarter), jnp.bfloat16),),
        name="split_panel",
    )(centroids, col_pot[None, :])


def pair_kernel(scale, first, *refs):
    pts = refs[:4]
    if first:
        panel, row_pot, packed, row_out, scores = refs[4:]
    else:
        panel, row_pot, row_in, packed, row_out, scores = refs[4:]
    depth, count = pts[0].shape
    features = 4 * depth
    turned = panel[...].T
    cols = turned[:, :features]
    extra = turned[:, features : features + 3].astype(jnp.float32)
    potential = jnp.sum(extra, axis=1, keepdims=True)
    wide = cols.astype(jnp.float32)
    bias = (-0.5 * scale) * jnp.sum(wide * wide, axis=1, keepdims=True)
    top = None
    for at in range(0, count, CHUNK):
        here = pl.ds(at, CHUNK)
        score = None
        for m in range(4):
            part = jnp.dot(
                cols[:, depth * m : depth * (m + 1)], pts[m][:, here], preferred_element_type=jnp.float32
            )
            score = part if score is None else score + part
        score = score * scale + bias
        row_terms = score + potential
        row_max = jnp.max(row_terms, axis=0, keepdims=True)
        row_sum = jnp.sum(jnp.exp(row_terms - row_max), axis=0, keepdims=True)
        row_part = row_max + jnp.log(row_sum)
        if not first:
            before = row_in[:, here]
            larger = jnp.maximum(before, row_part)
            row_part = larger + jnp.log(jnp.exp(before - larger) + jnp.exp(row_part - larger))
        row_out[:, here] = row_part
        col_terms = score - row_pot[:, here]
        scores[:, here] = col_terms
        for j in range(0, CHUNK, 128):
            lane_part = col_terms[:, j : j + 128]
            top = lane_part if top is None else jnp.maximum(top, lane_part)
    col_max = jnp.max(top, axis=1, keepdims=True)
    lane_sum = None
    acc = [None] * 4
    for at in range(0, count, CHUNK):
        here = pl.ds(at, CHUNK)
        expo = jnp.exp(scores[:, here] - col_max)
        for j in range(0, CHUNK, 128):
            lane_part = expo[:, j : j + 128]
            lane_sum = lane_part if lane_sum is None else lane_sum + lane_part
        weight = expo.astype(jnp.bfloat16)
        for m in range(4):
            part = lax.dot_general(
                weight, pts[m][:, here], (((1,), (1,)), ((), ())), preferred_element_type=jnp.float32
            )
            acc[m] = part if acc[m] is None else acc[m] + part
    col_sum = jnp.sum(lane_sum, axis=1, keepdims=True)
    inverse = 1.0 / col_sum
    for m in range(4):
        packed[:, depth * m : depth * (m + 1)] = acc[m] * inverse
    packed[:, features:] = stat_lanes(col_max + jnp.log(col_sum))


def pair(points, panel, row_pot, row_in, name):
    depth, count = points[0].shape
    features = 4 * depth
    quarter = panel.shape[1]
    operands = (*points, panel, row_pot) + (() if row_in is None else (row_in,))
    return pl.pallas_call(
        functools.partial(pair_kernel, 1.0 / (0.02 * features), row_in is None),
        out_shape=(
            jax.ShapeDtypeStruct((quarter, features + STAT), jnp.float32),
            jax.ShapeDtypeStruct((1, count), jnp.float32),
        ),
        scratch_shapes=[pltpu.VMEM((quarter, count), jnp.float32)],
        compiler_params=pltpu.CompilerParams(vmem_limit_bytes=24 * 2**20),
        cost_estimate=pl.CostEstimate(
            flops=4 * features * count * quarter, bytes_accessed=8 * 2**20, transcendentals=2 * count * quarter
        ),
        name=name,
    )(*operands)


def half(packed):
    return packed.astype(jnp.float16)


def whole(packed):
    return packed.astype(jnp.float32)


def merge_kernel(count, final, *refs):
    features = refs[0].shape[1] - STAT
    stats = [ref[:, features : features + 3] for ref in refs[:count]]
    lses = [jnp.sum(stat, axis=1, keepdims=True) for stat in stats]
    top = functools.reduce(jnp.maximum, lses)
    weights = [jnp.exp(lse - top) for lse in lses]
    total = functools.reduce(jnp.add, weights)
    inverse = 1.0 / total
    lse = top + jnp.log(total)
    mean = None
    for weight, ref in zip(weights, refs[:count]):
        part = ref[:, :features] * (weight * inverse)
        mean = part if mean is None else mean + part
    if not final:
        packed = refs[count]
        packed[:, :features] = mean
        packed[:, features:] = stat_lanes(lse)
        return
    mean_out, lse_out = refs[count:]
    lse_out[...] = jnp.broadcast_to(lse, (lse.shape[0], lse.shape[0])).T[:1, :]
    member = lax.axis_index("feat")
    depth = features // 4
    for at in range(4):

        @pl.when(member == at)
        def _():
            for m in range(4):
                mean_out[:, depth * (m ^ at) : depth * ((m ^ at) + 1)] = mean[:, depth * m : depth * (m + 1)]


def merge(parts, final, name):
    quarter, width = parts[0].shape
    if final:
        shapes = (
            jax.ShapeDtypeStruct((quarter, width - STAT), jnp.float32),
            jax.ShapeDtypeStruct((1, quarter), jnp.float32),
        )
    else:
        shapes = jax.ShapeDtypeStruct((quarter, width), jnp.float32)
    return pl.pallas_call(
        functools.partial(merge_kernel, len(parts), final),
        out_shape=shapes,
        cost_estimate=pl.CostEstimate(
            flops=2 * len(parts) * quarter * width,
            bytes_accessed=4 * (len(parts) + 1) * quarter * width,
            transcendentals=0,
        ),
        name=name,
    )(*parts)


def local(points, centroids, col_pot, row_pot):
    depth, count = points.shape
    features = 4 * depth
    member = lax.axis_index("feat")
    across = swapped(points, 2)
    pieces = split_panel(centroids, col_pot)
    panel0 = jnp.concatenate(
        [pieces[0]] + [swapped(pieces[mask], mask) for mask in (1, 2, 3)] + [pieces[4]], axis=0
    )
    beside = swapped(points, 1)
    panel1 = shifted(panel0, 1)
    panel4 = shifted(panel0, 4)
    panel2 = shifted(panel1, 1)
    diagonal = swapped(across, 1)
    panel3 = shifted(panel2, 1)
    full = (points, beside, across, diagonal)
    pot = row_pot[None, :]
    part4, rows = pair(full, panel4, pot, None, "pair4")
    back4 = shifted(half(part4), -4)
    part1, rows = pair(full, panel1, pot, rows, "pair1")
    back1 = shifted(half(part1), -1)
    part0, rows = pair(full, panel0, pot, rows, "pair0")
    part2, rows = pair(full, panel2, pot, rows, "pair2")
    part3, rows = pair(full, panel3, pot, rows, "pair3")
    back3 = whole(shifted(half(part3), -1))
    both = merge((part2, back3), False, "merge_pair")
    back2 = whole(shifted(half(both), -2))
    row_parts = lax.all_gather(rows[0], "feat")
    row_top = jnp.max(row_parts, axis=0)
    row_lse = row_top + jnp.log(jnp.sum(jnp.exp(row_parts - row_top[None, :]), axis=0))
    mean, col_lse = merge((part0, whole(back1), whole(back4), back2), True, "merge_last")
    return (row_lse, col_lse[0], mean)


def solution(mesh):
    return jax.shard_map(
        local,
        mesh=mesh,
        in_specs=(P("feat", "blk"), P("feat", "blk"), P("blk"), P("blk")),
        out_specs=(P("blk"), P(("blk", "feat")), P(("blk", "feat"), None)),
        check_vma=False,
    )
```

time: 271 us -> 129 us (0.48)
  the two profiles are of different devices: /device:TPU:16 before, /device:TPU:8 now
where the time goes in v1:
time: 129 us; the launch traced here: 128 us
  starting transfers between devices  63.7 us (49%)
  waiting for transfers between devices  29.2 us (23%)
  Pallas kernels  18.3 us (14%)
  blocking collectives  6.7 us (5%)
  other arithmetic  5.04 us (4%)
  local copies, waits for them, and re-layouts  4.17 us (3%)
    ppermute x8, starting transfers between devices, shifted(): lax.ppermute(block, 'blk', [(i, (i + distance) % size) for i in range(siz...  45.8 us
    ppermute x8, waiting for transfers between devices, shifted(): lax.ppermute(block, 'blk', [(i, (i + distance) % size) for i in range(siz...  23.6 us
    ppermute x6, starting transfers between devices, swapped(): return lax.ppermute(block, 'feat', [(i, i ^ mask) for i in range(size)])  17.8 us
    pallas_call x5, Pallas kernels, pair(): pl.pallas_call(functools.partial(pair_kernel, 1.0 / (0.02 * features), ro...  12.1 us
    all_gather x1, blocking collectives, local(): row_parts = lax.all_gather(rows[0], 'feat')  6.7 us
    ppermute x6, waiting for transfers between devices, swapped(): return lax.ppermute(block, 'feat', [(i, i ^ mask) for i in range(size)])  5.55 us
    pallas_call x2, Pallas kernels, merge(): pl.pallas_call(functools.partial(merge_kernel, len(parts), final), out_sh...  4.58 us
    unnamed x14, local copies, waits for them, and re-layouts  4.16 us
  transfers between devices with their start and end apart: 14, of which 5 were waited for; matrix products, arithmetic and copies ran while one was open for 4% of the time, Pallas kernels for 10%

profile of v1, /device:TPU:8, one launch (start us, length us, event | category | flops | bytes accessed | tf_op | source)
XLA Modules:
  0.0 128.0 jit_solution(16674005789186299958)
XLA Ops:
  0.6 4.9 %collective-permute-start.1 = (bf16[192,2048]{1,0:T(8,128)(2,1)}, bf16[192,2048]{1,0:T(8,128)(2,1)S(1)}, u32[]{:S(2)}, u32[]{:S(2)}) collective-permute-start(bf16[192,2048]{1,0:T(8,128)(2,1)} %refs_0_.9), channel_id=1, source_target_pairs={{0,2},{1,3},{2,0},{3,1},{4,6},{5,7},{6,4},{7,5},{8,10},{9,11},{10,... | collective-permute-start | bytes 2359304 | tf_op jit(solution)/shard_map/ppermute | solution.py:23
  5.6 1.9 %collective-permute-start = (bf16[192,2048]{1,0:T(8,128)(2,1)}, bf16[192,2048]{1,0:T(8,128)(2,1)S(1)}, u32[]{:S(2)}, u32[]{:S(2)}) collective-permute-start(bf16[192,2048]{1,0:T(8,128)(2,1)} %refs_0_.9), channel_id=1, source_target_pairs={{0,1},{1,0},{2,3},{3,2},{4,5},{5,4},{6,7},{7,6},{8,9},{9,8},{10,11... | collective-permute-start | bytes 2359304 | tf_op jit(solution)/shard_map/ppermute | solution.py:23
  7.5 1.6 %split_panel.1 = (bf16[192,128]{1,0:T(8,128)(2,1)}, bf16[192,128]{1,0:T(8,128)(2,1)}, bf16[192,128]{1,0:T(8,128)(2,1)}, bf16[192,128]{1,0:T(8,128)(2,1)}, bf16[16,128]{1,0:T(8,128)(2,1)}) custom-call(bf16[192,512]{1,0:T(8,128)(2,1)} %cent.1, f32[1,512]{1,0:T(1,128)} %bitcast.16), custom_call_target="tpu_custom_call" | custom-call | tf_op jit(solution)/shard_map/split_panel/pallas_call | solution.py:56
  9.1 2.4 %collective-permute-start.3 = (bf16[192,128]{1,0:T(8,128)(2,1)}, bf16[192,128]{1,0:T(8,128)(2,1)S(1)}, u32[]{:S(2)}, u32[]{:S(2)}) collective-permute-start(bf16[192,128]{1,0:T(8,128)(2,1)} %get-tuple-element.21), channel_id=1, source_target_pairs={{0,1},{1,0},{2,3},{3,2},{4,5},{5,4},{6,7},{7,6},{8,9},{9,8},{10,11... | collective-permute-start | bytes 147464 | tf_op jit(solution)/shard_map/ppermute | solution.py:23
  11.5 2.4 %collective-permute-start.4 = (bf16[192,128]{1,0:T(8,128)(2,1)}, bf16[192,128]{1,0:T(8,128)(2,1)S(1)}, u32[]{:S(2)}, u32[]{:S(2)}) collective-permute-start(bf16[192,128]{1,0:T(8,128)(2,1)} %get-tuple-element.22), channel_id=1, source_target_pairs={{0,2},{1,3},{2,0},{3,1},{4,6},{5,7},{6,4},{7,5},{8,10},{9,11},{10,... | collective-permute-start | bytes 147464 | tf_op jit(solution)/shard_map/ppermute | solution.py:23
  14.0 4.3 %collective-permute-start.5 = (bf16[192,128]{1,0:T(8,128)(2,1)}, bf16[192,128]{1,0:T(8,128)(2,1)S(1)}, u32[]{:S(2)}, u32[]{:S(2)}) collective-permute-start(bf16[192,128]{1,0:T(8,128)(2,1)} %get-tuple-element.23), channel_id=1, source_target_pairs={{0,3},{1,2},{2,1},{3,0},{4,7},{5,6},{6,5},{7,4},{8,11},{9,10},{10,... | collective-permute-start | bytes 147464 | tf_op jit(solution)/shard_map/ppermute | solution.py:23
  18.2 0.8 constant_dynamic-update-slice_fusion.4
  19.0 5.5 %collective-permute-done.1.refs_2_ = bf16[192,2048]{1,0:T(8,128)(2,1)S(1)} collective-permute-done((bf16[192,2048]{1,0:T(8,128)(2,1)}, bf16[192,2048]{1,0:T(8,128)(2,1)S(1)}, u32[]{:S(2)}, u32[]{:S(2)}) %collective-permute-start.1) | collective-permute-done | bytes 786464 | tf_op jit(solution)/shard_map/ppermute | solution.py:23
  24.6 1.9 %collective-permute-start.2 = (bf16[192,2048]{1,0:T(8,128)(2,1)S(1)}, bf16[192,2048]{1,0:T(8,128)(2,1)S(1)}, u32[]{:S(2)}, u32[]{:S(2)}) collective-permute-start(bf16[192,2048]{1,0:T(8,128)(2,1)S(1)} %collective-permute-done.1.refs_2_), channel_id=1, source_target_pairs={{0,1},{1,0},{2,3},{3,2},{4,5},{5,4},{6,7},{7,6},{8,9},{9,8},{10,11... | collective-permute-start | bytes 2359304 | tf_op jit(solution)/shard_map/ppermute | solution.py:23
  26.5 0.0 collective-permute-done.3
  26.5 0.0 collective-permute-done.4
  26.5 0.0 collective-permute-done.5
  26.6 0.0 copy-start.4
  26.6 0.0 copy-start.3
  26.6 0.6 copy-done.4
  27.3 3.5 %collective-permute-start.6 = (bf16[784,128]{1,0:T(8,128)(2,1)S(1)}, bf16[784,128]{1,0:T(8,128)(2,1)S(1)}, u32[]{:S(2)}, u32[]{:S(2)}) collective-permute-start(bf16[784,128]{1,0:T(8,128)(2,1)S(1)} %constant_dynamic-update-slice_fusion.refs_4_), channel_id=1, source_target_pairs={{0,4},{4,8},{8,12},{12,16},{16,20},{20,24},{24,28},{28,32},{32,36}... | collective-permute-start | bytes 602120 | tf_op jit(solution)/shard_map/ppermute | solution.py:18
  30.7 5.8 %collective-permute-done.6.refs_4_ = bf16[784,128]{1,0:T(8,128)(2,1)S(1)} collective-permute-done((bf16[784,128]{1,0:T(8,128)(2,1)S(1)}, bf16[784,128]{1,0:T(8,128)(2,1)S(1)}, u32[]{:S(2)}, u32[]{:S(2)}) %collective-permute-start.6) | collective-permute-done | bytes 200736 | tf_op jit(solution)/shard_map/ppermute | solution.py:18
  36.5 3.5 %collective-permute-start.7 = (bf16[784,128]{1,0:T(8,128)(2,1)S(1)}, bf16[784,128]{1,0:T(8,128)(2,1)S(1)}, u32[]{:S(2)}, u32[]{:S(2)}) collective-permute-start(bf16[784,128]{1,0:T(8,128)(2,1)S(1)} %collective-permute-done.6.refs_4_), channel_id=1, source_target_pairs={{0,4},{4,8},{8,12},{12,16},{16,20},{20,24},{24,28},{28,32},{32,36}... | collective-permute-start | bytes 602120 | tf_op jit(solution)/shard_map/ppermute | solution.py:18
  40.0 5.9 %collective-permute-start.9 = (bf16[784,128]{1,0:T(8,128)(2,1)S(1)}, bf16[784,128]{1,0:T(8,128)(2,1)S(1)}, u32[]{:S(2)}, u32[]{:S(2)}) collective-permute-start(bf16[784,128]{1,0:T(8,128)(2,1)S(1)} %constant_dynamic-update-slice_fusion.refs_4_), channel_id=1, source_target_pairs={{0,16},{4,20},{8,24},{12,28},{16,32},{20,36},{24,40},{28,44},{32,4... | collective-permute-start | bytes 602120 | tf_op jit(solution)/shard_map/ppermute | solution.py:18
  46.0 13.0 %collective-permute-done.7.refs_4_ = bf16[784,128]{1,0:T(8,128)(2,1)S(1)} collective-permute-done((bf16[784,128]{1,0:T(8,128)(2,1)S(1)}, bf16[784,128]{1,0:T(8,128)(2,1)S(1)}, u32[]{:S(2)}, u32[]{:S(2)}) %collective-permute-start.7) | collective-permute-done | bytes 200736 | tf_op jit(solution)/shard_map/ppermute | solution.py:18
  59.0 1.9 %collective-permute-start.8 = (bf16[784,128]{1,0:T(8,128)(2,1)S(1)}, bf16[784,128]{1,0:T(8,128)(2,1)S(1)}, u32[]{:S(2)}, u32[]{:S(2)}) collective-permute-start(bf16[784,128]{1,0:T(8,128)(2,1)S(1)} %collective-permute-done.7.refs_4_), channel_id=1, source_target_pairs={{0,4},{4,8},{8,12},{12,16},{16,20},{20,24},{24,28},{28,32},{32,36}... | collective-permute-start | bytes 602120 | tf_op jit(solution)/shard_map/ppermute | solution.py:18
  60.9 0.0 collective-permute-done.9.refs_4_
  60.9 0.0 collective-permute-done.refs_1_
  60.9 0.0 collective-permute-done.2.refs_3_
  61.0 0.0 copy-done.3
  61.0 0.0 copy-start
  61.0 1.1 copy-done
  62.1 2.4 %pair4.1 = (f32[128,896]{1,0:T(8,128)S(1)}, f32[1,2048]{1,0:T(1,128)S(1)}) custom-call(bf16[192,2048]{1,0:T(8,128)(2,1)S(1)} %copy-done, bf16[192,2048]{1,0:T(8,128)(2,1)S(1)} %collective-permute-done.refs_1_, bf16[192,2048]{1,0:T(8,128)(2,1)S(1)} %collective-permute-done.1.refs_2_, bf16[192,2048]{1,0:T(8,128)(2,1)S(1)} %collective-permute-done.2.refs_3_, ...), custom_call_target="tpu_custom_call" | custom-call | flops 805306368 | bytes 8388608 | tf_op jit(solution)/shard_map/pair4/pallas_call | solution.py:128
  64.5 2.4 %pair1.1 = (f32[128,896]{1,0:T(8,128)S(1)}, f32[1,2048]{1,0:T(1,128)S(1)}) custom-call(bf16[192,2048]{1,0:T(8,128)(2,1)S(1)} %copy-done, bf16[192,2048]{1,0:T(8,128)(2,1)S(1)} %collective-permute-done.refs_1_, bf16[192,2048]{1,0:T(8,128)(2,1)S(1)} %collective-permute-done.1.refs_2_, bf16[192,2048]{1,0:T(8,128)(2,1)S(1)} %collective-permute-done.2.refs_3_, ...), custom_call_target="tpu_custom_call" | custom-call | flops 805306368 | bytes 8388608 | tf_op jit(solution)/shard_map/pair1/pallas_call | solution.py:128
  66.9 2.4 %pair0.1 = (f32[128,896]{1,0:T(8,128)S(1)}, f32[1,2048]{1,0:T(1,128)S(1)}) custom-call(bf16[192,2048]{1,0:T(8,128)(2,1)S(1)} %copy-done, bf16[192,2048]{1,0:T(8,128)(2,1)S(1)} %collective-permute-done.refs_1_, bf16[192,2048]{1,0:T(8,128)(2,1)S(1)} %collective-permute-done.1.refs_2_, bf16[192,2048]{1,0:T(8,128)(2,1)S(1)} %collective-permute-done.2.refs_3_, ...), custom_call_target="tpu_custom_call" | custom-call | flops 805306368 | bytes 8388608 | tf_op jit(solution)/shard_map/pair0/pallas_call | solution.py:128
  69.4 0.0 copy-start.1
  69.4 0.8 copy-done.1
  70.1 2.4 %pair2.1 = (f32[128,896]{1,0:T(8,128)S(1)}, f32[1,2048]{1,0:T(1,128)S(1)}) custom-call(bf16[192,2048]{1,0:T(8,128)(2,1)S(1)} %copy-done, bf16[192,2048]{1,0:T(8,128)(2,1)S(1)} %collective-permute-done.refs_1_, bf16[192,2048]{1,0:T(8,128)(2,1)S(1)} %collective-permute-done.1.refs_2_, bf16[192,2048]{1,0:T(8,128)(2,1)S(1)} %collective-permute-done.2.refs_3_, ...), custom_call_target="tpu_custom_call" | custom-call | flops 805306368 | bytes 8388608 | tf_op jit(solution)/shard_map/pair2/pallas_call | solution.py:128
  72.6 0.0 copy-start.2
  72.6 0.8 copy-done.2
  73.3 1.8 %collective-permute-done.8.refs_4_ = bf16[784,128]{1,0:T(8,128)(2,1)S(1)} collective-permute-done((bf16[784,128]{1,0:T(8,128)(2,1)S(1)}, bf16[784,128]{1,0:T(8,128)(2,1)S(1)}, u32[]{:S(2)}, u32[]{:S(2)}) %collective-permute-start.8) | collective-permute-done | bytes 200736 | tf_op jit(solution)/shard_map/ppermute | solution.py:18
  75.1 2.4 %pair3.1 = (f32[128,896]{1,0:T(8,128)S(1)}, f32[1,2048]{1,0:T(1,128)S(1)}) custom-call(bf16[192,2048]{1,0:T(8,128)(2,1)S(1)} %copy-done, bf16[192,2048]{1,0:T(8,128)(2,1)S(1)} %collective-permute-done.refs_1_, bf16[192,2048]{1,0:T(8,128)(2,1)S(1)} %collective-permute-done.1.refs_2_, bf16[192,2048]{1,0:T(8,128)(2,1)S(1)} %collective-permute-done.2.refs_3_, ...), custom_call_target="tpu_custom_call" | custom-call | flops 805306368 | bytes 8388608 | tf_op jit(solution)/shard_map/pair3/pallas_call | solution.py:128
  77.6 10.7 %collective-permute-start.12 = (f16[128,896]{1,0:T(8,128)(2,1)S(1)}, f16[128,896]{1,0:T(8,128)(2,1)S(1)}, u32[]{:S(2)}, u32[]{:S(2)}) collective-permute-start(f16[128,896]{1,0:T(8,128)(2,1)S(1)} %convert_element_type.28), channel_id=1, source_target_pairs={{0,508},{4,0},{8,4},{12,8},{16,12},{20,16},{24,20},{28,24},{32,28}... | collective-permute-start | bytes 688136 | tf_op jit(solution)/shard_map/ppermute | solution.py:18
  88.3 3.9 %collective-permute-start.11 = (f16[128,896]{1,0:T(8,128)(2,1)S(1)}, f16[128,896]{1,0:T(8,128)(2,1)S(1)}, u32[]{:S(2)}, u32[]{:S(2)}) collective-permute-start(f16[128,896]{1,0:T(8,128)(2,1)S(1)} %convert_element_type.26), channel_id=1, source_target_pairs={{0,496},{4,500},{8,504},{12,508},{16,0},{20,4},{24,8},{28,12},{32,... | collective-permute-start | bytes 688136 | tf_op jit(solution)/shard_map/ppermute | solution.py:18
  92.2 6.2 %collective-permute-start.10 = (f16[128,896]{1,0:T(8,128)(2,1)S(1)}, f16[128,896]{1,0:T(8,128)(2,1)S(1)}, u32[]{:S(2)}, u32[]{:S(2)}) collective-permute-start(f16[128,896]{1,0:T(8,128)(2,1)S(1)} %convert_element_type.24), channel_id=1, source_target_pairs={{0,508},{4,0},{8,4},{12,8},{16,12},{20,16},{24,20},{28,24},{32,28}... | collective-permute-start | bytes 688136 | tf_op jit(solution)/shard_map/ppermute | solution.py:18
  98.4 6.7 %all-gather = f32[4,1,2048]{2,1,0:T(1,128)S(1)} all-gather(f32[1,1,2048]{2,1,0:T(1,128)S(1)} %bitcast.15), channel_id=1, replica_groups=mesh['blk'=128,'feat'=4] {'feat'}, dimensions={0}, use_global_device_ids=true | all-gather | bytes 40960 | tf_op jit(solution)/shard_map/all_gather | solution.py:229
  105.1 0.0 collective-permute-done.12
  105.1 0.8 convert_element_type.29.refs_1_
  105.9 2.1 %merge_pair.1 = f32[128,896]{1,0:T(8,128)} custom-call(f32[128,896]{1,0:T(8,128)} %copy-done.2, f32[128,896]{1,0:T(8,128)} %convert_element_type.29.refs_1_), custom_call_target="tpu_custom_call" | custom-call | flops 458752 | bytes 1376256 | tf_op jit(solution)/shard_map/merge_pair/pallas_call | solution.py:190
  108.0 1.0 convert_element_type.30
  109.1 10.3 %collective-permute-start.13 = (f16[128,896]{1,0:T(8,128)(2,1)S(1)}, f16[128,896]{1,0:T(8,128)(2,1)S(1)}, u32[]{:S(2)}, u32[]{:S(2)}) collective-permute-start(f16[128,896]{1,0:T(8,128)(2,1)S(1)} %convert_element_type.30), channel_id=1, source_target_pairs={{0,504},{4,508},{8,0},{12,4},{16,8},{20,12},{24,16},{28,20},{32,24... | collective-permute-start | bytes 688136 | tf_op jit(solution)/shard_map/ppermute | solution.py:18
  119.5 0.6 log_add_fusion
  120.1 0.0 collective-permute-done.11
  120.1 0.8 convert_element_type.27.refs_2_
  120.9 0.0 collective-permute-done.10
  120.9 0.8 convert_element_type.25.refs_1_
  121.7 3.0 %collective-permute-done.13 = f16[128,896]{1,0:T(8,128)(2,1)S(1)} collective-permute-done((f16[128,896]{1,0:T(8,128)(2,1)S(1)}, f16[128,896]{1,0:T(8,128)(2,1)S(1)}, u32[]{:S(2)}, u32[]{:S(2)}) %collective-permute-start.13) | collective-permute-done | bytes 229408 | tf_op jit(solution)/shard_map/ppermute | solution.py:18
  124.7 0.8 convert_element_type.31.refs_3_
  125.5 2.5 %merge_last.1 = (f32[128,768]{1,0:T(8,128)}, f32[1,128]{1,0:T(1,128)}) custom-call(f32[128,896]{1,0:T(8,128)} %copy-done.1, f32[128,896]{1,0:T(8,128)} %convert_element_type.25.refs_1_, f32[128,896]{1,0:T(8,128)} %convert_element_type.27.refs_2_, f32[128,896]{1,0:T(8,128)} %convert_element_type.31.refs_3_), custom_call_target="tpu_custom_call" | custom-call | flops 917504 | bytes 2293760 | tf_op jit(solution)/shard_map/merge_last/pallas_call | solution.py:190
  (9 shorter events, 0.2 us)
Async XLA Ops:
  0.6 23.9 %collective-permute-start.1 = (bf16[192,2048]{1,0:T(8,128)(2,1)}, bf16[192,2048]{1,0:T(8,128)(2,1)S(1)}, u32[]{:S(2)}, u32[]{:S(2)}) collective-permute-start(bf16[192,2048]{1,0:T(8,128)(2,1)} %refs_0_.9), channel_id=1, source_target_pairs={{0,2},{1,3},{2,0},{3,1},{4,6},{5,7},{6,4},{7,5},{8,10},{9,11},{10,... | collective-permute-start | bytes 2359304 | tf_op jit(solution)/shard_map/ppermute | solution.py:23
  5.6 55.4 %collective-permute-start = (bf16[192,2048]{1,0:T(8,128)(2,1)}, bf16[192,2048]{1,0:T(8,128)(2,1)S(1)}, u32[]{:S(2)}, u32[]{:S(2)}) collective-permute-start(bf16[192,2048]{1,0:T(8,128)(2,1)} %refs_0_.9), channel_id=1, source_target_pairs={{0,1},{1,0},{2,3},{3,2},{4,5},{5,4},{6,7},{7,6},{8,9},{9,8},{10,11... | collective-permute-start | bytes 2359304 | tf_op jit(solution)/shard_map/ppermute | solution.py:23
  9.1 17.4 %collective-permute-start.3 = (bf16[192,128]{1,0:T(8,128)(2,1)}, bf16[192,128]{1,0:T(8,128)(2,1)S(1)}, u32[]{:S(2)}, u32[]{:S(2)}) collective-permute-start(bf16[192,128]{1,0:T(8,128)(2,1)} %get-tuple-element.21), channel_id=1, source_target_pairs={{0,1},{1,0},{2,3},{3,2},{4,5},{5,4},{6,7},{7,6},{8,9},{9,8},{10,11... | collective-permute-start | bytes 147464 | tf_op jit(solution)/shard_map/ppermute | solution.py:23
  11.5 15.0 %collective-permute-start.4 = (bf16[192,128]{1,0:T(8,128)(2,1)}, bf16[192,128]{1,0:T(8,128)(2,1)S(1)}, u32[]{:S(2)}, u32[]{:S(2)}) collective-permute-start(bf16[192,128]{1,0:T(8,128)(2,1)} %get-tuple-element.22), channel_id=1, source_target_pairs={{0,2},{1,3},{2,0},{3,1},{4,6},{5,7},{6,4},{7,5},{8,10},{9,11},{10,... | collective-permute-start | bytes 147464 | tf_op jit(solution)/shard_map/ppermute | solution.py:23
  14.0 12.6 %collective-permute-start.5 = (bf16[192,128]{1,0:T(8,128)(2,1)}, bf16[192,128]{1,0:T(8,128)(2,1)S(1)}, u32[]{:S(2)}, u32[]{:S(2)}) collective-permute-start(bf16[192,128]{1,0:T(8,128)(2,1)} %get-tuple-element.23), channel_id=1, source_target_pairs={{0,3},{1,2},{2,1},{3,0},{4,7},{5,6},{6,5},{7,4},{8,11},{9,10},{10,... | collective-permute-start | bytes 147464 | tf_op jit(solution)/shard_map/ppermute | solution.py:23
  24.6 36.4 %collective-permute-start.2 = (bf16[192,2048]{1,0:T(8,128)(2,1)S(1)}, bf16[192,2048]{1,0:T(8,128)(2,1)S(1)}, u32[]{:S(2)}, u32[]{:S(2)}) collective-permute-start(bf16[192,2048]{1,0:T(8,128)(2,1)S(1)} %collective-permute-done.1.refs_2_), channel_id=1, source_target_pairs={{0,1},{1,0},{2,3},{3,2},{4,5},{5,4},{6,7},{7,6},{8,9},{9,8},{10,11... | collective-permute-start | bytes 2359304 | tf_op jit(solution)/shard_map/ppermute | solution.py:23
  26.6 0.7 copy-start.4
  26.6 34.4 %copy-start.3 = (f32[2048]{0:T(1024)S(1)}, f32[2048]{0:T(1024)}, u32[]{:S(2)}) copy-start(f32[2048]{0:T(1024)} %param.7) | copy-start | bytes 24580
  27.3 9.3 %collective-permute-start.6 = (bf16[784,128]{1,0:T(8,128)(2,1)S(1)}, bf16[784,128]{1,0:T(8,128)(2,1)S(1)}, u32[]{:S(2)}, u32[]{:S(2)}) collective-permute-start(bf16[784,128]{1,0:T(8,128)(2,1)S(1)} %constant_dynamic-update-slice_fusion.refs_4_), channel_id=1, source_target_pairs={{0,4},{4,8},{8,12},{12,16},{16,20},{20,24},{24,28},{28,32},{32,36}... | collective-permute-start | bytes 602120 | tf_op jit(solution)/shard_map/ppermute | solution.py:18
  36.5 22.5 %collective-permute-start.7 = (bf16[784,128]{1,0:T(8,128)(2,1)S(1)}, bf16[784,128]{1,0:T(8,128)(2,1)S(1)}, u32[]{:S(2)}, u32[]{:S(2)}) collective-permute-start(bf16[784,128]{1,0:T(8,128)(2,1)S(1)} %collective-permute-done.6.refs_4_), channel_id=1, source_target_pairs={{0,4},{4,8},{8,12},{12,16},{16,20},{20,24},{24,28},{28,32},{32,36}... | collective-permute-start | bytes 602120 | tf_op jit(solution)/shard_map/ppermute | solution.py:18
  40.0 20.9 %collective-permute-start.9 = (bf16[784,128]{1,0:T(8,128)(2,1)S(1)}, bf16[784,128]{1,0:T(8,128)(2,1)S(1)}, u32[]{:S(2)}, u32[]{:S(2)}) collective-permute-start(bf16[784,128]{1,0:T(8,128)(2,1)S(1)} %constant_dynamic-update-slice_fusion.refs_4_), channel_id=1, source_target_pairs={{0,16},{4,20},{8,24},{12,28},{16,32},{20,36},{24,40},{28,44},{32,4... | collective-permute-start | bytes 602120 | tf_op jit(solution)/shard_map/ppermute | solution.py:18
  59.0 16.1 %collective-permute-start.8 = (bf16[784,128]{1,0:T(8,128)(2,1)S(1)}, bf16[784,128]{1,0:T(8,128)(2,1)S(1)}, u32[]{:S(2)}, u32[]{:S(2)}) collective-permute-start(bf16[784,128]{1,0:T(8,128)(2,1)S(1)} %collective-permute-done.7.refs_4_), channel_id=1, source_target_pairs={{0,4},{4,8},{8,12},{12,16},{16,20},{20,24},{24,28},{28,32},{32,36}... | collective-permute-start | bytes 602120 | tf_op jit(solution)/shard_map/ppermute | solution.py:18
  61.0 1.1 copy-start
  69.4 0.8 copy-start.1
  72.6 0.8 copy-start.2
  77.6 27.5 %collective-permute-start.12 = (f16[128,896]{1,0:T(8,128)(2,1)S(1)}, f16[128,896]{1,0:T(8,128)(2,1)S(1)}, u32[]{:S(2)}, u32[]{:S(2)}) collective-permute-start(f16[128,896]{1,0:T(8,128)(2,1)S(1)} %convert_element_type.28), channel_id=1, source_target_pairs={{0,508},{4,0},{8,4},{12,8},{16,12},{20,16},{24,20},{28,24},{32,28}... | collective-permute-start | bytes 688136 | tf_op jit(solution)/shard_map/ppermute | solution.py:18
  88.3 31.8 %collective-permute-start.11 = (f16[128,896]{1,0:T(8,128)(2,1)S(1)}, f16[128,896]{1,0:T(8,128)(2,1)S(1)}, u32[]{:S(2)}, u32[]{:S(2)}) collective-permute-start(f16[128,896]{1,0:T(8,128)(2,1)S(1)} %convert_element_type.26), channel_id=1, source_target_pairs={{0,496},{4,500},{8,504},{12,508},{16,0},{20,4},{24,8},{28,12},{32,... | collective-permute-start | bytes 688136 | tf_op jit(solution)/shard_map/ppermute | solution.py:18
  92.2 28.7 %collective-permute-start.10 = (f16[128,896]{1,0:T(8,128)(2,1)S(1)}, f16[128,896]{1,0:T(8,128)(2,1)S(1)}, u32[]{:S(2)}, u32[]{:S(2)}) collective-permute-start(f16[128,896]{1,0:T(8,128)(2,1)S(1)} %convert_element_type.24), channel_id=1, source_target_pairs={{0,508},{4,0},{8,4},{12,8},{16,12},{20,16},{24,20},{28,24},{32,28}... | collective-permute-start | bytes 688136 | tf_op jit(solution)/shard_map/ppermute | solution.py:18
  109.1 15.6 %collective-permute-start.13 = (f16[128,896]{1,0:T(8,128)(2,1)S(1)}, f16[128,896]{1,0:T(8,128)(2,1)S(1)}, u32[]{:S(2)}, u32[]{:S(2)}) collective-permute-start(f16[128,896]{1,0:T(8,128)(2,1)S(1)} %convert_element_type.30), channel_id=1, source_target_pairs={{0,504},{4,508},{8,0},{12,4},{16,8},{20,12},{24,16},{28,20},{32,24... | collective-permute-start | bytes 688136 | tf_op jit(solution)/shard_map/ppermute | solution.py:18

commit v2 on v1

v2 whole, which is shorter than its diff:
```python
import functools

import jax
import jax.numpy as jnp
from jax import lax
from jax.experimental import pallas as pl
from jax.experimental.pallas import tpu as pltpu
from jax.sharding import PartitionSpec as P

HOPS = 4
EXTRA = 16
CHUNK = 512
STAT = 128


def shifted(block, distance):
    size = lax.axis_size("blk")
    return lax.ppermute(block, "blk", [(i, (i + distance) % size) for i in range(size)])


def swapped(block, mask):
    size = lax.axis_size("feat")
    return lax.ppermute(block, "feat", [(i, i ^ mask) for i in range(size)])


def three_terms(value):
    high = value.astype(jnp.bfloat16).astype(jnp.float32)
    rest = value - high
    middle = rest.astype(jnp.bfloat16).astype(jnp.float32)
    return high, middle, rest - middle


def stat_lanes(lse):
    high, middle, low = three_terms(lse)
    lane = lax.broadcasted_iota(jnp.int32, (lse.shape[0], STAT), 1)
    return jnp.where(lane == 0, high, jnp.where(lane == 1, middle, jnp.where(lane == 2, low, 0.0)))


def stat_sum(packed):
    features = packed.shape[1] - STAT
    return jnp.sum(packed[:, features : features + 3], axis=1, keepdims=True)


def joined(lses):
    top = functools.reduce(jnp.maximum, lses)
    weights = [jnp.exp(lse - top) for lse in lses]
    total = functools.reduce(jnp.add, weights)
    return [weight / total for weight in weights], top + jnp.log(total)


def split_kernel(cent, pot, out):
    depth, quarter = cent.shape[0], out.shape[2]
    for at in range(out.shape[0]):
        cut = slice(at * quarter, (at + 1) * quarter)
        out[at, :depth, :] = cent[:, cut]
        high, middle, low = three_terms(pot[:, cut])
        row = lax.broadcasted_iota(jnp.int32, (EXTRA, quarter), 0)
        rows = jnp.where(row == 0, high, jnp.where(row == 1, middle, jnp.where(row == 2, low, 0.0)))
        out[at, depth:, :] = rows.astype(jnp.bfloat16)


def split_panel(centroids, col_pot):
    depth, width = centroids.shape
    return pl.pallas_call(
        split_kernel,
        out_shape=jax.ShapeDtypeStruct((4, depth + EXTRA, width // 4), centroids.dtype),
        compiler_params=pltpu.CompilerParams(vmem_limit_bytes=4 * 2**20),
        name="split_panel",
    )(centroids, col_pot[None, :])


def hand_on_kernel(value, *refs):
    refs[-1][...] = value[...]


def hand_on(value, arrays, name):
    return pl.pallas_call(
        hand_on_kernel,
        in_specs=[pl.BlockSpec(memory_space=pltpu.VMEM)] + [pl.BlockSpec(memory_space=pl.ANY)] * len(arrays),
        out_shape=jax.ShapeDtypeStruct(value.shape, value.dtype),
        compiler_params=pltpu.CompilerParams(vmem_limit_bytes=2**20),
        cost_estimate=pl.CostEstimate(flops=10**11, bytes_accessed=2**28, transcendentals=10**8),
        name=name,
    )(value, *arrays)


def pair_kernel(scale, first, *refs):
    pts = refs[:4]
    panel, row_pot = refs[4:6]
    packed, row_out, scores = refs[-3:]
    row_in = None if first else refs[6]
    arrived = refs[6 if first else 7 : -3]
    depth, count = pts[0].shape
    features = 4 * depth
    member = lax.axis_index("feat")
    cols = []
    squares = None
    for m in range(4):
        turned = panel[member ^ m].T
        cols.append(turned[:, :depth])
        wide = turned[:, :depth].astype(jnp.float32)
        part = jnp.sum(wide * wide, axis=1, keepdims=True)
        squares = part if squares is None else squares + part
    extra = turned[:, depth : depth + 3].astype(jnp.float32)
    potential = jnp.sum(extra, axis=1, keepdims=True)
    bias = (-0.5 * scale) * squares
    top = None
    for at in range(0, count, CHUNK):
        here = pl.ds(at, CHUNK)
        score = None
        for m in range(4):
            part = jnp.dot(cols[m], pts[m][:, here], preferred_element_type=jnp.float32)
            score = part if score is None else score + part
        score = score * scale + bias
        row_terms = score + potential
        row_max = jnp.max(row_terms, axis=0, keepdims=True)
        row_sum = jnp.sum(jnp.exp(row_terms - row_max), axis=0, keepdims=True)
        row_part = row_max + jnp.log(row_sum)
        if not first:
            before = row_in[:, here]
            larger = jnp.maximum(before, row_part)
            row_part = larger + jnp.log(jnp.exp(before - larger) + jnp.exp(row_part - larger))
        row_out[:, here] = row_part
        col_terms = score - row_pot[:, here]
        scores[:, here] = col_terms
        for j in range(0, CHUNK, 128):
            lane_part = col_terms[:, j : j + 128]
            top = lane_part if top is None else jnp.maximum(top, lane_part)
    col_max = jnp.max(top, axis=1, keepdims=True)
    lane_sum = None
    acc = [None] * 4
    for at in range(0, count, CHUNK):
        here = pl.ds(at, CHUNK)
        expo = jnp.exp(scores[:, here] - col_max)
        for j in range(0, CHUNK, 128):
            lane_part = expo[:, j : j + 128]
            lane_sum = lane_part if lane_sum is None else lane_sum + lane_part
        weight = expo.astype(jnp.bfloat16)
        for m in range(4):
            part = lax.dot_general(
                weight, pts[m][:, here], (((1,), (1,)), ((), ())), preferred_element_type=jnp.float32
            )
            acc[m] = part if acc[m] is None else acc[m] + part
    col_sum = jnp.sum(lane_sum, axis=1, keepdims=True)
    lse = col_max + jnp.log(col_sum)
    scales, lse = joined([lse] + [stat_sum(ref) for ref in arrived])
    scales[0] = scales[0] / col_sum
    for m in range(4):
        cut = slice(depth * m, depth * (m + 1))
        mean = acc[m] * scales[0]
        for scaling, ref in zip(scales[1:], arrived):
            mean = mean + ref[:, cut] * scaling
        packed[:, cut] = mean
    packed[:, features:] = stat_lanes(lse)


def pair(points, panel, row_pot, row_in, name, arrived=()):
    depth, count = points[0].shape
    features = 4 * depth
    quarter = panel.shape[2]
    operands = (*points, panel, row_pot)
    operands += () if row_in is None else (row_in,)
    operands += tuple(arrived)
    return pl.pallas_call(
        functools.partial(pair_kernel, 1.0 / (0.02 * features), row_in is None),
        out_shape=(
            jax.ShapeDtypeStruct((quarter, features + STAT), jnp.float32),
            jax.ShapeDtypeStruct((1, count), jnp.float32),
        ),
        scratch_shapes=[pltpu.VMEM((quarter, count), jnp.float32)],
        compiler_params=pltpu.CompilerParams(vmem_limit_bytes=12 * 2**20),
        cost_estimate=pl.CostEstimate(flops=1, bytes_accessed=1, transcendentals=0),
        name=name,
    )(*operands)


def half(packed):
    return packed.astype(jnp.float16)


def whole(packed):
    return packed.astype(jnp.float32)


def merge_kernel(*refs):
    parts, mean_out, lse_out = refs[:-2], refs[-2], refs[-1]
    features = mean_out.shape[1]
    scales, lse = joined([stat_sum(part) for part in parts])
    mean = functools.reduce(jnp.add, [part[:, :features] * scaling for part, scaling in zip(parts, scales)])
    lse_out[...] = jnp.broadcast_to(lse, (lse.shape[0], lse.shape[0])).T[:1, :]
    member = lax.axis_index("feat")
    depth = features // 4
    for at in range(4):

        @pl.when(member == at)
        def _():
            for m in range(4):
                mean_out[:, depth * (m ^ at) : depth * ((m ^ at) + 1)] = mean[:, depth * m : depth * (m + 1)]


def merge(parts):
    quarter, width = parts[0].shape
    return pl.pallas_call(
        merge_kernel,
        out_shape=(
            jax.ShapeDtypeStruct((quarter, width - STAT), jnp.float32),
            jax.ShapeDtypeStruct((1, quarter), jnp.float32),
        ),
        compiler_params=pltpu.CompilerParams(vmem_limit_bytes=8 * 2**20),
        cost_estimate=pl.CostEstimate(flops=1, bytes_accessed=1, transcendentals=0),
        name="merge_last",
    )(*parts)


def rows_kernel(parts, out):
    top = jnp.max(parts[...], axis=0, keepdims=True)
    out[...] = top + jnp.log(jnp.sum(jnp.exp(parts[...] - top), axis=0, keepdims=True))


def rows_merged(parts):
    return pl.pallas_call(
        rows_kernel,
        out_shape=jax.ShapeDtypeStruct((1, parts.shape[1]), jnp.float32),
        compiler_params=pltpu.CompilerParams(vmem_limit_bytes=2**20),
        cost_estimate=pl.CostEstimate(flops=1, bytes_accessed=1, transcendentals=0),
        name="rows_merged",
    )(parts)[0]


def after(value, earlier):
    return lax.optimization_barrier((value, earlier))[0]


def local(points, centroids, col_pot, row_pot):
    panel0 = lax.all_to_all(split_panel(centroids, col_pot), "feat", split_axis=0, concat_axis=0, tiled=True)
    panel4 = shifted(panel0, 4)
    across = swapped(after(points, panel0), 2)
    panel1 = shifted(panel0, 1)
    beside = swapped(after(points, panel0), 1)
    panel2 = shifted(panel1, 1)
    pot = hand_on(row_pot[None, :], (panel4,), "far_panel")
    panel3 = shifted(after(panel4, pot), -1)
    diagonal = swapped(across, 1)
    pot = hand_on(pot, (panel3, panel2), "all_panels")
    full = (points, beside, across, diagonal)
    part4, rows = pair(full, panel4, pot, None, "pair4")
    back4 = whole(shifted(half(part4), -4))
    part3, rows = pair(full, panel3, pot, rows, "pair3")
    next3 = whole(shifted(half(part3), -1))
    part1, rows = pair(full, panel1, pot, rows, "pair1")
    back1 = whole(shifted(half(part1), -1))
    part0, rows = pair(full, panel0, pot, rows, "pair0")
    part2, rows = pair(full, panel2, pot, rows, "pair2", (next3,))
    back2 = whole(shifted(half(part2), -2))
    row_lse = rows_merged(lax.all_gather(rows, "feat", axis=0, tiled=True))
    mean, col_lse = merge((part0, back1, back4, back2))
    return (row_lse, col_lse[0], mean)


def solution(mesh):
    return jax.shard_map(
        local,
        mesh=mesh,
        in_specs=(P("feat", "blk"), P("feat", "blk"), P("blk"), P("blk")),
        out_specs=(P("blk"), P(("blk", "feat")), P(("blk", "feat"), None)),
        check_vma=False,
    )
```

time: 129 us -> 101 us (0.78)
  starting transfers between devices: 63.7 us -> 45.7 us
  blocking collectives: 6.7 us -> 17.8 us
  waiting for transfers between devices: 29.2 us -> 20.1 us
  other arithmetic: 5.04 us -> 0.24 us
  Pallas kernels: 18.3 us -> 13.7 us
  local copies, waits for them, and re-layouts: 4.17 us -> 1.7 us
    ppermute x6 -> x3, starting transfers between devices: 17.8 us -> 6.1 us  [swapped(): return lax.ppermute(block, 'feat', [(i, i ^ mask) for i in range(size)])]
    all_to_all x0 -> x1, blocking collectives: none -> 11.1 us  [local(): lax.all_to_all(split_panel(centroids, col_pot), 'feat', split_axis=0, con...]
    ppermute x8, starting transfers between devices: 45.8 us -> 39.6 us  [shifted(): lax.ppermute(block, 'blk', [(i, (i + distance) % size) for i in range(siz...]
    ppermute x8, waiting for transfers between devices: 23.6 us -> 18.6 us  [shifted(): lax.ppermute(block, 'blk', [(i, (i + distance) % size) for i in range(siz...]
    pallas_call x3 -> x5, Pallas kernels: 6.22 us -> 1.77 us  [the longest x1 1.06 us: merge(): pl.pallas_call(merge_kernel, out_shape=(jax.ShapeDtypeStruct((quarter, wi...]
    ppermute x6 -> x3, waiting for transfers between devices: 5.55 us -> 1.5 us  [swapped(): return lax.ppermute(block, 'feat', [(i, i ^ mask) for i in range(size)])]
    convert_element_type x4, other arithmetic: 3.23 us -> 0.13 us  [whole(): return packed.astype(jnp.float32)]
    unnamed x14 -> x9, local copies, waits for them, and re-layouts: 4.16 us -> 1.7 us
  transfers between devices with their start and end apart: 14 -> 11, of which waited for: 5 -> 6; matrix products, arithmetic and copies ran while one was open for 4% -> 0% of each run, Pallas kernels for 10% -> 8%
where the time goes in v2:
time: 101 us; the launch traced here: 100 us
  starting transfers between devices  45.7 us (45%)
  waiting for transfers between devices  20.1 us (20%)
  blocking collectives  17.8 us (18%)
  Pallas kernels  13.7 us (14%)
  local copies, waits for them, and re-layouts  1.7 us (2%)
    ppermute x8, starting transfers between devices, shifted(): lax.ppermute(block, 'blk', [(i, (i + distance) % size) for i in range(siz...  39.6 us
    ppermute x8, waiting for transfers between devices, shifted(): lax.ppermute(block, 'blk', [(i, (i + distance) % size) for i in range(siz...  18.6 us
    pallas_call x5, Pallas kernels, pair(): pl.pallas_call(functools.partial(pair_kernel, 1.0 / (0.02 * features), ro...  11.9 us
    all_to_all x1, blocking collectives, local(): lax.all_to_all(split_panel(centroids, col_pot), 'feat', split_axis=0, con...  11.1 us
    all_gather x1, blocking collectives, local(): row_lse = rows_merged(lax.all_gather(rows, 'feat', axis=0, tiled=True))  6.7 us
    ppermute x3, starting transfers between devices, swapped(): return lax.ppermute(block, 'feat', [(i, i ^ mask) for i in range(size)])  6.1 us
  transfers between devices with their start and end apart: 11, of which 6 were waited for; matrix products, arithmetic and copies ran while one was open for 0% of the time, Pallas kernels for 8%

profile of v2, /device:TPU:8, one launch (start us, length us, event | category | flops | bytes accessed | tf_op | source)
XLA Modules:
  0.0 100.1 jit_solution(1448777243120509194)
XLA Ops:
  0.6 0.0 copy-start
  0.6 0.0 copy-start.1
  0.7 1.0 copy-done.1
  1.6 0.0 copy-start.2
  1.6 0.7 copy-done.2
  2.4 0.0 copy-start.3
  2.4 11.1 %all_to_all.5.refs_4_ = bf16[4,208,128]{2,1,0:T(8,128)(2,1)S(1)} all-to-all(bf16[4,208,128]{2,1,0:T(8,128)(2,1)S(1)} %split_panel.1), channel_id=1, replica_groups=mesh['blk'=128,'feat'=4] {'feat'}, dimensions={0} | all-to-all | bytes 425984 | tf_op jit(solution)/shard_map/all_to_all | solution.py:235
  13.5 6.8 %collective-permute-start.5 = (bf16[4,208,128]{2,1,0:T(8,128)(2,1)S(1)}, bf16[4,208,128]{2,1,0:T(8,128)(2,1)S(1)}, u32[]{:S(2)}, u32[]{:S(2)}) collective-permute-start(bf16[4,208,128]{2,1,0:T(8,128)(2,1)S(1)} %all_to_all.5.refs_4_), channel_id=1, source_target_pairs={{0,16},{4,20},{8,24},{12,28},{16,32},{20,36},{24,40},{28,44},{32,4... | collective-permute-start | bytes 638984 | tf_op jit(solution)/shard_map/ppermute | solution.py:18
  20.3 0.0 copy-done
  20.3 2.3 %collective-permute-start.1 = (bf16[192,2048]{1,0:T(8,128)(2,1)S(1)}, bf16[192,2048]{1,0:T(8,128)(2,1)S(1)}, u32[]{:S(2)}, u32[]{:S(2)}) collective-permute-start(bf16[192,2048]{1,0:T(8,128)(2,1)S(1)} %copy-done), channel_id=1, source_target_pairs={{0,2},{1,3},{2,0},{3,1},{4,6},{5,7},{6,4},{7,5},{8,10},{9,11},{10,... | collective-permute-start | bytes 2359304 | tf_op jit(solution)/shard_map/ppermute | solution.py:23
  22.6 2.6 %collective-permute-start.3 = (bf16[4,208,128]{2,1,0:T(8,128)(2,1)S(1)}, bf16[4,208,128]{2,1,0:T(8,128)(2,1)S(1)}, u32[]{:S(2)}, u32[]{:S(2)}) collective-permute-start(bf16[4,208,128]{2,1,0:T(8,128)(2,1)S(1)} %all_to_all.5.refs_4_), channel_id=1, source_target_pairs={{0,4},{4,8},{8,12},{12,16},{16,20},{20,24},{24,28},{28,32},{32,36}... | collective-permute-start | bytes 638984 | tf_op jit(solution)/shard_map/ppermute | solution.py:18
  25.2 13.4 %collective-permute-done.5.refs_0_.refs_4_ = bf16[4,208,128]{2,1,0:T(8,128)(2,1)S(1)} collective-permute-done((bf16[4,208,128]{2,1,0:T(8,128)(2,1)S(1)}, bf16[4,208,128]{2,1,0:T(8,128)(2,1)S(1)}, u32[]{:S(2)}, u32[]{:S(2)}) %collective-permute-start.5) | collective-permute-done | bytes 213024 | tf_op jit(solution)/shard_map/ppermute | solution.py:18
  38.6 0.0 copy-done.3
  38.6 1.9 %collective-permute-start.6 = (bf16[4,208,128]{2,1,0:T(8,128)(2,1)S(1)}, bf16[4,208,128]{2,1,0:T(8,128)(2,1)S(1)}, u32[]{:S(2)}, u32[]{:S(2)}) collective-permute-start(bf16[4,208,128]{2,1,0:T(8,128)(2,1)S(1)} %collective-permute-done.5.refs_0_.refs_4_), channel_id=1, source_target_pairs={{0,508},{4,0},{8,4},{12,8},{16,12},{20,16},{24,20},{28,24},{32,28}... | collective-permute-start | bytes 638984 | tf_op jit(solution)/shard_map/ppermute | solution.py:18
  40.5 0.0 collective-permute-done.3.refs_4_
  40.6 3.9 %collective-permute-start.4 = (bf16[4,208,128]{2,1,0:T(8,128)(2,1)S(1)}, bf16[4,208,128]{2,1,0:T(8,128)(2,1)S(1)}, u32[]{:S(2)}, u32[]{:S(2)}) collective-permute-start(bf16[4,208,128]{2,1,0:T(8,128)(2,1)S(1)} %collective-permute-done.3.refs_4_), channel_id=1, source_target_pairs={{0,4},{4,8},{8,12},{12,16},{16,20},{20,24},{24,28},{28,32},{32,36}... | collective-permute-start | bytes 638984 | tf_op jit(solution)/shard_map/ppermute | solution.py:18
  44.5 1.9 %collective-permute-start = (bf16[192,2048]{1,0:T(8,128)(2,1)S(1)}, bf16[192,2048]{1,0:T(8,128)(2,1)S(1)}, u32[]{:S(2)}, u32[]{:S(2)}) collective-permute-start(bf16[192,2048]{1,0:T(8,128)(2,1)S(1)} %copy-done), channel_id=1, source_target_pairs={{0,1},{1,0},{2,3},{3,2},{4,5},{5,4},{6,7},{7,6},{8,9},{9,8},{10,11... | collective-permute-start | bytes 2359304 | tf_op jit(solution)/shard_map/ppermute | solution.py:23
  46.4 0.7 collective-permute-done.1.refs_2_
  47.1 1.9 %collective-permute-start.2 = (bf16[192,2048]{1,0:T(8,128)(2,1)S(1)}, bf16[192,2048]{1,0:T(8,128)(2,1)S(1)}, u32[]{:S(2)}, u32[]{:S(2)}) collective-permute-start(bf16[192,2048]{1,0:T(8,128)(2,1)S(1)} %collective-permute-done.1.refs_2_), channel_id=1, source_target_pairs={{0,1},{1,0},{2,3},{3,2},{4,5},{5,4},{6,7},{7,6},{8,9},{9,8},{10,11... | collective-permute-start | bytes 2359304 | tf_op jit(solution)/shard_map/ppermute | solution.py:23
  49.1 0.0 collective-permute-done.6.refs_0_.refs_4_
  49.1 1.5 %collective-permute-done.4.refs_1_.refs_4_ = bf16[4,208,128]{2,1,0:T(8,128)(2,1)S(1)} collective-permute-done((bf16[4,208,128]{2,1,0:T(8,128)(2,1)S(1)}, bf16[4,208,128]{2,1,0:T(8,128)(2,1)S(1)}, u32[]{:S(2)}, u32[]{:S(2)}) %collective-permute-start.4) | collective-permute-done | bytes 213024 | tf_op jit(solution)/shard_map/ppermute | solution.py:18
  50.5 0.0 collective-permute-done.refs_1_
  50.5 0.8 collective-permute-done.2.refs_3_
  51.3 2.4 %pair4.1 = (f32[128,896]{1,0:T(8,128)S(1)}, f32[1,2048]{1,0:T(1,128)S(1)}) custom-call(bf16[192,2048]{1,0:T(8,128)(2,1)S(1)} %copy-done, bf16[192,2048]{1,0:T(8,128)(2,1)S(1)} %collective-permute-done.refs_1_, bf16[192,2048]{1,0:T(8,128)(2,1)S(1)} %collective-permute-done.1.refs_2_, bf16[192,2048]{1,0:T(8,128)(2,1)S(1)} %collective-permute-done.2.refs_3_, ...), custom_call_target="tpu_custom_call" | custom-call | flops 1 | bytes 1 | tf_op jit(solution)/shard_map/pair4/pallas_call | solution.py:164
  53.7 2.4 %pair3.1 = (f32[128,896]{1,0:T(8,128)S(1)}, f32[1,2048]{1,0:T(1,128)S(1)}) custom-call(bf16[192,2048]{1,0:T(8,128)(2,1)S(1)} %copy-done, bf16[192,2048]{1,0:T(8,128)(2,1)S(1)} %collective-permute-done.refs_1_, bf16[192,2048]{1,0:T(8,128)(2,1)S(1)} %collective-permute-done.1.refs_2_, bf16[192,2048]{1,0:T(8,128)(2,1)S(1)} %collective-permute-done.2.refs_3_, ...), custom_call_target="tpu_custom_call" | custom-call | flops 1 | bytes 1 | tf_op jit(solution)/shard_map/pair3/pallas_call | solution.py:164
  56.1 12.4 %collective-permute-start.7 = (f16[128,896]{1,0:T(8,128)(2,1)S(1)}, f16[128,896]{1,0:T(8,128)(2,1)S(1)}, u32[]{:S(2)}, u32[]{:S(2)}) collective-permute-start(f16[128,896]{1,0:T(8,128)(2,1)S(1)} %convert_element_type.24), channel_id=1, source_target_pairs={{0,508},{4,0},{8,4},{12,8},{16,12},{20,16},{24,20},{28,24},{32,28}... | collective-permute-start | bytes 688136 | tf_op jit(solution)/shard_map/ppermute | solution.py:18
  68.5 1.9 %collective-permute-start.9 = (f16[128,896]{1,0:T(8,128)(2,1)S(1)}, f16[128,896]{1,0:T(8,128)(2,1)S(1)}, u32[]{:S(2)}, u32[]{:S(2)}) collective-permute-start(f16[128,896]{1,0:T(8,128)(2,1)S(1)} %convert_element_type.28), channel_id=1, source_target_pairs={{0,496},{4,500},{8,504},{12,508},{16,0},{20,4},{24,8},{28,12},{32,... | collective-permute-start | bytes 688136 | tf_op jit(solution)/shard_map/ppermute | solution.py:18
  70.5 2.4 %pair1.1 = (f32[128,896]{1,0:T(8,128)S(1)}, f32[1,2048]{1,0:T(1,128)S(1)}) custom-call(bf16[192,2048]{1,0:T(8,128)(2,1)S(1)} %copy-done, bf16[192,2048]{1,0:T(8,128)(2,1)S(1)} %collective-permute-done.refs_1_, bf16[192,2048]{1,0:T(8,128)(2,1)S(1)} %collective-permute-done.1.refs_2_, bf16[192,2048]{1,0:T(8,128)(2,1)S(1)} %collective-permute-done.2.refs_3_, ...), custom_call_target="tpu_custom_call" | custom-call | flops 1 | bytes 1 | tf_op jit(solution)/shard_map/pair1/pallas_call | solution.py:164
  72.9 1.9 %collective-permute-start.8 = (f16[128,896]{1,0:T(8,128)(2,1)S(1)}, f16[128,896]{1,0:T(8,128)(2,1)S(1)}, u32[]{:S(2)}, u32[]{:S(2)}) collective-permute-start(f16[128,896]{1,0:T(8,128)(2,1)S(1)} %convert_element_type.26), channel_id=1, source_target_pairs={{0,508},{4,0},{8,4},{12,8},{16,12},{20,16},{24,20},{28,24},{32,28}... | collective-permute-start | bytes 688136 | tf_op jit(solution)/shard_map/ppermute | solution.py:18
  74.8 2.4 %pair0.1 = (f32[128,896]{1,0:T(8,128)S(1)}, f32[1,2048]{1,0:T(1,128)S(1)}) custom-call(bf16[192,2048]{1,0:T(8,128)(2,1)S(1)} %copy-done, bf16[192,2048]{1,0:T(8,128)(2,1)S(1)} %collective-permute-done.refs_1_, bf16[192,2048]{1,0:T(8,128)(2,1)S(1)} %collective-permute-done.1.refs_2_, bf16[192,2048]{1,0:T(8,128)(2,1)S(1)} %collective-permute-done.2.refs_3_, ...), custom_call_target="tpu_custom_call" | custom-call | flops 1 | bytes 1 | tf_op jit(solution)/shard_map/pair0/pallas_call | solution.py:164
  77.2 2.2 %collective-permute-done.7 = f16[128,896]{1,0:T(8,128)(2,1)S(1)} collective-permute-done((f16[128,896]{1,0:T(8,128)(2,1)S(1)}, f16[128,896]{1,0:T(8,128)(2,1)S(1)}, u32[]{:S(2)}, u32[]{:S(2)}) %collective-permute-start.7) | collective-permute-done | bytes 229408 | tf_op jit(solution)/shard_map/ppermute | solution.py:18
  79.4 2.4 %pair2.1 = (f32[128,896]{1,0:T(8,128)S(1)}, f32[1,2048]{1,0:T(1,128)S(1)}) custom-call(bf16[192,2048]{1,0:T(8,128)(2,1)S(1)} %copy-done, bf16[192,2048]{1,0:T(8,128)(2,1)S(1)} %collective-permute-done.refs_1_, bf16[192,2048]{1,0:T(8,128)(2,1)S(1)} %collective-permute-done.1.refs_2_, bf16[192,2048]{1,0:T(8,128)(2,1)S(1)} %collective-permute-done.2.refs_3_, ...), custom_call_target="tpu_custom_call" | custom-call | flops 1 | bytes 1 | tf_op jit(solution)/shard_map/pair2/pallas_call | solution.py:164
  81.9 8.1 %collective-permute-start.10 = (f16[128,896]{1,0:T(8,128)(2,1)S(1)}, f16[128,896]{1,0:T(8,128)(2,1)S(1)}, u32[]{:S(2)}, u32[]{:S(2)}) collective-permute-start(f16[128,896]{1,0:T(8,128)(2,1)S(1)} %convert_element_type.30), channel_id=1, source_target_pairs={{0,504},{4,508},{8,0},{12,4},{16,8},{20,12},{24,16},{28,20},{32,24... | collective-permute-start | bytes 688136 | tf_op jit(solution)/shard_map/ppermute | solution.py:18
  90.0 6.7 %all-gather = f32[4,1,2048]{2,1,0:T(1,128)S(1)} all-gather(f32[1,1,2048]{2,1,0:T(1,128)S(1)} %bitcast.9), channel_id=1, replica_groups=mesh['blk'=128,'feat'=4] {'feat'}, dimensions={0}, use_global_device_ids=true | all-gather | bytes 40960 | tf_op jit(solution)/shard_map/all_gather | solution.py:255
  96.7 0.7 rows_merged.1
  97.4 0.0 collective-permute-done.9
  97.4 0.0 collective-permute-done.8
  97.5 1.5 %collective-permute-done.10 = f16[128,896]{1,0:T(8,128)(2,1)S(1)} collective-permute-done((f16[128,896]{1,0:T(8,128)(2,1)S(1)}, f16[128,896]{1,0:T(8,128)(2,1)S(1)}, u32[]{:S(2)}, u32[]{:S(2)}) %collective-permute-start.10) | collective-permute-done | bytes 229408 | tf_op jit(solution)/shard_map/ppermute | solution.py:18
  99.0 1.1 %merge_last.1 = (f32[128,768]{1,0:T(8,128)}, f32[1,128]{1,0:T(1,128)}) custom-call(f32[128,896]{1,0:T(8,128)S(1)} %get-tuple-element.25.refs_0_, f32[128,896]{1,0:T(8,128)S(1)} %convert_element_type.27.refs_1_, f32[128,896]{1,0:T(8,128)S(1)} %convert_element_type.29.refs_2_, f32[128,896]{1,0:T(8,128)S(1)} %convert_element_type.31.refs_3_), custom_call_target="tpu_custom_call" | custom-call | flops 1 | bytes 1 | tf_op jit(solution)/shard_map/merge_last/pallas_call | solution.py:203
  (12 shorter events, 0.3 us)
Async XLA Ops:
  0.6 19.7 %copy-start = (bf16[192,2048]{1,0:T(8,128)(2,1)S(1)}, bf16[192,2048]{1,0:T(8,128)(2,1)}, u32[]{:S(2)}) copy-start(bf16[192,2048]{1,0:T(8,128)(2,1)} %refs_0_.9) | copy-start | bytes 2359300
  0.6 1.0 copy-start.1
  1.6 0.7 copy-start.2
  2.4 36.3 %copy-start.3 = (f32[2048]{0:T(1024)S(1)}, f32[2048]{0:T(1024)}, u32[]{:S(2)}) copy-start(f32[2048]{0:T(1024)} %param.7) | copy-start | bytes 24580
  13.5 25.1 %collective-permute-start.5 = (bf16[4,208,128]{2,1,0:T(8,128)(2,1)S(1)}, bf16[4,208,128]{2,1,0:T(8,128)(2,1)S(1)}, u32[]{:S(2)}, u32[]{:S(2)}) collective-permute-start(bf16[4,208,128]{2,1,0:T(8,128)(2,1)S(1)} %all_to_all.5.refs_4_), channel_id=1, source_target_pairs={{0,16},{4,20},{8,24},{12,28},{16,32},{20,36},{24,40},{28,44},{32,4... | collective-permute-start | bytes 638984 | tf_op jit(solution)/shard_map/ppermute | solution.py:18
  20.3 26.8 %collective-permute-start.1 = (bf16[192,2048]{1,0:T(8,128)(2,1)S(1)}, bf16[192,2048]{1,0:T(8,128)(2,1)S(1)}, u32[]{:S(2)}, u32[]{:S(2)}) collective-permute-start(bf16[192,2048]{1,0:T(8,128)(2,1)S(1)} %copy-done), channel_id=1, source_target_pairs={{0,2},{1,3},{2,0},{3,1},{4,6},{5,7},{6,4},{7,5},{8,10},{9,11},{10,... | collective-permute-start | bytes 2359304 | tf_op jit(solution)/shard_map/ppermute | solution.py:23
  22.6 17.9 %collective-permute-start.3 = (bf16[4,208,128]{2,1,0:T(8,128)(2,1)S(1)}, bf16[4,208,128]{2,1,0:T(8,128)(2,1)S(1)}, u32[]{:S(2)}, u32[]{:S(2)}) collective-permute-start(bf16[4,208,128]{2,1,0:T(8,128)(2,1)S(1)} %all_to_all.5.refs_4_), channel_id=1, source_target_pairs={{0,4},{4,8},{8,12},{12,16},{16,20},{20,24},{24,28},{28,32},{32,36}... | collective-permute-start | bytes 638984 | tf_op jit(solution)/shard_map/ppermute | solution.py:18
  38.6 10.4 %collective-permute-start.6 = (bf16[4,208,128]{2,1,0:T(8,128)(2,1)S(1)}, bf16[4,208,128]{2,1,0:T(8,128)(2,1)S(1)}, u32[]{:S(2)}, u32[]{:S(2)}) collective-permute-start(bf16[4,208,128]{2,1,0:T(8,128)(2,1)S(1)} %collective-permute-done.5.refs_0_.refs_4_), channel_id=1, source_target_pairs={{0,508},{4,0},{8,4},{12,8},{16,12},{20,16},{24,20},{28,24},{32,28}... | collective-permute-start | bytes 638984 | tf_op jit(solution)/shard_map/ppermute | solution.py:18
  40.6 10.0 %collective-permute-start.4 = (bf16[4,208,128]{2,1,0:T(8,128)(2,1)S(1)}, bf16[4,208,128]{2,1,0:T(8,128)(2,1)S(1)}, u32[]{:S(2)}, u32[]{:S(2)}) collective-permute-start(bf16[4,208,128]{2,1,0:T(8,128)(2,1)S(1)} %collective-permute-done.3.refs_4_), channel_id=1, source_target_pairs={{0,4},{4,8},{8,12},{12,16},{16,20},{20,24},{24,28},{28,32},{32,36}... | collective-permute-start | bytes 638984 | tf_op jit(solution)/shard_map/ppermute | solution.py:18
  44.5 6.0 %collective-permute-start = (bf16[192,2048]{1,0:T(8,128)(2,1)S(1)}, bf16[192,2048]{1,0:T(8,128)(2,1)S(1)}, u32[]{:S(2)}, u32[]{:S(2)}) collective-permute-start(bf16[192,2048]{1,0:T(8,128)(2,1)S(1)} %copy-done), channel_id=1, source_target_pairs={{0,1},{1,0},{2,3},{3,2},{4,5},{5,4},{6,7},{7,6},{8,9},{9,8},{10,11... | collective-permute-start | bytes 2359304 | tf_op jit(solution)/shard_map/ppermute | solution.py:23
  47.1 4.2 %collective-permute-start.2 = (bf16[192,2048]{1,0:T(8,128)(2,1)S(1)}, bf16[192,2048]{1,0:T(8,128)(2,1)S(1)}, u32[]{:S(2)}, u32[]{:S(2)}) collective-permute-start(bf16[192,2048]{1,0:T(8,128)(2,1)S(1)} %collective-permute-done.1.refs_2_), channel_id=1, source_target_pairs={{0,1},{1,0},{2,3},{3,2},{4,5},{5,4},{6,7},{7,6},{8,9},{9,8},{10,11... | collective-permute-start | bytes 2359304 | tf_op jit(solution)/shard_map/ppermute | solution.py:23
  56.1 23.2 %collective-permute-start.7 = (f16[128,896]{1,0:T(8,128)(2,1)S(1)}, f16[128,896]{1,0:T(8,128)(2,1)S(1)}, u32[]{:S(2)}, u32[]{:S(2)}) collective-permute-start(f16[128,896]{1,0:T(8,128)(2,1)S(1)} %convert_element_type.24), channel_id=1, source_target_pairs={{0,508},{4,0},{8,4},{12,8},{16,12},{20,16},{24,20},{28,24},{32,28}... | collective-permute-start | bytes 688136 | tf_op jit(solution)/shard_map/ppermute | solution.py:18
  68.5 28.9 %collective-permute-start.9 = (f16[128,896]{1,0:T(8,128)(2,1)S(1)}, f16[128,896]{1,0:T(8,128)(2,1)S(1)}, u32[]{:S(2)}, u32[]{:S(2)}) collective-permute-start(f16[128,896]{1,0:T(8,128)(2,1)S(1)} %convert_element_type.28), channel_id=1, source_target_pairs={{0,496},{4,500},{8,504},{12,508},{16,0},{20,4},{24,8},{28,12},{32,... | collective-permute-start | bytes 688136 | tf_op jit(solution)/shard_map/ppermute | solution.py:18
  72.9 24.6 %collective-permute-start.8 = (f16[128,896]{1,0:T(8,128)(2,1)S(1)}, f16[128,896]{1,0:T(8,128)(2,1)S(1)}, u32[]{:S(2)}, u32[]{:S(2)}) collective-permute-start(f16[128,896]{1,0:T(8,128)(2,1)S(1)} %convert_element_type.26), channel_id=1, source_target_pairs={{0,508},{4,0},{8,4},{12,8},{16,12},{20,16},{24,20},{28,24},{32,28}... | collective-permute-start | bytes 688136 | tf_op jit(solution)/shard_map/ppermute | solution.py:18
  81.9 17.1 %collective-permute-start.10 = (f16[128,896]{1,0:T(8,128)(2,1)S(1)}, f16[128,896]{1,0:T(8,128)(2,1)S(1)}, u32[]{:S(2)}, u32[]{:S(2)}) collective-permute-start(f16[128,896]{1,0:T(8,128)(2,1)S(1)} %convert_element_type.30), channel_id=1, source_target_pairs={{0,504},{4,508},{8,0},{12,4},{16,8},{20,12},{24,16},{28,20},{32,24... | collective-permute-start | bytes 688136 | tf_op jit(solution)/shard_map/ppermute | solution.py:18

commit v3 on v2

--- a/solution.py
+++ b/solution.py
@@ -7,15 +7,29 @@
 from jax.experimental.pallas import tpu as pltpu
 from jax.sharding import PartitionSpec as P
 
-HOPS = 4
+ROW = 8
 EXTRA = 16
 CHUNK = 512
-STAT = 128
+STAT = 16
 
 
 def shifted(block, distance):
     size = lax.axis_size("blk")
     return lax.ppermute(block, "blk", [(i, (i + distance) % size) for i in range(size)])
+
+
+def half_way(size):
+    return [i // ROW * ROW + (i + 2) % ROW for i in range(size)]
+
+
+def four_back_first(block):
+    size = lax.axis_size("blk")
+    return lax.ppermute(block, "blk", list(enumerate(half_way(size))))
+
+
+def four_back_second(block):
+    size = lax.axis_size("blk")
+    return lax.ppermute(block, "blk", [(at, (i - 4) % size) for i, at in enumerate(half_way(size))])
 
 
 def swapped(block, mask):
@@ -30,15 +44,18 @@
     return high, middle, rest - middle
 
 
-def stat_lanes(lse):
-    high, middle, low = three_terms(lse)
-    lane = lax.broadcasted_iota(jnp.int32, (lse.shape[0], STAT), 1)
-    return jnp.where(lane == 0, high, jnp.where(lane == 1, middle, jnp.where(lane == 2, low, 0.0)))
+def stat_rows(lse):
+    count = lse.shape[0]
+    high, middle, low = three_terms(jnp.broadcast_to(lse, (count, count)).T[:STAT])
+    row = lax.broadcasted_iota(jnp.int32, (STAT, count), 0)
+    rows = jnp.where(row == 0, high, jnp.where(row == 1, middle, jnp.where(row == 2, low, 0.0)))
+    return rows
 
 
 def stat_sum(packed):
-    features = packed.shape[1] - STAT
-    return jnp.sum(packed[:, features : features + 3], axis=1, keepdims=True)
+    count = packed.shape[0] - STAT
+    total = jnp.sum(packed[count : count + 3, :count], axis=0, keepdims=True)
+    return jnp.broadcast_to(total, (count, count)).T[:, :1]
 
 
 def joined(lses):
@@ -48,23 +65,33 @@
     return [weight / total for weight in weights], top + jnp.log(total)
 
 
-def split_kernel(cent, pot, out):
+def split_kernel(cent, pot, out, pots, sems):
     depth, quarter = cent.shape[0], out.shape[2]
-    for at in range(out.shape[0]):
-        cut = slice(at * quarter, (at + 1) * quarter)
-        out[at, :depth, :] = cent[:, cut]
-        high, middle, low = three_terms(pot[:, cut])
+    parts = out.shape[0]
+    copies = [pltpu.make_async_copy(pot, pots, sems.at[parts])]
+    for at in range(parts):
+        columns = cent.at[:, pl.ds(at * quarter, quarter)]
+        copies.append(pltpu.make_async_copy(columns, out.at[at, pl.ds(0, depth), :], sems.at[at]))
+    for copy in copies:
+        copy.start()
+    copies[0].wait()
+    for at in range(parts):
+        high, middle, low = three_terms(pots[:, at * quarter : (at + 1) * quarter])
         row = lax.broadcasted_iota(jnp.int32, (EXTRA, quarter), 0)
         rows = jnp.where(row == 0, high, jnp.where(row == 1, middle, jnp.where(row == 2, low, 0.0)))
         out[at, depth:, :] = rows.astype(jnp.bfloat16)
+    for copy in copies[1:]:
+        copy.wait()
 
 
 def split_panel(centroids, col_pot):
     depth, width = centroids.shape
     return pl.pallas_call(
         split_kernel,
+        in_specs=[pl.BlockSpec(memory_space=pl.ANY)] * 2,
         out_shape=jax.ShapeDtypeStruct((4, depth + EXTRA, width // 4), centroids.dtype),
-        compiler_params=pltpu.CompilerParams(vmem_limit_bytes=4 * 2**20),
+        scratch_shapes=[pltpu.VMEM((1, width), jnp.float32), pltpu.SemaphoreType.DMA((5,))],
+        compiler_params=pltpu.CompilerParams(vmem_limit_bytes=32 * 2**20),
         name="split_panel",
     )(centroids, col_pot[None, :])
 
@@ -84,19 +111,19 @@
     )(value, *arrays)
 
 
-def pair_kernel(scale, first, *refs):
-    pts = refs[:4]
-    panel, row_pot = refs[4:6]
-    packed, row_out, scores = refs[-3:]
-    row_in = None if first else refs[6]
-    arrived = refs[6 if first else 7 : -3]
+def pair_kernel(scale, panels, first, *refs):
+    pts, panel_refs, row_pot = refs[:4], refs[4 : 4 + panels], refs[4 + panels]
+    outs, row_out, scores = refs[-2 - panels : -2], refs[-2], refs[-1]
+    rest = refs[5 + panels : -2 - panels]
+    row_in, arrived = (None, rest) if first else (rest[0], rest[1:])
     depth, count = pts[0].shape
     features = 4 * depth
+    quarter = outs[0].shape[0] - STAT
     member = lax.axis_index("feat")
     cols = []
     squares = None
     for m in range(4):
-        turned = panel[member ^ m].T
+        turned = jnp.concatenate([panel[member ^ m].T for panel in panel_refs], axis=0)
         cols.append(turned[:, :depth])
         wide = turned[:, :depth].astype(jnp.float32)
         part = jnp.sum(wide * wide, axis=1, keepdims=True)
@@ -143,32 +170,35 @@
             acc[m] = part if acc[m] is None else acc[m] + part
     col_sum = jnp.sum(lane_sum, axis=1, keepdims=True)
     lse = col_max + jnp.log(col_sum)
-    scales, lse = joined([lse] + [stat_sum(ref) for ref in arrived])
-    scales[0] = scales[0] / col_sum
-    for m in range(4):
-        cut = slice(depth * m, depth * (m + 1))
-        mean = acc[m] * scales[0]
-        for scaling, ref in zip(scales[1:], arrived):
-            mean = mean + ref[:, cut] * scaling
-        packed[:, cut] = mean
-    packed[:, features:] = stat_lanes(lse)
-
-
-def pair(points, panel, row_pot, row_in, name, arrived=()):
+    shares, lse = joined([lse] + [stat_sum(ref) for ref in arrived])
+    shares[0] = shares[0] / col_sum
+    for i, packed in enumerate(outs):
+        mine = slice(i * quarter, (i + 1) * quarter)
+        for m in range(4):
+            cut = slice(depth * m, depth * (m + 1))
+            mean = acc[m][mine] * shares[0][mine]
+            for share, ref in zip(shares[1:], arrived):
+                mean = mean + ref[:quarter, cut] * share
+            packed[:quarter, cut] = mean
+        packed[quarter:, :] = jnp.zeros((STAT, features), jnp.float32)
+        packed[quarter:, :quarter] = stat_rows(lse[mine])
+
+
+def pair(points, panels, row_pot, row_in, name, arrived=()):
     depth, count = points[0].shape
     features = 4 * depth
-    quarter = panel.shape[2]
-    operands = (*points, panel, row_pot)
+    quarter = panels[0].shape[2]
+    operands = (*points, *panels, row_pot)
     operands += () if row_in is None else (row_in,)
     operands += tuple(arrived)
     return pl.pallas_call(
-        functools.partial(pair_kernel, 1.0 / (0.02 * features), row_in is None),
+        functools.partial(pair_kernel, 1.0 / (0.02 * features), len(panels), row_in is None),
         out_shape=(
-            jax.ShapeDtypeStruct((quarter, features + STAT), jnp.float32),
+            *[jax.ShapeDtypeStruct((quarter + STAT, features), jnp.float32)] * len(panels),
             jax.ShapeDtypeStruct((1, count), jnp.float32),
         ),
-        scratch_shapes=[pltpu.VMEM((quarter, count), jnp.float32)],
-        compiler_params=pltpu.CompilerParams(vmem_limit_bytes=12 * 2**20),
+        scratch_shapes=[pltpu.VMEM((quarter * len(panels), count), jnp.float32)],
+        compiler_params=pltpu.CompilerParams(vmem_limit_bytes=16 * 2**20),
         cost_estimate=pl.CostEstimate(flops=1, bytes_accessed=1, transcendentals=0),
         name=name,
     )(*operands)
@@ -186,7 +216,8 @@
     parts, mean_out, lse_out = refs[:-2], refs[-2], refs[-1]
     features = mean_out.shape[1]
     scales, lse = joined([stat_sum(part) for part in parts])
-    mean = functools.reduce(jnp.add, [part[:, :features] * scaling for part, scaling in zip(parts, scales)])
+    count = mean_out.shape[0]
+    mean = functools.reduce(jnp.add, [part[:count] * scaling for part, scaling in zip(parts, scales)])
     lse_out[...] = jnp.broadcast_to(lse, (lse.shape[0], lse.shape[0])).T[:1, :]
     member = lax.axis_index("feat")
     depth = features // 4
@@ -199,11 +230,12 @@
 
 
 def merge(parts):
-    quarter, width = parts[0].shape
+    rows, width = parts[0].shape
+    quarter = rows - STAT
     return pl.pallas_call(
         merge_kernel,
         out_shape=(
-            jax.ShapeDtypeStruct((quarter, width - STAT), jnp.float32),
+            jax.ShapeDtypeStruct((quarter, width), jnp.float32),
             jax.ShapeDtypeStruct((1, quarter), jnp.float32),
         ),
         compiler_params=pltpu.CompilerParams(vmem_limit_bytes=8 * 2**20),
@@ -233,24 +265,22 @@
 
 def local(points, centroids, col_pot, row_pot):
     panel0 = lax.all_to_all(split_panel(centroids, col_pot), "feat", split_axis=0, concat_axis=0, tiled=True)
+    across = swapped(after(points, panel0), 2)
     panel4 = shifted(panel0, 4)
-    across = swapped(after(points, panel0), 2)
     panel1 = shifted(panel0, 1)
     beside = swapped(after(points, panel0), 1)
     panel2 = shifted(panel1, 1)
-    pot = hand_on(row_pot[None, :], (panel4,), "far_panel")
-    panel3 = shifted(after(panel4, pot), -1)
+    panel3 = shifted(panel4, -1)
     diagonal = swapped(across, 1)
-    pot = hand_on(pot, (panel3, panel2), "all_panels")
+    pot = hand_on(row_pot[None, :], (panel3, panel2), "all_panels")
     full = (points, beside, across, diagonal)
-    part4, rows = pair(full, panel4, pot, None, "pair4")
-    back4 = whole(shifted(half(part4), -4))
-    part3, rows = pair(full, panel3, pot, rows, "pair3")
+    part3, part4, rows = pair(full, (panel3, panel4), pot, None, "pair34")
+    under_way = four_back_first(half(part4))
     next3 = whole(shifted(half(part3), -1))
-    part1, rows = pair(full, panel1, pot, rows, "pair1")
+    part1, part0, rows = pair(full, (panel1, panel0), pot, rows, "pair10")
     back1 = whole(shifted(half(part1), -1))
-    part0, rows = pair(full, panel0, pot, rows, "pair0")
-    part2, rows = pair(full, panel2, pot, rows, "pair2", (next3,))
+    back4 = whole(four_back_second(under_way))
+    part2, rows = pair(full, (panel2,), pot, rows, "pair2", (next3,))
     back2 = whole(shifted(half(part2), -2))
     row_lse = rows_merged(lax.all_gather(rows, "feat", axis=0, tiled=True))
     mean, col_lse = merge((part0, back1, back4, back2))

time: 101 us -> 98.2 us (0.972)
  the two profiles are of different devices: /device:TPU:8 before, /device:TPU:20 now
where the time goes in v3:
time: 98.2 us; the launch traced here: 97.7 us
  starting transfers between devices  44.8 us (46%)
  waiting for transfers between devices  24.3 us (25%)
  blocking collectives  15.1 us (15%)
  Pallas kernels  10.6 us (11%)
  local copies, waits for them, and re-layouts  1.7 us (2%)
    ppermute x7, starting transfers between devices, shifted(): lax.ppermute(block, 'blk', [(i, (i + distance) % size) for i in range(siz...  26 us
    ppermute x7, waiting for transfers between devices, shifted(): lax.ppermute(block, 'blk', [(i, (i + distance) % size) for i in range(siz...  22.7 us
    ppermute x3, starting transfers between devices, swapped(): return lax.ppermute(block, 'feat', [(i, i ^ mask) for i in range(size)])  9.39 us
    pallas_call x3, Pallas kernels, pair(): pl.pallas_call(functools.partial(pair_kernel, 1.0 / (0.02 * features), le...  8.69 us
    all_to_all x1, blocking collectives, local(): lax.all_to_all(split_panel(centroids, col_pot), 'feat', split_axis=0, con...  8.45 us
    ppermute x1, starting transfers between devices, four_back_second(): lax.ppermute(block, 'blk', [(at, (i - 4) % size) for i, at in enumerate(h...  7.21 us
    all_gather x1, blocking collectives, local(): row_lse = rows_merged(lax.all_gather(rows, 'feat', axis=0, tiled=True))  6.7 us
    ppermute x1, starting transfers between devices, four_back_first(): return lax.ppermute(block, 'blk', list(enumerate(half_way(size))))  2.17 us
  transfers between devices with their start and end apart: 12, of which 4 were waited for; matrix products, arithmetic and copies ran while one was open for 0% of the time, Pallas kernels for 6%

profile of v3, /device:TPU:20, one launch (start us, length us, event | category | flops | bytes accessed | tf_op | source)
XLA Modules:
  0.0 97.7 jit_solution(10872412842947567097)
XLA Ops:
  0.6 0.0 copy-start
  0.6 0.0 copy-start.1
  0.7 1.0 %copy-done.1 = bf16[192,512]{1,0:T(8,128)(2,1)S(1)} copy-done((bf16[192,512]{1,0:T(8,128)(2,1)S(1)}, bf16[192,512]{1,0:T(8,128)(2,1)}, u32[]{:S(2)}) %copy-start.1) | copy-done | bytes 196632
  1.6 0.0 copy-start.2
  1.6 0.7 copy-done.2
  2.3 0.1 split_panel.1
  2.4 0.0 copy-start.3
  2.4 8.4 %all_to_all.5.refs_5_ = bf16[4,208,128]{2,1,0:T(8,128)(2,1)S(1)} all-to-all(bf16[4,208,128]{2,1,0:T(8,128)(2,1)S(1)} %split_panel.1), channel_id=1, replica_groups=mesh['blk'=128,'feat'=4] {'feat'}, dimensions={0} | all-to-all | bytes 425984 | tf_op jit(solution)/shard_map/all_to_all | solution.py:267
  10.9 0.0 copy-done
  10.9 5.1 %collective-permute-start.1 = (bf16[192,2048]{1,0:T(8,128)(2,1)S(1)}, bf16[192,2048]{1,0:T(8,128)(2,1)S(1)}, u32[]{:S(2)}, u32[]{:S(2)}) collective-permute-start(bf16[192,2048]{1,0:T(8,128)(2,1)S(1)} %copy-done), channel_id=1, source_target_pairs={{0,2},{1,3},{2,0},{3,1},{4,6},{5,7},{6,4},{7,5},{8,10},{9,11},{10,... | collective-permute-start | bytes 2359304 | tf_op jit(solution)/shard_map/ppermute | solution.py:37
  16.0 5.9 %collective-permute-start.5 = (bf16[4,208,128]{2,1,0:T(8,128)(2,1)S(1)}, bf16[4,208,128]{2,1,0:T(8,128)(2,1)S(1)}, u32[]{:S(2)}, u32[]{:S(2)}) collective-permute-start(bf16[4,208,128]{2,1,0:T(8,128)(2,1)S(1)} %all_to_all.5.refs_5_), channel_id=1, source_target_pairs={{0,16},{4,20},{8,24},{12,28},{16,32},{20,36},{24,40},{28,44},{32,4... | collective-permute-start | bytes 638984 | tf_op jit(solution)/shard_map/ppermute | solution.py:18
  21.9 2.6 %collective-permute-start.3 = (bf16[4,208,128]{2,1,0:T(8,128)(2,1)S(1)}, bf16[4,208,128]{2,1,0:T(8,128)(2,1)S(1)}, u32[]{:S(2)}, u32[]{:S(2)}) collective-permute-start(bf16[4,208,128]{2,1,0:T(8,128)(2,1)S(1)} %all_to_all.5.refs_5_), channel_id=1, source_target_pairs={{0,4},{4,8},{8,12},{12,16},{16,20},{20,24},{24,28},{28,32},{32,36}... | collective-permute-start | bytes 638984 | tf_op jit(solution)/shard_map/ppermute | solution.py:18
  24.5 17.3 %collective-permute-done.5.refs_5_ = bf16[4,208,128]{2,1,0:T(8,128)(2,1)S(1)} collective-permute-done((bf16[4,208,128]{2,1,0:T(8,128)(2,1)S(1)}, bf16[4,208,128]{2,1,0:T(8,128)(2,1)S(1)}, u32[]{:S(2)}, u32[]{:S(2)}) %collective-permute-start.5) | collective-permute-done | bytes 213024 | tf_op jit(solution)/shard_map/ppermute | solution.py:18
  41.8 2.0 %collective-permute-start.6 = (bf16[4,208,128]{2,1,0:T(8,128)(2,1)S(1)}, bf16[4,208,128]{2,1,0:T(8,128)(2,1)S(1)}, u32[]{:S(2)}, u32[]{:S(2)}) collective-permute-start(bf16[4,208,128]{2,1,0:T(8,128)(2,1)S(1)} %collective-permute-done.5.refs_5_), channel_id=1, source_target_pairs={{0,508},{4,0},{8,4},{12,8},{16,12},{20,16},{24,20},{28,24},{32,28}... | collective-permute-start | bytes 638984 | tf_op jit(solution)/shard_map/ppermute | solution.py:18
  43.8 0.0 collective-permute-done.3.refs_4_
  43.8 3.8 %collective-permute-start.4 = (bf16[4,208,128]{2,1,0:T(8,128)(2,1)S(1)}, bf16[4,208,128]{2,1,0:T(8,128)(2,1)S(1)}, u32[]{:S(2)}, u32[]{:S(2)}) collective-permute-start(bf16[4,208,128]{2,1,0:T(8,128)(2,1)S(1)} %collective-permute-done.3.refs_4_), channel_id=1, source_target_pairs={{0,4},{4,8},{8,12},{12,16},{16,20},{20,24},{24,28},{28,32},{32,36}... | collective-permute-start | bytes 638984 | tf_op jit(solution)/shard_map/ppermute | solution.py:18
  47.6 1.9 %collective-permute-start = (bf16[192,2048]{1,0:T(8,128)(2,1)S(1)}, bf16[192,2048]{1,0:T(8,128)(2,1)S(1)}, u32[]{:S(2)}, u32[]{:S(2)}) collective-permute-start(bf16[192,2048]{1,0:T(8,128)(2,1)S(1)} %copy-done), channel_id=1, source_target_pairs={{0,1},{1,0},{2,3},{3,2},{4,5},{5,4},{6,7},{7,6},{8,9},{9,8},{10,11... | collective-permute-start | bytes 2359304 | tf_op jit(solution)/shard_map/ppermute | solution.py:37
  49.5 0.0 collective-permute-done.1.refs_2_
  49.6 2.4 %collective-permute-start.2 = (bf16[192,2048]{1,0:T(8,128)(2,1)S(1)}, bf16[192,2048]{1,0:T(8,128)(2,1)S(1)}, u32[]{:S(2)}, u32[]{:S(2)}) collective-permute-start(bf16[192,2048]{1,0:T(8,128)(2,1)S(1)} %collective-permute-done.1.refs_2_), channel_id=1, source_target_pairs={{0,1},{1,0},{2,3},{3,2},{4,5},{5,4},{6,7},{7,6},{8,9},{9,8},{10,11... | collective-permute-start | bytes 2359304 | tf_op jit(solution)/shard_map/ppermute | solution.py:37
  52.0 0.0 collective-permute-done.6.refs_0_.refs_4_
  52.0 0.2 collective-permute-done.4.refs_1_.refs_4_
  52.2 0.0 copy-done.3
  52.2 0.0 collective-permute-done.refs_1_
  52.2 1.6 %collective-permute-done.2.refs_3_ = bf16[192,2048]{1,0:T(8,128)(2,1)S(1)} collective-permute-done((bf16[192,2048]{1,0:T(8,128)(2,1)S(1)}, bf16[192,2048]{1,0:T(8,128)(2,1)S(1)}, u32[]{:S(2)}, u32[]{:S(2)}) %collective-permute-start.2) | collective-permute-done | bytes 786464 | tf_op jit(solution)/shard_map/ppermute | solution.py:37
  53.9 3.2 %pair34.1 = (f32[144,768]{1,0:T(8,128)S(1)}, f32[144,768]{1,0:T(8,128)S(1)}, f32[1,2048]{1,0:T(1,128)S(1)}) custom-call(bf16[192,2048]{1,0:T(8,128)(2,1)S(1)} %copy-done, bf16[192,2048]{1,0:T(8,128)(2,1)S(1)} %collective-permute-done.refs_1_, bf16[192,2048]{1,0:T(8,128)(2,1)S(1)} %collective-permute-done.1.refs_2_, ...), custom_call_target="tpu_custom_call" | custom-call | flops 1 | bytes 1 | tf_op jit(solution)/shard_map/pair34/pallas_call | solution.py:194
  57.1 2.2 %collective-permute-start.9 = (f16[144,768]{1,0:T(8,128)(2,1)S(1)}, f16[144,768]{1,0:T(8,128)(2,1)S(1)}, u32[]{:S(2)}, u32[]{:S(2)}) collective-permute-start(f16[144,768]{1,0:T(8,128)(2,1)S(1)} %convert_element_type.28), channel_id=1, source_target_pairs={{0,8},{4,12},{8,16},{12,20},{16,24},{20,28},{24,0},{28,4},{32,40},... | collective-permute-start | bytes 663560 | tf_op jit(solution)/shard_map/ppermute | solution.py:27
  59.3 3.1 %collective-permute-start.7 = (f16[144,768]{1,0:T(8,128)(2,1)S(1)}, f16[144,768]{1,0:T(8,128)(2,1)S(1)}, u32[]{:S(2)}, u32[]{:S(2)}) collective-permute-start(f16[144,768]{1,0:T(8,128)(2,1)S(1)} %convert_element_type.24), channel_id=1, source_target_pairs={{0,508},{4,0},{8,4},{12,8},{16,12},{20,16},{24,20},{28,24},{32,28}... | collective-permute-start | bytes 663560 | tf_op jit(solution)/shard_map/ppermute | solution.py:18
  62.4 3.2 %pair10.1 = (f32[144,768]{1,0:T(8,128)S(1)}, f32[144,768]{1,0:T(8,128)S(1)}, f32[1,2048]{1,0:T(1,128)S(1)}) custom-call(bf16[192,2048]{1,0:T(8,128)(2,1)S(1)} %copy-done, bf16[192,2048]{1,0:T(8,128)(2,1)S(1)} %collective-permute-done.refs_1_, bf16[192,2048]{1,0:T(8,128)(2,1)S(1)} %collective-permute-done.1.refs_2_, ...), custom_call_target="tpu_custom_call" | custom-call | flops 1 | bytes 1 | tf_op jit(solution)/shard_map/pair10/pallas_call | solution.py:194
  65.6 6.6 %collective-permute-start.8 = (f16[144,768]{1,0:T(8,128)(2,1)S(1)}, f16[144,768]{1,0:T(8,128)(2,1)S(1)}, u32[]{:S(2)}, u32[]{:S(2)}) collective-permute-start(f16[144,768]{1,0:T(8,128)(2,1)S(1)} %convert_element_type.26), channel_id=1, source_target_pairs={{0,508},{4,0},{8,4},{12,8},{16,12},{20,16},{24,20},{28,24},{32,28}... | collective-permute-start | bytes 663560 | tf_op jit(solution)/shard_map/ppermute | solution.py:18
  72.3 0.0 collective-permute-done.9
  72.3 7.2 %collective-permute-start.10 = (f16[144,768]{1,0:T(8,128)(2,1)S(1)}, f16[144,768]{1,0:T(8,128)(2,1)S(1)}, u32[]{:S(2)}, u32[]{:S(2)}) collective-permute-start(f16[144,768]{1,0:T(8,128)(2,1)S(1)} %collective-permute-done.9), channel_id=1, source_target_pairs={{8,496},{12,500},{16,504},{20,508},{24,0},{28,4},{0,8},{4,12},{40,... | collective-permute-start | bytes 663560 | tf_op jit(solution)/shard_map/ppermute | solution.py:32
  79.5 0.0 collective-permute-done.7
  79.5 2.3 %pair2.1 = (f32[144,768]{1,0:T(8,128)S(1)}, f32[1,2048]{1,0:T(1,128)S(1)}) custom-call(bf16[192,2048]{1,0:T(8,128)(2,1)S(1)} %copy-done, bf16[192,2048]{1,0:T(8,128)(2,1)S(1)} %collective-permute-done.refs_1_, bf16[192,2048]{1,0:T(8,128)(2,1)S(1)} %collective-permute-done.1.refs_2_, bf16[192,2048]{1,0:T(8,128)(2,1)S(1)} %collective-permute-done.2.refs_3_, ...), custom_call_target="tpu_custom_call" | custom-call | flops 1 | bytes 1 | tf_op jit(solution)/shard_map/pair2/pallas_call | solution.py:194
  81.9 1.9 %collective-permute-start.11 = (f16[144,768]{1,0:T(8,128)(2,1)S(1)}, f16[144,768]{1,0:T(8,128)(2,1)S(1)}, u32[]{:S(2)}, u32[]{:S(2)}) collective-permute-start(f16[144,768]{1,0:T(8,128)(2,1)S(1)} %convert_element_type.30), channel_id=1, source_target_pairs={{0,504},{4,508},{8,0},{12,4},{16,8},{20,12},{24,16},{28,20},{32,24... | collective-permute-start | bytes 663560 | tf_op jit(solution)/shard_map/ppermute | solution.py:18
  83.8 6.7 %all-gather = f32[4,1,2048]{2,1,0:T(1,128)S(1)} all-gather(f32[1,1,2048]{2,1,0:T(1,128)S(1)} %bitcast.9), channel_id=1, replica_groups=mesh['blk'=128,'feat'=4] {'feat'}, dimensions={0}, use_global_device_ids=true | all-gather | bytes 40960 | tf_op jit(solution)/shard_map/all_gather | solution.py:285
  90.5 0.7 rows_merged.1
  91.2 0.0 collective-permute-done.8
  91.2 0.0 collective-permute-done.10
  91.3 5.2 %collective-permute-done.11 = f16[144,768]{1,0:T(8,128)(2,1)S(1)} collective-permute-done((f16[144,768]{1,0:T(8,128)(2,1)S(1)}, f16[144,768]{1,0:T(8,128)(2,1)S(1)}, u32[]{:S(2)}, u32[]{:S(2)}) %collective-permute-start.11) | collective-permute-done | bytes 221216 | tf_op jit(solution)/shard_map/ppermute | solution.py:18
  96.5 1.2 %merge_last.1 = (f32[128,768]{1,0:T(8,128)}, f32[1,128]{1,0:T(1,128)}) custom-call(f32[144,768]{1,0:T(8,128)S(1)} %get-tuple-element.19.refs_0_, f32[144,768]{1,0:T(8,128)S(1)} %convert_element_type.27.refs_1_, f32[144,768]{1,0:T(8,128)S(1)} %convert_element_type.29.refs_2_, f32[144,768]{1,0:T(8,128)S(1)} %convert_element_type.31.refs_3_), custom_call_target="tpu_custom_call" | custom-call | flops 1 | bytes 1 | tf_op jit(solution)/shard_map/merge_last/pallas_call | solution.py:235
  (10 shorter events, 0.2 us)
Async XLA Ops:
  0.6 10.3 %copy-start = (bf16[192,2048]{1,0:T(8,128)(2,1)S(1)}, bf16[192,2048]{1,0:T(8,128)(2,1)}, u32[]{:S(2)}) copy-start(bf16[192,2048]{1,0:T(8,128)(2,1)} %refs_0_.5) | copy-start | bytes 2359300
  0.6 1.0 %copy-start.1 = (bf16[192,512]{1,0:T(8,128)(2,1)S(1)}, bf16[192,512]{1,0:T(8,128)(2,1)}, u32[]{:S(2)}) copy-start(bf16[192,512]{1,0:T(8,128)(2,1)} %cent.1) | copy-start | bytes 589828
  1.6 0.7 copy-start.2
  2.4 49.8 %copy-start.3 = (f32[2048]{0:T(1024)S(1)}, f32[2048]{0:T(1024)}, u32[]{:S(2)}) copy-start(f32[2048]{0:T(1024)} %param.7) | copy-start | bytes 24580
  10.9 38.7 %collective-permute-start.1 = (bf16[192,2048]{1,0:T(8,128)(2,1)S(1)}, bf16[192,2048]{1,0:T(8,128)(2,1)S(1)}, u32[]{:S(2)}, u32[]{:S(2)}) collective-permute-start(bf16[192,2048]{1,0:T(8,128)(2,1)S(1)} %copy-done), channel_id=1, source_target_pairs={{0,2},{1,3},{2,0},{3,1},{4,6},{5,7},{6,4},{7,5},{8,10},{9,11},{10,... | collective-permute-start | bytes 2359304 | tf_op jit(solution)/shard_map/ppermute | solution.py:37
  16.0 25.8 %collective-permute-start.5 = (bf16[4,208,128]{2,1,0:T(8,128)(2,1)S(1)}, bf16[4,208,128]{2,1,0:T(8,128)(2,1)S(1)}, u32[]{:S(2)}, u32[]{:S(2)}) collective-permute-start(bf16[4,208,128]{2,1,0:T(8,128)(2,1)S(1)} %all_to_all.5.refs_5_), channel_id=1, source_target_pairs={{0,16},{4,20},{8,24},{12,28},{16,32},{20,36},{24,40},{28,44},{32,4... | collective-permute-start | bytes 638984 | tf_op jit(solution)/shard_map/ppermute | solution.py:18
  21.9 21.9 %collective-permute-start.3 = (bf16[4,208,128]{2,1,0:T(8,128)(2,1)S(1)}, bf16[4,208,128]{2,1,0:T(8,128)(2,1)S(1)}, u32[]{:S(2)}, u32[]{:S(2)}) collective-permute-start(bf16[4,208,128]{2,1,0:T(8,128)(2,1)S(1)} %all_to_all.5.refs_5_), channel_id=1, source_target_pairs={{0,4},{4,8},{8,12},{12,16},{16,20},{20,24},{24,28},{28,32},{32,36}... | collective-permute-start | bytes 638984 | tf_op jit(solution)/shard_map/ppermute | solution.py:18
  41.8 10.2 %collective-permute-start.6 = (bf16[4,208,128]{2,1,0:T(8,128)(2,1)S(1)}, bf16[4,208,128]{2,1,0:T(8,128)(2,1)S(1)}, u32[]{:S(2)}, u32[]{:S(2)}) collective-permute-start(bf16[4,208,128]{2,1,0:T(8,128)(2,1)S(1)} %collective-permute-done.5.refs_5_), channel_id=1, source_target_pairs={{0,508},{4,0},{8,4},{12,8},{16,12},{20,16},{24,20},{28,24},{32,28}... | collective-permute-start | bytes 638984 | tf_op jit(solution)/shard_map/ppermute | solution.py:18
  43.8 8.4 %collective-permute-start.4 = (bf16[4,208,128]{2,1,0:T(8,128)(2,1)S(1)}, bf16[4,208,128]{2,1,0:T(8,128)(2,1)S(1)}, u32[]{:S(2)}, u32[]{:S(2)}) collective-permute-start(bf16[4,208,128]{2,1,0:T(8,128)(2,1)S(1)} %collective-permute-done.3.refs_4_), channel_id=1, source_target_pairs={{0,4},{4,8},{8,12},{12,16},{16,20},{20,24},{24,28},{28,32},{32,36}... | collective-permute-start | bytes 638984 | tf_op jit(solution)/shard_map/ppermute | solution.py:18
  47.6 4.6 %collective-permute-start = (bf16[192,2048]{1,0:T(8,128)(2,1)S(1)}, bf16[192,2048]{1,0:T(8,128)(2,1)S(1)}, u32[]{:S(2)}, u32[]{:S(2)}) collective-permute-start(bf16[192,2048]{1,0:T(8,128)(2,1)S(1)} %copy-done), channel_id=1, source_target_pairs={{0,1},{1,0},{2,3},{3,2},{4,5},{5,4},{6,7},{7,6},{8,9},{9,8},{10,11... | collective-permute-start | bytes 2359304 | tf_op jit(solution)/shard_map/ppermute | solution.py:37
  49.6 4.3 %collective-permute-start.2 = (bf16[192,2048]{1,0:T(8,128)(2,1)S(1)}, bf16[192,2048]{1,0:T(8,128)(2,1)S(1)}, u32[]{:S(2)}, u32[]{:S(2)}) collective-permute-start(bf16[192,2048]{1,0:T(8,128)(2,1)S(1)} %collective-permute-done.1.refs_2_), channel_id=1, source_target_pairs={{0,1},{1,0},{2,3},{3,2},{4,5},{5,4},{6,7},{7,6},{8,9},{9,8},{10,11... | collective-permute-start | bytes 2359304 | tf_op jit(solution)/shard_map/ppermute | solution.py:37
  57.1 15.2 %collective-permute-start.9 = (f16[144,768]{1,0:T(8,128)(2,1)S(1)}, f16[144,768]{1,0:T(8,128)(2,1)S(1)}, u32[]{:S(2)}, u32[]{:S(2)}) collective-permute-start(f16[144,768]{1,0:T(8,128)(2,1)S(1)} %convert_element_type.28), channel_id=1, source_target_pairs={{0,8},{4,12},{8,16},{12,20},{16,24},{20,28},{24,0},{28,4},{32,40},... | collective-permute-start | bytes 663560 | tf_op jit(solution)/shard_map/ppermute | solution.py:27
  59.3 20.2 %collective-permute-start.7 = (f16[144,768]{1,0:T(8,128)(2,1)S(1)}, f16[144,768]{1,0:T(8,128)(2,1)S(1)}, u32[]{:S(2)}, u32[]{:S(2)}) collective-permute-start(f16[144,768]{1,0:T(8,128)(2,1)S(1)} %convert_element_type.24), channel_id=1, source_target_pairs={{0,508},{4,0},{8,4},{12,8},{16,12},{20,16},{24,20},{28,24},{32,28}... | collective-permute-start | bytes 663560 | tf_op jit(solution)/shard_map/ppermute | solution.py:18
  65.6 25.6 %collective-permute-start.8 = (f16[144,768]{1,0:T(8,128)(2,1)S(1)}, f16[144,768]{1,0:T(8,128)(2,1)S(1)}, u32[]{:S(2)}, u32[]{:S(2)}) collective-permute-start(f16[144,768]{1,0:T(8,128)(2,1)S(1)} %convert_element_type.26), channel_id=1, source_target_pairs={{0,508},{4,0},{8,4},{12,8},{16,12},{20,16},{24,20},{28,24},{32,28}... | collective-permute-start | bytes 663560 | tf_op jit(solution)/shard_map/ppermute | solution.py:18
  72.3 19.0 %collective-permute-start.10 = (f16[144,768]{1,0:T(8,128)(2,1)S(1)}, f16[144,768]{1,0:T(8,128)(2,1)S(1)}, u32[]{:S(2)}, u32[]{:S(2)}) collective-permute-start(f16[144,768]{1,0:T(8,128)(2,1)S(1)} %collective-permute-done.9), channel_id=1, source_target_pairs={{8,496},{12,500},{16,504},{20,508},{24,0},{28,4},{0,8},{4,12},{40,... | collective-permute-start | bytes 663560 | tf_op jit(solution)/shard_map/ppermute | solution.py:32
  81.9 14.6 %collective-permute-start.11 = (f16[144,768]{1,0:T(8,128)(2,1)S(1)}, f16[144,768]{1,0:T(8,128)(2,1)S(1)}, u32[]{:S(2)}, u32[]{:S(2)}) collective-permute-start(f16[144,768]{1,0:T(8,128)(2,1)S(1)} %convert_element_type.30), channel_id=1, source_target_pairs={{0,504},{4,508},{8,0},{12,4},{16,8},{20,12},{24,16},{28,20},{32,24... | collective-permute-start | bytes 663560 | tf_op jit(solution)/shard_map/ppermute | solution.py:18

commit v4 on v3

--- a/solution.py
+++ b/solution.py
@@ -244,6 +244,24 @@
     )(*parts)
 
 
+def blend_kernel(first, second, out):
+    count = out.shape[0] - STAT
+    shares, lse = joined([stat_sum(first), stat_sum(second)])
+    out[:count] = first[:count] * shares[0] + second[:count] * shares[1]
+    out[count:, :] = jnp.zeros((STAT, out.shape[1]), jnp.float32)
+    out[count:, :count] = stat_rows(lse)
+
+
+def blend(first, second):
+    return pl.pallas_call(
+        blend_kernel,
+        out_shape=jax.ShapeDtypeStruct(first.shape, jnp.float32),
+        compiler_params=pltpu.CompilerParams(vmem_limit_bytes=4 * 2**20),
+        cost_estimate=pl.CostEstimate(flops=1, bytes_accessed=1, transcendentals=0),
+        name="blend",
+    )(first, second)
+
+
 def rows_kernel(parts, out):
     top = jnp.max(parts[...], axis=0, keepdims=True)
     out[...] = top + jnp.log(jnp.sum(jnp.exp(parts[...] - top), axis=0, keepdims=True))
@@ -277,11 +295,10 @@
     part3, part4, rows = pair(full, (panel3, panel4), pot, None, "pair34")
     under_way = four_back_first(half(part4))
     next3 = whole(shifted(half(part3), -1))
-    part1, part0, rows = pair(full, (panel1, panel0), pot, rows, "pair10")
+    part1, part0, part2, rows = pair(full, (panel1, panel0, panel2), pot, rows, "pair102")
     back1 = whole(shifted(half(part1), -1))
     back4 = whole(four_back_second(under_way))
-    part2, rows = pair(full, (panel2,), pot, rows, "pair2", (next3,))
-    back2 = whole(shifted(half(part2), -2))
+    back2 = whole(shifted(half(blend(part2, next3)), -2))
     row_lse = rows_merged(lax.all_gather(rows, "feat", axis=0, tiled=True))
     mean, col_lse = merge((part0, back1, back4, back2))
     return (row_lse, col_lse[0], mean)

time: 98.2 us -> 98.1 us (level)
  the two profiles are of different devices: /device:TPU:20 before, /device:TPU:76 now
where the time goes in v4:
time: 98.1 us; the launch traced here: 97.5 us
  starting transfers between devices  54.3 us (55%)
  waiting for transfers between devices  15.4 us (16%)
  blocking collectives  15.1 us (15%)
  Pallas kernels  9.95 us (10%)
  local copies, waits for them, and re-layouts  1.7 us (2%)
    ppermute x7, starting transfers between devices, shifted(): lax.ppermute(block, 'blk', [(i, (i + distance) % size) for i in range(siz...  41 us
    ppermute x3, starting transfers between devices, swapped(): return lax.ppermute(block, 'feat', [(i, i ^ mask) for i in range(size)])  9.39 us
    all_to_all x1, blocking collectives, local(): lax.all_to_all(split_panel(centroids, col_pot), 'feat', split_axis=0, con...  8.45 us
    ppermute x7, waiting for transfers between devices, shifted(): lax.ppermute(block, 'blk', [(i, (i + distance) % size) for i in range(siz...  8.25 us
    pallas_call x2, Pallas kernels, pair(): pl.pallas_call(functools.partial(pair_kernel, 1.0 / (0.02 * features), le...  7.77 us
    all_gather x1, blocking collectives, local(): row_lse = rows_merged(lax.all_gather(rows, 'feat', axis=0, tiled=True))  6.7 us
    ppermute x1, waiting for transfers between devices, four_back_second(): lax.ppermute(block, 'blk', [(at, (i - 4) % size) for i, at in enumerate(h...  5.79 us
    ppermute x1, starting transfers between devices, four_back_first(): return lax.ppermute(block, 'blk', list(enumerate(half_way(size))))  1.98 us
  transfers between devices with their start and end apart: 12, of which 5 were waited for; matrix products, arithmetic and copies ran while one was open for 0% of the time, Pallas kernels for 6%

profile of v4, /device:TPU:76, one launch (start us, length us, event | category | flops | bytes accessed | tf_op | source)
XLA Modules:
  0.0 97.5 jit_solution(12582936642556937686)
XLA Ops:
  0.6 0.0 copy-start
  0.6 0.0 copy-start.1
  0.7 1.0 %copy-done.1 = bf16[192,512]{1,0:T(8,128)(2,1)S(1)} copy-done((bf16[192,512]{1,0:T(8,128)(2,1)S(1)}, bf16[192,512]{1,0:T(8,128)(2,1)}, u32[]{:S(2)}) %copy-start.1) | copy-done | bytes 196632
  1.6 0.0 copy-start.2
  1.6 0.7 copy-done.2
  2.3 0.1 split_panel.1
  2.4 0.0 copy-start.3
  2.4 8.4 %all_to_all.5.refs_5_ = bf16[4,208,128]{2,1,0:T(8,128)(2,1)S(1)} all-to-all(bf16[4,208,128]{2,1,0:T(8,128)(2,1)S(1)} %split_panel.1), channel_id=1, replica_groups=mesh['blk'=128,'feat'=4] {'feat'}, dimensions={0} | all-to-all | bytes 425984 | tf_op jit(solution)/shard_map/all_to_all | solution.py:285
  10.9 0.0 copy-done
  10.9 5.1 %collective-permute-start.1 = (bf16[192,2048]{1,0:T(8,128)(2,1)S(1)}, bf16[192,2048]{1,0:T(8,128)(2,1)S(1)}, u32[]{:S(2)}, u32[]{:S(2)}) collective-permute-start(bf16[192,2048]{1,0:T(8,128)(2,1)S(1)} %copy-done), channel_id=1, source_target_pairs={{0,2},{1,3},{2,0},{3,1},{4,6},{5,7},{6,4},{7,5},{8,10},{9,11},{10,... | collective-permute-start | bytes 2359304 | tf_op jit(solution)/shard_map/ppermute | solution.py:37
  16.0 6.8 %collective-permute-start.5 = (bf16[4,208,128]{2,1,0:T(8,128)(2,1)S(1)}, bf16[4,208,128]{2,1,0:T(8,128)(2,1)S(1)}, u32[]{:S(2)}, u32[]{:S(2)}) collective-permute-start(bf16[4,208,128]{2,1,0:T(8,128)(2,1)S(1)} %all_to_all.5.refs_5_), channel_id=1, source_target_pairs={{0,16},{4,20},{8,24},{12,28},{16,32},{20,36},{24,40},{28,44},{32,4... | collective-permute-start | bytes 638984 | tf_op jit(solution)/shard_map/ppermute | solution.py:18
  22.8 2.6 %collective-permute-start.3 = (bf16[4,208,128]{2,1,0:T(8,128)(2,1)S(1)}, bf16[4,208,128]{2,1,0:T(8,128)(2,1)S(1)}, u32[]{:S(2)}, u32[]{:S(2)}) collective-permute-start(bf16[4,208,128]{2,1,0:T(8,128)(2,1)S(1)} %all_to_all.5.refs_5_), channel_id=1, source_target_pairs={{0,4},{4,8},{8,12},{12,16},{16,20},{20,24},{24,28},{28,32},{32,36}... | collective-permute-start | bytes 638984 | tf_op jit(solution)/shard_map/ppermute | solution.py:18
  25.4 6.6 %collective-permute-done.5.refs_5_ = bf16[4,208,128]{2,1,0:T(8,128)(2,1)S(1)} collective-permute-done((bf16[4,208,128]{2,1,0:T(8,128)(2,1)S(1)}, bf16[4,208,128]{2,1,0:T(8,128)(2,1)S(1)}, u32[]{:S(2)}, u32[]{:S(2)}) %collective-permute-start.5) | collective-permute-done | bytes 213024 | tf_op jit(solution)/shard_map/ppermute | solution.py:18
  32.0 4.7 %collective-permute-start.6 = (bf16[4,208,128]{2,1,0:T(8,128)(2,1)S(1)}, bf16[4,208,128]{2,1,0:T(8,128)(2,1)S(1)}, u32[]{:S(2)}, u32[]{:S(2)}) collective-permute-start(bf16[4,208,128]{2,1,0:T(8,128)(2,1)S(1)} %collective-permute-done.5.refs_5_), channel_id=1, source_target_pairs={{0,508},{4,0},{8,4},{12,8},{16,12},{20,16},{24,20},{28,24},{32,28}... | collective-permute-start | bytes 638984 | tf_op jit(solution)/shard_map/ppermute | solution.py:18
  36.8 1.1 %collective-permute-done.3.refs_4_ = bf16[4,208,128]{2,1,0:T(8,128)(2,1)S(1)} collective-permute-done((bf16[4,208,128]{2,1,0:T(8,128)(2,1)S(1)}, bf16[4,208,128]{2,1,0:T(8,128)(2,1)S(1)}, u32[]{:S(2)}, u32[]{:S(2)}) %collective-permute-start.3) | collective-permute-done | bytes 213024 | tf_op jit(solution)/shard_map/ppermute | solution.py:18
  37.8 3.4 %collective-permute-start.4 = (bf16[4,208,128]{2,1,0:T(8,128)(2,1)S(1)}, bf16[4,208,128]{2,1,0:T(8,128)(2,1)S(1)}, u32[]{:S(2)}, u32[]{:S(2)}) collective-permute-start(bf16[4,208,128]{2,1,0:T(8,128)(2,1)S(1)} %collective-permute-done.3.refs_4_), channel_id=1, source_target_pairs={{0,4},{4,8},{8,12},{12,16},{16,20},{20,24},{24,28},{28,32},{32,36}... | collective-permute-start | bytes 638984 | tf_op jit(solution)/shard_map/ppermute | solution.py:18
  41.2 1.9 %collective-permute-start = (bf16[192,2048]{1,0:T(8,128)(2,1)S(1)}, bf16[192,2048]{1,0:T(8,128)(2,1)S(1)}, u32[]{:S(2)}, u32[]{:S(2)}) collective-permute-start(bf16[192,2048]{1,0:T(8,128)(2,1)S(1)} %copy-done), channel_id=1, source_target_pairs={{0,1},{1,0},{2,3},{3,2},{4,5},{5,4},{6,7},{7,6},{8,9},{9,8},{10,11... | collective-permute-start | bytes 2359304 | tf_op jit(solution)/shard_map/ppermute | solution.py:37
  43.1 0.0 collective-permute-done.1.refs_2_
  43.1 2.4 %collective-permute-start.2 = (bf16[192,2048]{1,0:T(8,128)(2,1)S(1)}, bf16[192,2048]{1,0:T(8,128)(2,1)S(1)}, u32[]{:S(2)}, u32[]{:S(2)}) collective-permute-start(bf16[192,2048]{1,0:T(8,128)(2,1)S(1)} %collective-permute-done.1.refs_2_), channel_id=1, source_target_pairs={{0,1},{1,0},{2,3},{3,2},{4,5},{5,4},{6,7},{7,6},{8,9},{9,8},{10,11... | collective-permute-start | bytes 2359304 | tf_op jit(solution)/shard_map/ppermute | solution.py:37
  45.6 0.0 collective-permute-done.6.refs_0_.refs_4_
  45.6 0.6 collective-permute-done.4.refs_1_.refs_6_
  46.1 0.0 copy-done.3
  46.1 0.0 collective-permute-done.refs_1_
  46.1 1.3 %collective-permute-done.2.refs_3_ = bf16[192,2048]{1,0:T(8,128)(2,1)S(1)} collective-permute-done((bf16[192,2048]{1,0:T(8,128)(2,1)S(1)}, bf16[192,2048]{1,0:T(8,128)(2,1)S(1)}, u32[]{:S(2)}, u32[]{:S(2)}) %collective-permute-start.2) | collective-permute-done | bytes 786464 | tf_op jit(solution)/shard_map/ppermute | solution.py:37
  47.5 3.2 %pair34.1 = (f32[144,768]{1,0:T(8,128)S(1)}, f32[144,768]{1,0:T(8,128)S(1)}, f32[1,2048]{1,0:T(1,128)S(1)}) custom-call(bf16[192,2048]{1,0:T(8,128)(2,1)S(1)} %copy-done, bf16[192,2048]{1,0:T(8,128)(2,1)S(1)} %collective-permute-done.refs_1_, bf16[192,2048]{1,0:T(8,128)(2,1)S(1)} %collective-permute-done.1.refs_2_, ...), custom_call_target="tpu_custom_call" | custom-call | flops 1 | bytes 1 | tf_op jit(solution)/shard_map/pair34/pallas_call | solution.py:194
  50.7 4.4 %collective-permute-start.10 = (f16[144,768]{1,0:T(8,128)(2,1)S(1)}, f16[144,768]{1,0:T(8,128)(2,1)S(1)}, u32[]{:S(2)}, u32[]{:S(2)}) collective-permute-start(f16[144,768]{1,0:T(8,128)(2,1)S(1)} %convert_element_type.28), channel_id=1, source_target_pairs={{0,508},{4,0},{8,4},{12,8},{16,12},{20,16},{24,20},{28,24},{32,28}... | collective-permute-start | bytes 663560 | tf_op jit(solution)/shard_map/ppermute | solution.py:18
  55.2 2.0 %collective-permute-start.8 = (f16[144,768]{1,0:T(8,128)(2,1)S(1)}, f16[144,768]{1,0:T(8,128)(2,1)S(1)}, u32[]{:S(2)}, u32[]{:S(2)}) collective-permute-start(f16[144,768]{1,0:T(8,128)(2,1)S(1)} %convert_element_type.26), channel_id=1, source_target_pairs={{0,8},{4,12},{8,16},{12,20},{16,24},{20,28},{24,0},{28,4},{32,40},... | collective-permute-start | bytes 663560 | tf_op jit(solution)/shard_map/ppermute | solution.py:27
  57.2 4.6 %pair102.1 = (f32[144,768]{1,0:T(8,128)S(1)}, f32[144,768]{1,0:T(8,128)S(1)}, f32[144,768]{1,0:T(8,128)S(1)}, f32[1,2048]{1,0:T(1,128)S(1)}) custom-call(bf16[192,2048]{1,0:T(8,128)(2,1)S(1)} %copy-done, bf16[192,2048]{1,0:T(8,128)(2,1)S(1)} %collective-permute-done.refs_1_, bf16[192,2048]{1,0:T(8,128)(2,1)S(1)} %collective-permute-done.1.refs_2_, ...), custom_call_target="tpu_custom_call" | custom-call | flops 1 | bytes 1 | tf_op jit(solution)/shard_map/pair102/pallas_call | solution.py:194
  61.8 3.0 %collective-permute-start.7 = (f16[144,768]{1,0:T(8,128)(2,1)S(1)}, f16[144,768]{1,0:T(8,128)(2,1)S(1)}, u32[]{:S(2)}, u32[]{:S(2)}) collective-permute-start(f16[144,768]{1,0:T(8,128)(2,1)S(1)} %convert_element_type.24), channel_id=1, source_target_pairs={{0,508},{4,0},{8,4},{12,8},{16,12},{20,16},{24,20},{28,24},{32,28}... | collective-permute-start | bytes 663560 | tf_op jit(solution)/shard_map/ppermute | solution.py:18
  64.7 0.0 collective-permute-done.10
  64.8 0.3 blend.1
  65.1 16.0 %collective-permute-start.11 = (f16[144,768]{1,0:T(8,128)(2,1)S(1)}, f16[144,768]{1,0:T(8,128)(2,1)S(1)}, u32[]{:S(2)}, u32[]{:S(2)}) collective-permute-start(f16[144,768]{1,0:T(8,128)(2,1)S(1)} %convert_element_type.30), channel_id=1, source_target_pairs={{0,504},{4,508},{8,0},{12,4},{16,8},{20,12},{24,16},{28,20},{32,24... | collective-permute-start | bytes 663560 | tf_op jit(solution)/shard_map/ppermute | solution.py:18
  81.1 0.0 collective-permute-done.8
  81.1 1.9 %collective-permute-start.9 = (f16[144,768]{1,0:T(8,128)(2,1)S(1)}, f16[144,768]{1,0:T(8,128)(2,1)S(1)}, u32[]{:S(2)}, u32[]{:S(2)}) collective-permute-start(f16[144,768]{1,0:T(8,128)(2,1)S(1)} %collective-permute-done.8), channel_id=1, source_target_pairs={{8,496},{12,500},{16,504},{20,508},{24,0},{28,4},{0,8},{4,12},{40,... | collective-permute-start | bytes 663560 | tf_op jit(solution)/shard_map/ppermute | solution.py:32
  83.1 6.7 %all-gather = f32[4,1,2048]{2,1,0:T(1,128)S(1)} all-gather(f32[1,1,2048]{2,1,0:T(1,128)S(1)} %bitcast.9), channel_id=1, replica_groups=mesh['blk'=128,'feat'=4] {'feat'}, dimensions={0}, use_global_device_ids=true | all-gather | bytes 40960 | tf_op jit(solution)/shard_map/all_gather | solution.py:302
  89.8 0.7 rows_merged.1
  90.5 0.0 collective-permute-done.7
  90.5 0.0 collective-permute-done.11
  90.5 5.8 %collective-permute-done.9 = f16[144,768]{1,0:T(8,128)(2,1)S(1)} collective-permute-done((f16[144,768]{1,0:T(8,128)(2,1)S(1)}, f16[144,768]{1,0:T(8,128)(2,1)S(1)}, u32[]{:S(2)}, u32[]{:S(2)}) %collective-permute-start.9) | collective-permute-done | bytes 221216 | tf_op jit(solution)/shard_map/ppermute | solution.py:32
  96.4 1.2 %merge_last.1 = (f32[128,768]{1,0:T(8,128)}, f32[1,128]{1,0:T(1,128)}) custom-call(f32[144,768]{1,0:T(8,128)S(1)} %get-tuple-element.16.refs_0_, f32[144,768]{1,0:T(8,128)S(1)} %convert_element_type.25.refs_1_, f32[144,768]{1,0:T(8,128)S(1)} %convert_element_type.27.refs_2_, f32[144,768]{1,0:T(8,128)S(1)} %convert_element_type.31.refs_3_), custom_call_target="tpu_custom_call" | custom-call | flops 1 | bytes 1 | tf_op jit(solution)/shard_map/merge_last/pallas_call | solution.py:235
  (10 shorter events, 0.2 us)
Async XLA Ops:
  0.6 10.3 %copy-start = (bf16[192,2048]{1,0:T(8,128)(2,1)S(1)}, bf16[192,2048]{1,0:T(8,128)(2,1)}, u32[]{:S(2)}) copy-start(bf16[192,2048]{1,0:T(8,128)(2,1)} %refs_0_.3) | copy-start | bytes 2359300
  0.6 1.0 %copy-start.1 = (bf16[192,512]{1,0:T(8,128)(2,1)S(1)}, bf16[192,512]{1,0:T(8,128)(2,1)}, u32[]{:S(2)}) copy-start(bf16[192,512]{1,0:T(8,128)(2,1)} %cent.1) | copy-start | bytes 589828
  1.6 0.7 copy-start.2
  2.4 43.7 %copy-start.3 = (f32[2048]{0:T(1024)S(1)}, f32[2048]{0:T(1024)}, u32[]{:S(2)}) copy-start(f32[2048]{0:T(1024)} %param.7) | copy-start | bytes 24580
  10.9 32.2 %collective-permute-start.1 = (bf16[192,2048]{1,0:T(8,128)(2,1)S(1)}, bf16[192,2048]{1,0:T(8,128)(2,1)S(1)}, u32[]{:S(2)}, u32[]{:S(2)}) collective-permute-start(bf16[192,2048]{1,0:T(8,128)(2,1)S(1)} %copy-done), channel_id=1, source_target_pairs={{0,2},{1,3},{2,0},{3,1},{4,6},{5,7},{6,4},{7,5},{8,10},{9,11},{10,... | collective-permute-start | bytes 2359304 | tf_op jit(solution)/shard_map/ppermute | solution.py:37
  16.0 16.0 %collective-permute-start.5 = (bf16[4,208,128]{2,1,0:T(8,128)(2,1)S(1)}, bf16[4,208,128]{2,1,0:T(8,128)(2,1)S(1)}, u32[]{:S(2)}, u32[]{:S(2)}) collective-permute-start(bf16[4,208,128]{2,1,0:T(8,128)(2,1)S(1)} %all_to_all.5.refs_5_), channel_id=1, source_target_pairs={{0,16},{4,20},{8,24},{12,28},{16,32},{20,36},{24,40},{28,44},{32,4... | collective-permute-start | bytes 638984 | tf_op jit(solution)/shard_map/ppermute | solution.py:18
  22.8 15.0 %collective-permute-start.3 = (bf16[4,208,128]{2,1,0:T(8,128)(2,1)S(1)}, bf16[4,208,128]{2,1,0:T(8,128)(2,1)S(1)}, u32[]{:S(2)}, u32[]{:S(2)}) collective-permute-start(bf16[4,208,128]{2,1,0:T(8,128)(2,1)S(1)} %all_to_all.5.refs_5_), channel_id=1, source_target_pairs={{0,4},{4,8},{8,12},{12,16},{16,20},{20,24},{24,28},{28,32},{32,36}... | collective-permute-start | bytes 638984 | tf_op jit(solution)/shard_map/ppermute | solution.py:18
  32.0 13.6 %collective-permute-start.6 = (bf16[4,208,128]{2,1,0:T(8,128)(2,1)S(1)}, bf16[4,208,128]{2,1,0:T(8,128)(2,1)S(1)}, u32[]{:S(2)}, u32[]{:S(2)}) collective-permute-start(bf16[4,208,128]{2,1,0:T(8,128)(2,1)S(1)} %collective-permute-done.5.refs_5_), channel_id=1, source_target_pairs={{0,508},{4,0},{8,4},{12,8},{16,12},{20,16},{24,20},{28,24},{32,28}... | collective-permute-start | bytes 638984 | tf_op jit(solution)/shard_map/ppermute | solution.py:18
  37.8 8.3 %collective-permute-start.4 = (bf16[4,208,128]{2,1,0:T(8,128)(2,1)S(1)}, bf16[4,208,128]{2,1,0:T(8,128)(2,1)S(1)}, u32[]{:S(2)}, u32[]{:S(2)}) collective-permute-start(bf16[4,208,128]{2,1,0:T(8,128)(2,1)S(1)} %collective-permute-done.3.refs_4_), channel_id=1, source_target_pairs={{0,4},{4,8},{8,12},{12,16},{16,20},{20,24},{24,28},{28,32},{32,36}... | collective-permute-start | bytes 638984 | tf_op jit(solution)/shard_map/ppermute | solution.py:18
  41.2 4.9 %collective-permute-start = (bf16[192,2048]{1,0:T(8,128)(2,1)S(1)}, bf16[192,2048]{1,0:T(8,128)(2,1)S(1)}, u32[]{:S(2)}, u32[]{:S(2)}) collective-permute-start(bf16[192,2048]{1,0:T(8,128)(2,1)S(1)} %copy-done), channel_id=1, source_target_pairs={{0,1},{1,0},{2,3},{3,2},{4,5},{5,4},{6,7},{7,6},{8,9},{9,8},{10,11... | collective-permute-start | bytes 2359304 | tf_op jit(solution)/shard_map/ppermute | solution.py:37
  43.1 4.3 %collective-permute-start.2 = (bf16[192,2048]{1,0:T(8,128)(2,1)S(1)}, bf16[192,2048]{1,0:T(8,128)(2,1)S(1)}, u32[]{:S(2)}, u32[]{:S(2)}) collective-permute-start(bf16[192,2048]{1,0:T(8,128)(2,1)S(1)} %collective-permute-done.1.refs_2_), channel_id=1, source_target_pairs={{0,1},{1,0},{2,3},{3,2},{4,5},{5,4},{6,7},{7,6},{8,9},{9,8},{10,11... | collective-permute-start | bytes 2359304 | tf_op jit(solution)/shard_map/ppermute | solution.py:37
  50.7 14.1 %collective-permute-start.10 = (f16[144,768]{1,0:T(8,128)(2,1)S(1)}, f16[144,768]{1,0:T(8,128)(2,1)S(1)}, u32[]{:S(2)}, u32[]{:S(2)}) collective-permute-start(f16[144,768]{1,0:T(8,128)(2,1)S(1)} %convert_element_type.28), channel_id=1, source_target_pairs={{0,508},{4,0},{8,4},{12,8},{16,12},{20,16},{24,20},{28,24},{32,28}... | collective-permute-start | bytes 663560 | tf_op jit(solution)/shard_map/ppermute | solution.py:18
  55.2 26.0 %collective-permute-start.8 = (f16[144,768]{1,0:T(8,128)(2,1)S(1)}, f16[144,768]{1,0:T(8,128)(2,1)S(1)}, u32[]{:S(2)}, u32[]{:S(2)}) collective-permute-start(f16[144,768]{1,0:T(8,128)(2,1)S(1)} %convert_element_type.26), channel_id=1, source_target_pairs={{0,8},{4,12},{8,16},{12,20},{16,24},{20,28},{24,0},{28,4},{32,40},... | collective-permute-start | bytes 663560 | tf_op jit(solution)/shard_map/ppermute | solution.py:27
  61.8 28.7 %collective-permute-start.7 = (f16[144,768]{1,0:T(8,128)(2,1)S(1)}, f16[144,768]{1,0:T(8,128)(2,1)S(1)}, u32[]{:S(2)}, u32[]{:S(2)}) collective-permute-start(f16[144,768]{1,0:T(8,128)(2,1)S(1)} %convert_element_type.24), channel_id=1, source_target_pairs={{0,508},{4,0},{8,4},{12,8},{16,12},{20,16},{24,20},{28,24},{32,28}... | collective-permute-start | bytes 663560 | tf_op jit(solution)/shard_map/ppermute | solution.py:18
  65.1 25.4 %collective-permute-start.11 = (f16[144,768]{1,0:T(8,128)(2,1)S(1)}, f16[144,768]{1,0:T(8,128)(2,1)S(1)}, u32[]{:S(2)}, u32[]{:S(2)}) collective-permute-start(f16[144,768]{1,0:T(8,128)(2,1)S(1)} %convert_element_type.30), channel_id=1, source_target_pairs={{0,504},{4,508},{8,0},{12,4},{16,8},{20,12},{24,16},{28,20},{32,24... | collective-permute-start | bytes 663560 | tf_op jit(solution)/shard_map/ppermute | solution.py:18
  81.1 15.2 %collective-permute-start.9 = (f16[144,768]{1,0:T(8,128)(2,1)S(1)}, f16[144,768]{1,0:T(8,128)(2,1)S(1)}, u32[]{:S(2)}, u32[]{:S(2)}) collective-permute-start(f16[144,768]{1,0:T(8,128)(2,1)S(1)} %collective-permute-done.8), channel_id=1, source_target_pairs={{8,496},{12,500},{16,504},{20,508},{24,0},{28,4},{0,8},{4,12},{40,... | collective-permute-start | bytes 663560 | tf_op jit(solution)/shard_map/ppermute | solution.py:32

commit v5 on v4

--- a/solution.py
+++ b/solution.py
@@ -10,7 +10,7 @@
 ROW = 8
 EXTRA = 16
 CHUNK = 512
-STAT = 16
+STAT = 8
 
 
 def shifted(block, distance):

time: 98.1 us -> 97.5 us (level)
  no operation moved by 1% of the time
where the time goes in v5:
time: 97.5 us; the launch traced here: 96.9 us
  starting transfers between devices  54.3 us (56%)
  blocking collectives  15.1 us (15%)
  waiting for transfers between devices  14.8 us (15%)
  Pallas kernels  9.91 us (10%)
  local copies, waits for them, and re-layouts  1.7 us (2%)
    ppermute x7, starting transfers between devices, shifted(): lax.ppermute(block, 'blk', [(i, (i + distance) % size) for i in range(siz...  41 us
    ppermute x3, starting transfers between devices, swapped(): return lax.ppermute(block, 'feat', [(i, i ^ mask) for i in range(size)])  9.39 us
    all_to_all x1, blocking collectives, local(): lax.all_to_all(split_panel(centroids, col_pot), 'feat', split_axis=0, con...  8.45 us
    ppermute x7, waiting for transfers between devices, shifted(): lax.ppermute(block, 'blk', [(i, (i + distance) % size) for i in range(siz...  8.25 us
    pallas_call x2, Pallas kernels, pair(): pl.pallas_call(functools.partial(pair_kernel, 1.0 / (0.02 * features), le...  7.72 us
    all_gather x1, blocking collectives, local(): row_lse = rows_merged(lax.all_gather(rows, 'feat', axis=0, tiled=True))  6.7 us
    ppermute x1, waiting for transfers between devices, four_back_second(): lax.ppermute(block, 'blk', [(at, (i - 4) % size) for i, at in enumerate(h...  5.26 us
    ppermute x1, starting transfers between devices, four_back_first(): return lax.ppermute(block, 'blk', list(enumerate(half_way(size))))  1.99 us
  transfers between devices with their start and end apart: 12, of which 5 were waited for; matrix products, arithmetic and copies ran while one was open for 0% of the time, Pallas kernels for 6%

profile of v5, /device:TPU:76, one launch (start us, length us, event | category | flops | bytes accessed | tf_op | source)
XLA Modules:
  0.0 96.9 jit_solution(13728308759792736859)
XLA Ops:
  0.6 0.0 copy-start
  0.6 0.0 copy-start.1
  0.7 1.0 %copy-done.1 = bf16[192,512]{1,0:T(8,128)(2,1)S(1)} copy-done((bf16[192,512]{1,0:T(8,128)(2,1)S(1)}, bf16[192,512]{1,0:T(8,128)(2,1)}, u32[]{:S(2)}) %copy-start.1) | copy-done | bytes 196632
  1.6 0.0 copy-start.2
  1.6 0.7 copy-done.2
  2.3 0.1 split_panel.1
  2.4 0.0 copy-start.3
  2.4 8.4 %all_to_all.5.refs_5_ = bf16[4,208,128]{2,1,0:T(8,128)(2,1)S(1)} all-to-all(bf16[4,208,128]{2,1,0:T(8,128)(2,1)S(1)} %split_panel.1), channel_id=1, replica_groups=mesh['blk'=128,'feat'=4] {'feat'}, dimensions={0} | all-to-all | bytes 425984 | tf_op jit(solution)/shard_map/all_to_all | solution.py:285
  10.9 0.0 copy-done
  10.9 5.1 %collective-permute-start.1 = (bf16[192,2048]{1,0:T(8,128)(2,1)S(1)}, bf16[192,2048]{1,0:T(8,128)(2,1)S(1)}, u32[]{:S(2)}, u32[]{:S(2)}) collective-permute-start(bf16[192,2048]{1,0:T(8,128)(2,1)S(1)} %copy-done), channel_id=1, source_target_pairs={{0,2},{1,3},{2,0},{3,1},{4,6},{5,7},{6,4},{7,5},{8,10},{9,11},{10,... | collective-permute-start | bytes 2359304 | tf_op jit(solution)/shard_map/ppermute | solution.py:37
  16.0 6.8 %collective-permute-start.5 = (bf16[4,208,128]{2,1,0:T(8,128)(2,1)S(1)}, bf16[4,208,128]{2,1,0:T(8,128)(2,1)S(1)}, u32[]{:S(2)}, u32[]{:S(2)}) collective-permute-start(bf16[4,208,128]{2,1,0:T(8,128)(2,1)S(1)} %all_to_all.5.refs_5_), channel_id=1, source_target_pairs={{0,16},{4,20},{8,24},{12,28},{16,32},{20,36},{24,40},{28,44},{32,4... | collective-permute-start | bytes 638984 | tf_op jit(solution)/shard_map/ppermute | solution.py:18
  22.8 2.6 %collective-permute-start.3 = (bf16[4,208,128]{2,1,0:T(8,128)(2,1)S(1)}, bf16[4,208,128]{2,1,0:T(8,128)(2,1)S(1)}, u32[]{:S(2)}, u32[]{:S(2)}) collective-permute-start(bf16[4,208,128]{2,1,0:T(8,128)(2,1)S(1)} %all_to_all.5.refs_5_), channel_id=1, source_target_pairs={{0,4},{4,8},{8,12},{12,16},{16,20},{20,24},{24,28},{28,32},{32,36}... | collective-permute-start | bytes 638984 | tf_op jit(solution)/shard_map/ppermute | solution.py:18
  25.4 6.6 %collective-permute-done.5.refs_5_ = bf16[4,208,128]{2,1,0:T(8,128)(2,1)S(1)} collective-permute-done((bf16[4,208,128]{2,1,0:T(8,128)(2,1)S(1)}, bf16[4,208,128]{2,1,0:T(8,128)(2,1)S(1)}, u32[]{:S(2)}, u32[]{:S(2)}) %collective-permute-start.5) | collective-permute-done | bytes 213024 | tf_op jit(solution)/shard_map/ppermute | solution.py:18
  32.0 4.7 %collective-permute-start.6 = (bf16[4,208,128]{2,1,0:T(8,128)(2,1)S(1)}, bf16[4,208,128]{2,1,0:T(8,128)(2,1)S(1)}, u32[]{:S(2)}, u32[]{:S(2)}) collective-permute-start(bf16[4,208,128]{2,1,0:T(8,128)(2,1)S(1)} %collective-permute-done.5.refs_5_), channel_id=1, source_target_pairs={{0,508},{4,0},{8,4},{12,8},{16,12},{20,16},{24,20},{28,24},{32,28}... | collective-permute-start | bytes 638984 | tf_op jit(solution)/shard_map/ppermute | solution.py:18
  36.8 1.1 %collective-permute-done.3.refs_4_ = bf16[4,208,128]{2,1,0:T(8,128)(2,1)S(1)} collective-permute-done((bf16[4,208,128]{2,1,0:T(8,128)(2,1)S(1)}, bf16[4,208,128]{2,1,0:T(8,128)(2,1)S(1)}, u32[]{:S(2)}, u32[]{:S(2)}) %collective-permute-start.3) | collective-permute-done | bytes 213024 | tf_op jit(solution)/shard_map/ppermute | solution.py:18
  37.8 3.4 %collective-permute-start.4 = (bf16[4,208,128]{2,1,0:T(8,128)(2,1)S(1)}, bf16[4,208,128]{2,1,0:T(8,128)(2,1)S(1)}, u32[]{:S(2)}, u32[]{:S(2)}) collective-permute-start(bf16[4,208,128]{2,1,0:T(8,128)(2,1)S(1)} %collective-permute-done.3.refs_4_), channel_id=1, source_target_pairs={{0,4},{4,8},{8,12},{12,16},{16,20},{20,24},{24,28},{28,32},{32,36}... | collective-permute-start | bytes 638984 | tf_op jit(solution)/shard_map/ppermute | solution.py:18
  41.2 1.9 %collective-permute-start = (bf16[192,2048]{1,0:T(8,128)(2,1)S(1)}, bf16[192,2048]{1,0:T(8,128)(2,1)S(1)}, u32[]{:S(2)}, u32[]{:S(2)}) collective-permute-start(bf16[192,2048]{1,0:T(8,128)(2,1)S(1)} %copy-done), channel_id=1, source_target_pairs={{0,1},{1,0},{2,3},{3,2},{4,5},{5,4},{6,7},{7,6},{8,9},{9,8},{10,11... | collective-permute-start | bytes 2359304 | tf_op jit(solution)/shard_map/ppermute | solution.py:37
  43.1 0.0 collective-permute-done.1.refs_2_
  43.1 2.4 %collective-permute-start.2 = (bf16[192,2048]{1,0:T(8,128)(2,1)S(1)}, bf16[192,2048]{1,0:T(8,128)(2,1)S(1)}, u32[]{:S(2)}, u32[]{:S(2)}) collective-permute-start(bf16[192,2048]{1,0:T(8,128)(2,1)S(1)} %collective-permute-done.1.refs_2_), channel_id=1, source_target_pairs={{0,1},{1,0},{2,3},{3,2},{4,5},{5,4},{6,7},{7,6},{8,9},{9,8},{10,11... | collective-permute-start | bytes 2359304 | tf_op jit(solution)/shard_map/ppermute | solution.py:37
  45.6 0.0 collective-permute-done.6.refs_0_.refs_4_
  45.6 0.6 collective-permute-done.4.refs_1_.refs_6_
  46.1 0.0 copy-done.3
  46.1 0.0 collective-permute-done.refs_1_
  46.1 1.3 %collective-permute-done.2.refs_3_ = bf16[192,2048]{1,0:T(8,128)(2,1)S(1)} collective-permute-done((bf16[192,2048]{1,0:T(8,128)(2,1)S(1)}, bf16[192,2048]{1,0:T(8,128)(2,1)S(1)}, u32[]{:S(2)}, u32[]{:S(2)}) %collective-permute-start.2) | collective-permute-done | bytes 786464 | tf_op jit(solution)/shard_map/ppermute | solution.py:37
  47.5 3.2 %pair34.1 = (f32[136,768]{1,0:T(8,128)S(1)}, f32[136,768]{1,0:T(8,128)S(1)}, f32[1,2048]{1,0:T(1,128)S(1)}) custom-call(bf16[192,2048]{1,0:T(8,128)(2,1)S(1)} %copy-done, bf16[192,2048]{1,0:T(8,128)(2,1)S(1)} %collective-permute-done.refs_1_, bf16[192,2048]{1,0:T(8,128)(2,1)S(1)} %collective-permute-done.1.refs_2_, ...), custom_call_target="tpu_custom_call" | custom-call | flops 1 | bytes 1 | tf_op jit(solution)/shard_map/pair34/pallas_call | solution.py:194
  50.7 4.4 %collective-permute-start.10 = (f16[136,768]{1,0:T(8,128)(2,1)S(1)}, f16[136,768]{1,0:T(8,128)(2,1)S(1)}, u32[]{:S(2)}, u32[]{:S(2)}) collective-permute-start(f16[136,768]{1,0:T(8,128)(2,1)S(1)} %convert_element_type.28), channel_id=1, source_target_pairs={{0,508},{4,0},{8,4},{12,8},{16,12},{20,16},{24,20},{28,24},{32,28}... | collective-permute-start | bytes 626696 | tf_op jit(solution)/shard_map/ppermute | solution.py:18
  55.1 2.0 %collective-permute-start.8 = (f16[136,768]{1,0:T(8,128)(2,1)S(1)}, f16[136,768]{1,0:T(8,128)(2,1)S(1)}, u32[]{:S(2)}, u32[]{:S(2)}) collective-permute-start(f16[136,768]{1,0:T(8,128)(2,1)S(1)} %convert_element_type.26), channel_id=1, source_target_pairs={{0,8},{4,12},{8,16},{12,20},{16,24},{20,28},{24,0},{28,4},{32,40},... | collective-permute-start | bytes 626696 | tf_op jit(solution)/shard_map/ppermute | solution.py:27
  57.1 4.6 %pair102.1 = (f32[136,768]{1,0:T(8,128)S(1)}, f32[136,768]{1,0:T(8,128)S(1)}, f32[136,768]{1,0:T(8,128)S(1)}, f32[1,2048]{1,0:T(1,128)S(1)}) custom-call(bf16[192,2048]{1,0:T(8,128)(2,1)S(1)} %copy-done, bf16[192,2048]{1,0:T(8,128)(2,1)S(1)} %collective-permute-done.refs_1_, bf16[192,2048]{1,0:T(8,128)(2,1)S(1)} %collective-permute-done.1.refs_2_, ...), custom_call_target="tpu_custom_call" | custom-call | flops 1 | bytes 1 | tf_op jit(solution)/shard_map/pair102/pallas_call | solution.py:194
  61.7 2.9 %collective-permute-start.7 = (f16[136,768]{1,0:T(8,128)(2,1)S(1)}, f16[136,768]{1,0:T(8,128)(2,1)S(1)}, u32[]{:S(2)}, u32[]{:S(2)}) collective-permute-start(f16[136,768]{1,0:T(8,128)(2,1)S(1)} %convert_element_type.24), channel_id=1, source_target_pairs={{0,508},{4,0},{8,4},{12,8},{16,12},{20,16},{24,20},{28,24},{32,28}... | collective-permute-start | bytes 626696 | tf_op jit(solution)/shard_map/ppermute | solution.py:18
  64.7 0.0 collective-permute-done.10
  64.7 0.3 blend.1
  65.0 16.0 %collective-permute-start.11 = (f16[136,768]{1,0:T(8,128)(2,1)S(1)}, f16[136,768]{1,0:T(8,128)(2,1)S(1)}, u32[]{:S(2)}, u32[]{:S(2)}) collective-permute-start(f16[136,768]{1,0:T(8,128)(2,1)S(1)} %convert_element_type.30), channel_id=1, source_target_pairs={{0,504},{4,508},{8,0},{12,4},{16,8},{20,12},{24,16},{28,20},{32,24... | collective-permute-start | bytes 626696 | tf_op jit(solution)/shard_map/ppermute | solution.py:18
  81.1 0.0 collective-permute-done.8
  81.1 1.9 %collective-permute-start.9 = (f16[136,768]{1,0:T(8,128)(2,1)S(1)}, f16[136,768]{1,0:T(8,128)(2,1)S(1)}, u32[]{:S(2)}, u32[]{:S(2)}) collective-permute-start(f16[136,768]{1,0:T(8,128)(2,1)S(1)} %collective-permute-done.8), channel_id=1, source_target_pairs={{8,496},{12,500},{16,504},{20,508},{24,0},{28,4},{0,8},{4,12},{40,... | collective-permute-start | bytes 626696 | tf_op jit(solution)/shard_map/ppermute | solution.py:32
  83.0 6.7 %all-gather = f32[4,1,2048]{2,1,0:T(1,128)S(1)} all-gather(f32[1,1,2048]{2,1,0:T(1,128)S(1)} %bitcast.9), channel_id=1, replica_groups=mesh['blk'=128,'feat'=4] {'feat'}, dimensions={0}, use_global_device_ids=true | all-gather | bytes 40960 | tf_op jit(solution)/shard_map/all_gather | solution.py:302
  89.7 0.7 rows_merged.1
  90.4 0.0 collective-permute-done.7
  90.4 0.0 collective-permute-done.11
  90.5 5.3 %collective-permute-done.9 = f16[136,768]{1,0:T(8,128)(2,1)S(1)} collective-permute-done((f16[136,768]{1,0:T(8,128)(2,1)S(1)}, f16[136,768]{1,0:T(8,128)(2,1)S(1)}, u32[]{:S(2)}, u32[]{:S(2)}) %collective-permute-start.9) | collective-permute-done | bytes 208928 | tf_op jit(solution)/shard_map/ppermute | solution.py:32
  95.8 1.2 %merge_last.1 = (f32[128,768]{1,0:T(8,128)}, f32[1,128]{1,0:T(1,128)}) custom-call(f32[136,768]{1,0:T(8,128)S(1)} %get-tuple-element.16.refs_0_, f32[136,768]{1,0:T(8,128)S(1)} %convert_element_type.25.refs_1_, f32[136,768]{1,0:T(8,128)S(1)} %convert_element_type.27.refs_2_, f32[136,768]{1,0:T(8,128)S(1)} %convert_element_type.31.refs_3_), custom_call_target="tpu_custom_call" | custom-call | flops 1 | bytes 1 | tf_op jit(solution)/shard_map/merge_last/pallas_call | solution.py:235
  (10 shorter events, 0.2 us)
Async XLA Ops:
  0.6 10.3 %copy-start = (bf16[192,2048]{1,0:T(8,128)(2,1)S(1)}, bf16[192,2048]{1,0:T(8,128)(2,1)}, u32[]{:S(2)}) copy-start(bf16[192,2048]{1,0:T(8,128)(2,1)} %refs_0_.3) | copy-start | bytes 2359300
  0.6 1.0 %copy-start.1 = (bf16[192,512]{1,0:T(8,128)(2,1)S(1)}, bf16[192,512]{1,0:T(8,128)(2,1)}, u32[]{:S(2)}) copy-start(bf16[192,512]{1,0:T(8,128)(2,1)} %cent.1) | copy-start | bytes 589828
  1.6 0.7 copy-start.2
  2.4 43.7 %copy-start.3 = (f32[2048]{0:T(1024)S(1)}, f32[2048]{0:T(1024)}, u32[]{:S(2)}) copy-start(f32[2048]{0:T(1024)} %param.7) | copy-start | bytes 24580
  10.9 32.2 %collective-permute-start.1 = (bf16[192,2048]{1,0:T(8,128)(2,1)S(1)}, bf16[192,2048]{1,0:T(8,128)(2,1)S(1)}, u32[]{:S(2)}, u32[]{:S(2)}) collective-permute-start(bf16[192,2048]{1,0:T(8,128)(2,1)S(1)} %copy-done), channel_id=1, source_target_pairs={{0,2},{1,3},{2,0},{3,1},{4,6},{5,7},{6,4},{7,5},{8,10},{9,11},{10,... | collective-permute-start | bytes 2359304 | tf_op jit(solution)/shard_map/ppermute | solution.py:37
  16.0 16.0 %collective-permute-start.5 = (bf16[4,208,128]{2,1,0:T(8,128)(2,1)S(1)}, bf16[4,208,128]{2,1,0:T(8,128)(2,1)S(1)}, u32[]{:S(2)}, u32[]{:S(2)}) collective-permute-start(bf16[4,208,128]{2,1,0:T(8,128)(2,1)S(1)} %all_to_all.5.refs_5_), channel_id=1, source_target_pairs={{0,16},{4,20},{8,24},{12,28},{16,32},{20,36},{24,40},{28,44},{32,4... | collective-permute-start | bytes 638984 | tf_op jit(solution)/shard_map/ppermute | solution.py:18
  22.8 15.0 %collective-permute-start.3 = (bf16[4,208,128]{2,1,0:T(8,128)(2,1)S(1)}, bf16[4,208,128]{2,1,0:T(8,128)(2,1)S(1)}, u32[]{:S(2)}, u32[]{:S(2)}) collective-permute-start(bf16[4,208,128]{2,1,0:T(8,128)(2,1)S(1)} %all_to_all.5.refs_5_), channel_id=1, source_target_pairs={{0,4},{4,8},{8,12},{12,16},{16,20},{20,24},{24,28},{28,32},{32,36}... | collective-permute-start | bytes 638984 | tf_op jit(solution)/shard_map/ppermute | solution.py:18
  32.0 13.6 %collective-permute-start.6 = (bf16[4,208,128]{2,1,0:T(8,128)(2,1)S(1)}, bf16[4,208,128]{2,1,0:T(8,128)(2,1)S(1)}, u32[]{:S(2)}, u32[]{:S(2)}) collective-permute-start(bf16[4,208,128]{2,1,0:T(8,128)(2,1)S(1)} %collective-permute-done.5.refs_5_), channel_id=1, source_target_pairs={{0,508},{4,0},{8,4},{12,8},{16,12},{20,16},{24,20},{28,24},{32,28}... | collective-permute-start | bytes 638984 | tf_op jit(solution)/shard_map/ppermute | solution.py:18
  37.8 8.3 %collective-permute-start.4 = (bf16[4,208,128]{2,1,0:T(8,128)(2,1)S(1)}, bf16[4,208,128]{2,1,0:T(8,128)(2,1)S(1)}, u32[]{:S(2)}, u32[]{:S(2)}) collective-permute-start(bf16[4,208,128]{2,1,0:T(8,128)(2,1)S(1)} %collective-permute-done.3.refs_4_), channel_id=1, source_target_pairs={{0,4},{4,8},{8,12},{12,16},{16,20},{20,24},{24,28},{28,32},{32,36}... | collective-permute-start | bytes 638984 | tf_op jit(solution)/shard_map/ppermute | solution.py:18
  41.2 4.9 %collective-permute-start = (bf16[192,2048]{1,0:T(8,128)(2,1)S(1)}, bf16[192,2048]{1,0:T(8,128)(2,1)S(1)}, u32[]{:S(2)}, u32[]{:S(2)}) collective-permute-start(bf16[192,2048]{1,0:T(8,128)(2,1)S(1)} %copy-done), channel_id=1, source_target_pairs={{0,1},{1,0},{2,3},{3,2},{4,5},{5,4},{6,7},{7,6},{8,9},{9,8},{10,11... | collective-permute-start | bytes 2359304 | tf_op jit(solution)/shard_map/ppermute | solution.py:37
  43.1 4.3 %collective-permute-start.2 = (bf16[192,2048]{1,0:T(8,128)(2,1)S(1)}, bf16[192,2048]{1,0:T(8,128)(2,1)S(1)}, u32[]{:S(2)}, u32[]{:S(2)}) collective-permute-start(bf16[192,2048]{1,0:T(8,128)(2,1)S(1)} %collective-permute-done.1.refs_2_), channel_id=1, source_target_pairs={{0,1},{1,0},{2,3},{3,2},{4,5},{5,4},{6,7},{7,6},{8,9},{9,8},{10,11... | collective-permute-start | bytes 2359304 | tf_op jit(solution)/shard_map/ppermute | solution.py:37
  50.7 14.0 %collective-permute-start.10 = (f16[136,768]{1,0:T(8,128)(2,1)S(1)}, f16[136,768]{1,0:T(8,128)(2,1)S(1)}, u32[]{:S(2)}, u32[]{:S(2)}) collective-permute-start(f16[136,768]{1,0:T(8,128)(2,1)S(1)} %convert_element_type.28), channel_id=1, source_target_pairs={{0,508},{4,0},{8,4},{12,8},{16,12},{20,16},{24,20},{28,24},{32,28}... | collective-permute-start | bytes 626696 | tf_op jit(solution)/shard_map/ppermute | solution.py:18
  55.1 25.9 %collective-permute-start.8 = (f16[136,768]{1,0:T(8,128)(2,1)S(1)}, f16[136,768]{1,0:T(8,128)(2,1)S(1)}, u32[]{:S(2)}, u32[]{:S(2)}) collective-permute-start(f16[136,768]{1,0:T(8,128)(2,1)S(1)} %convert_element_type.26), channel_id=1, source_target_pairs={{0,8},{4,12},{8,16},{12,20},{16,24},{20,28},{24,0},{28,4},{32,40},... | collective-permute-start | bytes 626696 | tf_op jit(solution)/shard_map/ppermute | solution.py:27
  61.7 28.7 %collective-permute-start.7 = (f16[136,768]{1,0:T(8,128)(2,1)S(1)}, f16[136,768]{1,0:T(8,128)(2,1)S(1)}, u32[]{:S(2)}, u32[]{:S(2)}) collective-permute-start(f16[136,768]{1,0:T(8,128)(2,1)S(1)} %convert_element_type.24), channel_id=1, source_target_pairs={{0,508},{4,0},{8,4},{12,8},{16,12},{20,16},{24,20},{28,24},{32,28}... | collective-permute-start | bytes 626696 | tf_op jit(solution)/shard_map/ppermute | solution.py:18
  65.0 25.4 %collective-permute-start.11 = (f16[136,768]{1,0:T(8,128)(2,1)S(1)}, f16[136,768]{1,0:T(8,128)(2,1)S(1)}, u32[]{:S(2)}, u32[]{:S(2)}) collective-permute-start(f16[136,768]{1,0:T(8,128)(2,1)S(1)} %convert_element_type.30), channel_id=1, source_target_pairs={{0,504},{4,508},{8,0},{12,4},{16,8},{20,12},{24,16},{28,20},{32,24... | collective-permute-start | bytes 626696 | tf_op jit(solution)/shard_map/ppermute | solution.py:18
  81.1 14.7 %collective-permute-start.9 = (f16[136,768]{1,0:T(8,128)(2,1)S(1)}, f16[136,768]{1,0:T(8,128)(2,1)S(1)}, u32[]{:S(2)}, u32[]{:S(2)}) collective-permute-start(f16[136,768]{1,0:T(8,128)(2,1)S(1)} %collective-permute-done.8), channel_id=1, source_target_pairs={{8,496},{12,500},{16,504},{20,508},{24,0},{28,4},{0,8},{4,12},{40,... | collective-permute-start | bytes 626696 | tf_op jit(solution)/shard_map/ppermute | solution.py:32
